TPU v7x, 32 devices: a whole 2x2x4 slice. The times are simulated.
32 devices in a mesh: dp: 8 (over z, x), expert: 4 (over y, core).
Axes of the slice: x: 2, y: 2, z: 4, core: 2. Of those that a mesh axis runs over, the one named last changes fastest.
Arguments:
- tokens: bfloat16 [16384, 768], P(('dp', 'expert')), may hold values from -6 to 6
- segments: int32 [32, 512], P(('dp', 'expert')), may hold values from 0 to 2, never falling along the last dimension, each value on 1 to 256 neighbouring positions
- routes: int32 [16384, 2], P(('dp', 'expert')), may hold values from 0 to 7, as said below
- prev_logits: float32 [16384, 8], P(('dp', 'expert')), may hold values from -3 to 3
- ln1_gain: float32 [768], replicated, may hold values from 0.25 to 1.75
- w_qkv: bfloat16 [768, 2304], replicated, may hold values from -0.21875 to 0.21875
- w_attn: bfloat16 [768, 768], replicated, may hold values from -0.875 to 0.875
- ln2_gain: float32 [768], replicated, may hold values from 0.25 to 1.75
- w_router: float32 [768, 8], replicated, may hold values from -0.109375 to 0.109375
- const_mix: float32 [768, 4], replicated, may hold values from -0.21875 to 0.21875
- const_vec: float32 [768, 2], replicated, may hold values from -6 to 6
- expert_in: bfloat16 [4, 768, 4096], P('expert'), may hold values from -0.21875 to 0.21875
- expert_out: bfloat16 [4, 2048, 768], P('expert'), may hold values from -0.1875 to 0.1875
- cotangent: bfloat16 [16384, 768], P(('dp', 'expert')), may hold values from -6 to 6
Outputs:
- output: bfloat16 [16384, 768], P(('dp', 'expert'))
- input_grad: bfloat16 [16384, 768], P(('dp', 'expert'))
- ln1_grad: float32 [768], P(('dp', 'expert'))
- qkv_grad: float32 [768, 2304], P(('dp', 'expert'))
- attn_grad: float32 [768, 768], P(('dp', 'expert'))
- ln2_grad: float32 [768], P(('dp', 'expert'))
- router_grad: float32 [768, 8], P(('dp', 'expert'))
- mix_grad: float32 [768, 4], P(('dp', 'expert'))
- vec_grad: float32 [768, 2], P(('dp', 'expert'))
- expert_in_grad: float32 [4, 768, 4096], P('expert', 'dp')
- expert_out_grad: float32 [4, 2048, 768], P('expert', 'dp')
Inputs may be any that keep to these rules, and one draw needn't show every extreme that they name: `routes`: the two experts of a token differ; the first 4 numbers are feed-forward experts. In each aligned block of 512 rows no expert is named more than 256 times, and in each aligned run of 4 such blocks one feed-forward expert is named exactly 256 times in every block. `segments`: segment numbers never fall along a row; a document spans 1 to 256 places, and in each row exactly one document spans 256 places.
All inputs are finite; a program needn't handle non-finite values.
Results may differ from a plain program's by a relative error of at most 0.015.
Values may be sent and summed in bfloat16 or wider, within the bound.
A program may use at most 192 MiB of HBM per device.

v0:
```python
import math

import jax
import jax.numpy as jnp
from jax import lax
from jax.sharding import PartitionSpec as P

HEAD_DIM = 64


precise = lax.Precision.HIGHEST
epsilon = 1e-06
masked_value = -1e30


def rotary_tables(length, head_size):
    half_size = head_size // 2
    inverse = jnp.exp(
        jnp.arange(half_size, dtype=jnp.float32) * (-2.0 * math.log(10000.0) / head_size)
    )
    angles = jnp.arange(length, dtype=jnp.float32)[:, None] * inverse[None, :]
    return (jnp.cos(angles)[:, None, :], jnp.sin(angles)[:, None, :])


def rotate(values, cos_table, sin_table):
    half_size = values.shape[-1] // 2
    front_half = values[..., :half_size]
    back_half = values[..., half_size:]
    return jnp.concatenate(
        [
            front_half * cos_table - back_half * sin_table,
            back_half * cos_table + front_half * sin_table,
        ],
        axis=-1,
    )


def block_scores(queries, key_rows, segments_row, offset, block_rows):
    positions = jnp.arange(key_rows.shape[0])
    raw_scores = (
        jnp.einsum("qhd,khd->hqk", queries, key_rows, preferred_element_type=jnp.float32) * 0.125
    )
    allowed = (segments_row[offset : offset + block_rows, None] == segments_row[None, :]) & (
        positions[offset : offset + block_rows, None] >= positions[None, :]
    )
    return jnp.where(allowed[None], raw_scores, masked_value)


def body(
    tokens,
    segments,
    routes,
    prev_logits,
    ln1_gain,
    w_qkv,
    w_attn,
    ln2_gain,
    w_router,
    const_mix,
    const_vec,
    expert_in,
    expert_out,
    cotangent,
):
    length, model_width = tokens.shape
    head_count = model_width // HEAD_DIM
    block_rows = min(length, 512)
    local_experts = expert_in.shape[0]
    hidden_width = expert_out.shape[1]
    group_size = lax.axis_size("expert")
    ffn_experts = local_experts * group_size
    total_experts = w_router.shape[1]
    capacity = length // 2
    buffer_rows = ffn_experts * capacity
    segments_row = segments[0]
    tokens_f = tokens.astype(jnp.float32)
    scale_one = lax.rsqrt(jnp.mean(tokens_f * tokens_f, axis=-1, keepdims=True) + epsilon)
    normed_one = (tokens_f * scale_one * ln1_gain).astype(jnp.bfloat16)
    projected = jnp.dot(normed_one, w_qkv, preferred_element_type=jnp.float32).reshape(
        length, 3, head_count, HEAD_DIM
    )
    cos_table, sin_table = rotary_tables(length, HEAD_DIM)
    queries = rotate(projected[:, 0], cos_table, sin_table).astype(jnp.bfloat16)
    key_rows = rotate(projected[:, 1], cos_table, sin_table).astype(jnp.bfloat16)
    values = projected[:, 2].astype(jnp.bfloat16)
    offset = 0
    scores = block_scores(queries, key_rows, segments_row, offset, block_rows)
    row_max = jnp.max(scores, axis=-1, keepdims=True)
    exponent = jnp.exp(scores - row_max)
    row_total = jnp.sum(exponent, axis=-1, keepdims=True)
    weights_low = (exponent / row_total).astype(jnp.bfloat16)
    log_totals = [row_max + jnp.log(row_total)]
    attended_parts = jnp.einsum(
        "hqk,khd->qhd", weights_low, values, preferred_element_type=jnp.float32
    ).astype(jnp.bfloat16)
    attended = attended_parts.reshape(length, model_width)
    residual = tokens_f + jnp.dot(attended, w_attn, preferred_element_type=jnp.float32)
    scale_two = lax.rsqrt(jnp.mean(residual * residual, axis=-1, keepdims=True) + epsilon)
    normed_two = residual * scale_two * ln2_gain
    logits = jnp.dot(normed_two, w_router, precision=precise) + prev_logits
    expert_ids = jnp.arange(total_experts)
    choose = (routes[:, :, None] == expert_ids).astype(jnp.float32)
    chosen = jnp.sum(choose * logits[:, None, :], axis=-1)
    gate_weights = jax.nn.softmax(chosen, axis=-1)
    flat_routes = routes.reshape(2 * length)
    hit_table = (flat_routes[:, None] == expert_ids).astype(jnp.int32)
    earlier = jnp.cumsum(hit_table, axis=0) - hit_table
    slot_index = jnp.sum(earlier * hit_table, axis=-1).reshape(length, 2)
    targets = jnp.where(routes < ffn_experts, routes * capacity + slot_index, buffer_rows)
    pair_source = (
        jnp.full((buffer_rows + 1,), 2 * length, jnp.int32)
        .at[targets.reshape(-1)]
        .set(jnp.arange(2 * length, dtype=jnp.int32))[:buffer_rows]
    )
    normed_low = normed_two.astype(jnp.bfloat16)
    padded_rows = jnp.concatenate([normed_low, jnp.zeros((1, model_width), jnp.bfloat16)], axis=0)
    outgoing = padded_rows[pair_source // 2].reshape(
        group_size, local_experts * capacity, model_width
    )
    arriving = lax.all_to_all(outgoing, "expert", split_axis=0, concat_axis=0, tiled=True)
    arriving_rows = arriving.reshape(group_size, local_experts, capacity, model_width)
    gate_up = jnp.einsum(
        "sjcd,jdf->sjcf", arriving_rows, expert_in, preferred_element_type=jnp.float32
    )
    hidden = (jax.nn.silu(gate_up[..., :hidden_width]) * gate_up[..., hidden_width:]).astype(
        jnp.bfloat16
    )
    produced = jnp.einsum(
        "sjcf,jfd->sjcd", hidden, expert_out, preferred_element_type=jnp.float32
    ).astype(jnp.bfloat16)
    returned = lax.all_to_all(
        produced.reshape(group_size, local_experts * capacity, model_width),
        "expert",
        split_axis=0,
        concat_axis=0,
        tiled=True,
    )
    returned_pad = jnp.concatenate(
        [returned.reshape(buffer_rows, model_width), jnp.zeros((1, model_width), jnp.bfloat16)],
        axis=0,
    )
    ffn_out = returned_pad[targets].astype(jnp.float32)
    mixing = jnp.dot(normed_two, const_mix, precision=precise).reshape(length, 2, 2)
    shares = jax.nn.softmax(mixing, axis=-1)
    const_out = (
        shares[..., 0:1] * normed_two[:, None, :]
        + shares[..., 1:2] * jnp.transpose(const_vec)[None]
    )
    copy_mask = choose[:, :, ffn_experts + 1]
    const_mask = choose[:, :, ffn_experts + 2 :]
    expert_values = ffn_out + copy_mask[..., None] * normed_two[:, None, :]
    expert_values = expert_values + jnp.einsum(
        "lkj,ljd->lkd", const_mask, const_out, precision=precise
    )
    output = (residual + jnp.sum(gate_weights[..., None] * expert_values, axis=1)).astype(
        jnp.bfloat16
    )
    cot_rows = cotangent.astype(jnp.float32)
    d_expert = gate_weights[..., None] * cot_rows[:, None, :]
    d_gates = jnp.sum(cot_rows[:, None, :] * expert_values, axis=-1)
    d_chosen = gate_weights * (d_gates - jnp.sum(gate_weights * d_gates, axis=-1, keepdims=True))
    d_logits = jnp.sum(d_chosen[..., None] * choose, axis=1)
    router_local = jnp.einsum("ld,le->de", normed_two, d_logits, precision=precise)
    d_normed_two = jnp.einsum("le,de->ld", d_logits, w_router, precision=precise)
    d_normed_two = d_normed_two + jnp.sum(copy_mask[..., None] * d_expert, axis=1)
    d_const_out = jnp.einsum("lkj,lkd->ljd", const_mask, d_expert, precision=precise)
    d_share_first = jnp.sum(d_const_out * normed_two[:, None, :], axis=-1)
    d_share_second = jnp.sum(d_const_out * jnp.transpose(const_vec)[None], axis=-1)
    d_shares = jnp.stack([d_share_first, d_share_second], axis=-1)
    d_mixing = (shares * (d_shares - jnp.sum(shares * d_shares, axis=-1, keepdims=True))).reshape(
        length, 4
    )
    vec_local = jnp.einsum("lj,ljd->dj", shares[..., 1], d_const_out, precision=precise)
    d_normed_two = d_normed_two + jnp.sum(shares[..., 0:1] * d_const_out, axis=1)
    mix_local = jnp.einsum("ld,lm->dm", normed_two, d_mixing, precision=precise)
    d_normed_two = d_normed_two + jnp.einsum("lm,dm->ld", d_mixing, const_mix, precision=precise)
    d_pairs = jnp.concatenate(
        [
            d_expert.astype(jnp.bfloat16).reshape(2 * length, model_width),
            jnp.zeros((1, model_width), jnp.bfloat16),
        ],
        axis=0,
    )
    grad_outgoing = d_pairs[pair_source].reshape(group_size, local_experts * capacity, model_width)
    grad_arriving = lax.all_to_all(grad_outgoing, "expert", split_axis=0, concat_axis=0, tiled=True)
    grad_rows = grad_arriving.reshape(group_size, local_experts, capacity, model_width)
    gate_again = jnp.einsum(
        "sjcd,jdf->sjcf", arriving_rows, expert_in, preferred_element_type=jnp.float32
    )
    gate_part = gate_again[..., :hidden_width]
    up_part = gate_again[..., hidden_width:]
    sigmoid_gate = jax.nn.sigmoid(gate_part)
    silu_gate = gate_part * sigmoid_gate
    hidden_low = (silu_gate * up_part).astype(jnp.bfloat16)
    d_hidden = jnp.einsum(
        "sjcd,jfd->sjcf", grad_rows, expert_out, preferred_element_type=jnp.float32
    )
    d_gate_part = d_hidden * up_part * sigmoid_gate * (1.0 + gate_part * (1.0 - sigmoid_gate))
    d_gate_up = jnp.concatenate([d_gate_part, d_hidden * silu_gate], axis=-1).astype(jnp.bfloat16)
    d_sent = jnp.einsum(
        "sjcf,jdf->sjcd", d_gate_up, expert_in, preferred_element_type=jnp.float32
    ).astype(jnp.bfloat16)
    back_rows = lax.all_to_all(
        d_sent.reshape(group_size, local_experts * capacity, model_width),
        "expert",
        split_axis=0,
        concat_axis=0,
        tiled=True,
    )
    back_pad = jnp.concatenate(
        [back_rows.reshape(buffer_rows, model_width), jnp.zeros((1, model_width), jnp.bfloat16)],
        axis=0,
    )
    d_normed_two = d_normed_two + jnp.sum(back_pad[targets].astype(jnp.float32), axis=1)
    in_terms = jnp.einsum(
        "sjcd,sjcf->jdf", arriving_rows, d_gate_up, preferred_element_type=jnp.float32
    )
    out_terms = jnp.einsum(
        "sjcf,sjcd->jfd", hidden_low, grad_rows, preferred_element_type=jnp.float32
    )
    expert_in_grad, expert_out_grad = (
        lax.psum_scatter(in_terms, "dp", scatter_dimension=1, tiled=True),
        lax.psum_scatter(out_terms, "dp", scatter_dimension=1, tiled=True),
    )
    d_norm_two = d_normed_two * ln2_gain
    ln2_local = jnp.sum(d_normed_two * residual * scale_two, axis=0)
    d_residual = (
        cot_rows
        + scale_two * d_norm_two
        - residual * scale_two**3 * jnp.mean(d_norm_two * residual, axis=-1, keepdims=True)
    )
    d_branch = d_residual.astype(jnp.bfloat16)
    attn_local = jnp.einsum("ld,le->de", attended, d_branch, preferred_element_type=jnp.float32)
    d_attended = (
        jnp.einsum("le,de->ld", d_branch, w_attn, preferred_element_type=jnp.float32)
        .astype(jnp.bfloat16)
        .reshape(length, head_count, HEAD_DIM)
    )
    d_query_parts = []
    d_keys = jnp.zeros((length, head_count, HEAD_DIM), jnp.float32)
    d_values = jnp.zeros((length, head_count, HEAD_DIM), jnp.float32)
    for block_number, offset in enumerate(range(0, length, block_rows)):
        scores = block_scores(queries, key_rows, segments_row, offset, block_rows)
        weights = jnp.exp(scores - log_totals[block_number])
        d_weights = jnp.einsum(
            "qhd,khd->hqk", d_attended, values, preferred_element_type=jnp.float32
        )
        row_delta = jnp.sum(weights * d_weights, axis=-1, keepdims=True)
        d_scores = (weights * (d_weights - row_delta)).astype(jnp.bfloat16)
        d_query_parts.append(
            jnp.einsum("hqk,khd->qhd", d_scores, key_rows, preferred_element_type=jnp.float32)
            * 0.125
        )
        d_keys = (
            jnp.einsum("hqk,qhd->khd", d_scores, queries, preferred_element_type=jnp.float32)
            * 0.125
        )
        d_values = jnp.einsum(
            "hqk,qhd->khd",
            weights.astype(jnp.bfloat16),
            d_attended,
            preferred_element_type=jnp.float32,
        )
    d_queries = rotate(d_query_parts[0], cos_table, -sin_table)
    d_keys = rotate(d_keys, cos_table, -sin_table)
    d_projected = (
        jnp.stack([d_queries, d_keys, d_values], axis=1)
        .reshape(length, 3 * model_width)
        .astype(jnp.bfloat16)
    )
    qkv_local = jnp.einsum("ld,le->de", normed_one, d_projected, preferred_element_type=jnp.float32)
    d_normed_one = jnp.einsum("le,de->ld", d_projected, w_qkv, preferred_element_type=jnp.float32)
    d_norm_one = d_normed_one * ln1_gain
    ln1_local = jnp.sum(d_normed_one * tokens_f * scale_one, axis=0)
    input_grad = (
        d_residual
        + scale_one * d_norm_one
        - tokens_f * scale_one**3 * jnp.mean(d_norm_one * tokens_f, axis=-1, keepdims=True)
    ).astype(jnp.bfloat16)
    ln1_grad, qkv_grad, attn_grad, ln2_grad, router_grad, mix_grad, vec_grad = (
        lax.psum_scatter(ln1_local, ("dp", "expert"), scatter_dimension=0, tiled=True),
        lax.psum_scatter(qkv_local, ("dp", "expert"), scatter_dimension=0, tiled=True),
        lax.psum_scatter(attn_local, ("dp", "expert"), scatter_dimension=0, tiled=True),
        lax.psum_scatter(ln2_local, ("dp", "expert"), scatter_dimension=0, tiled=True),
        lax.psum_scatter(router_local, ("dp", "expert"), scatter_dimension=0, tiled=True),
        lax.psum_scatter(mix_local, ("dp", "expert"), scatter_dimension=0, tiled=True),
        lax.psum_scatter(vec_local, ("dp", "expert"), scatter_dimension=0, tiled=True),
    )
    return (
        output,
        input_grad,
        ln1_grad,
        qkv_grad,
        attn_grad,
        ln2_grad,
        router_grad,
        mix_grad,
        vec_grad,
        expert_in_grad,
        expert_out_grad,
    )


def solution(mesh):
    return jax.shard_map(
        body,
        mesh=mesh,
        in_specs=(
            P(("dp", "expert"), None),
            P(("dp", "expert"), None),
            P(("dp", "expert"), None),
            P(("dp", "expert"), None),
            P(),
            P(),
            P(),
            P(),
            P(),
            P(),
            P(),
            P("expert", None, None),
            P("expert", None, None),
            P(("dp", "expert"), None),
        ),
        out_specs=(
            P(("dp", "expert"), None),
            P(("dp", "expert"), None),
            P(("dp", "expert")),
            P(("dp", "expert"), None),
            P(("dp", "expert"), None),
            P(("dp", "expert")),
            P(("dp", "expert"), None),
            P(("dp", "expert"), None),
            P(("dp", "expert"), None),
            P("expert", "dp", None),
            P("expert", "dp", None),
        ),
        check_vma=False,
    )
```

profile of v0, /device:TPU:0, one launch (start us, length us, event | category | flops | bytes accessed | tf_op | source)
XLA Modules:
  0.0 889.9 jit_solution(3549372176465753529)
XLA Ops:
  13.7 3.3 fusion.67
  23.1 3.7 fusion
  27.7 17.1 %fusion.52 = bf16[12,64,512]{2,1,0:T(8,128)(2,1)S(1)} fusion(f32[12,512]{1,0:T(8,128)S(1)} %fusion, f32[12,512]{1,0:T(8,128)S(1)} %get-tuple-element.60, f32[12,512,512]{1,2,0:T(8,128)S(1)} %get-tuple-element.61, pred[512,512]{0,1:T(8,128)(4,1)} %copy-done.13, f32[512,3,12,64]{0,3,2,1:T(8,128)} %bitcast.174), kind=kOutput, calls=%fused_computation.93 | convolution fusion | flops 418775040 | bytes 14467072 | tf_op jit(solution)/shard_map/hqk,khd->qhd/dot_general | solution.py:93
  48.1 5.1 reduce-window.6
  64.2 5.0 scatter_custom_fusion
  70.5 2.8 fusion.97
  74.3 6.8 gather_fusion
  81.1 4.4 all-to-all-start
  86.1 2.8 convolution_add_fusion
  92.9 2.5 convert_element_type.101
  95.4 2.5 mul.636
  97.9 5.3 mul.650
  122.7 19.1 %multiply_reduce_fusion.2 = (f32[512,2]{1,0:T(8,128)}, f32[512,2]{1,0:T(8,128)}, f32[512,768]{1,0:T(8,128)}, f32[512,2,768]{2,1,0:T(2,128)}) fusion(f32[512,768]{1,0:T(8,128)} %get-tuple-element.29, f32[2,768]{1,0:T(2,128)} %bitcast.189, f32[512,2]{1,0:T(8,128)} %bitcast.180, pred[512,2,2]{1,2,0:T(4,128)(4,1)} %copy.165, ...), kind=kOutput, calls=%fused_computation.54 | convolution fusion | flops 23984128 | bytes 7888896 | tf_op jit(solution)/shard_map/lkj,lkd->ljd/dot_general | solution.py:166
  152.5 7.8 gather_fusion.2
  163.1 4.4 all-to-all-start.2
  167.5 12.4 %convolution_bitcast_fusion = f32[4,1,256,4096]{3,2,0,1:T(8,128)} fusion(bf16[4,256,768]{2,1,0:T(8,128)(2,1)} %all-to-all-done, bf16[1,768,4096]{2,1,0:T(8,128)(2,1)} %param.25), kind=kOutput, calls=%fused_computation.13 | convolution fusion | flops 6442450944 | bytes 24641536 | tf_op jit(solution)/shard_map/sjcd,jdf->sjcf/dot_general | solution.py:122
  179.9 8.3 all-to-all-done.2
  188.3 14.4 %fusion.17 = (bf16[4,256,2048]{2,1,0:T(8,128)(2,1)}, bf16[4,256,2048]{2,1,0:T(8,128)(2,1)}, bf16[4,256,2048]{2,1,0:T(8,128)(2,1)S(1)}) fusion(f32[4,1,256,4096]{3,2,0,1:T(8,128)} %convolution_bitcast_fusion, bf16[4,256,768]{2,1,0:T(8,128)(2,1)} %all-to-all-done.2, bf16[1,2048,768]{2,1,0:T(8,128)(2,1)} %param.26), kind=kOutput, calls=%fused_computation.34 | convolution fusion | flops 3252682752 | bytes 34078720 | tf_op jit(solution)/shard_map/sjcd,jfd->sjcf/dot_general | solution.py:195
  204.6 4.5 fusion.31
  209.1 4.4 all-to-all-start.1
  213.5 11.9 %fusion.28 = bf16[4,256,768]{2,1,0:T(8,128)(2,1)} fusion(bf16[1,768,4096]{2,1,0:T(8,128)(2,1)} %param.25, bf16[4,256,2048]{2,1,0:T(8,128)(2,1)} %get-tuple-element.31, bf16[4,256,2048]{2,1,0:T(8,128)(2,1)} %get-tuple-element.30), kind=kOutput, calls=%fused_computation.62 | convolution fusion | flops 6460014592 | bytes 16252928 | tf_op jit(solution)/shard_map/sjcf,jdf->sjcd/dot_general | solution.py:200
  225.3 8.3 all-to-all-done.1
  233.6 4.3 all-to-all-start.3
  238.0 2.7 concatenate.43
  240.7 7.4 gather_fusion.1
  248.1 4.8 reshape.464
  252.9 28.8 %multiply_reduce_fusion.4 = (f32[512,2]{1,0:T(8,128)}, f32[512,768]{1,0:T(8,128)}, f32[512,768]{1,0:T(8,128)}) fusion(f32[512,768]{1,0:T(8,128)} %convert_element_type.101, f32[512,2]{1,0:T(8,128)} %copy.153, f32[512,2]{1,0:T(8,128)} %copy.159, pred[512,2,2]{1,2,0:T(4,128)(4,1)} %copy.165, f32[2,768]{1,0:T(2,128)} %bitcast.190, f32[512,2]{1,0:T(8,128)} %bitcast.182, ...), kind=kOutput, calls=%fused_computation.56 | convolution fusion | flops 28310528 | bytes 9465856 | tf_op jit(solution)/shard_map/lkj,ljd->lkd/dot_general | solution.py:152
  285.5 3.3 fusion.102
  288.8 2.7 concatenate.48
  291.5 7.2 gather_fusion.3
  298.7 4.9 reshape.465
  303.6 6.8 reduce_sum.214
  310.4 6.0 multiply_reduce_fusion.6
  321.8 2.3 copy.169
  324.7 13.3 %multiply_reduce_fusion = (f32[12,512]{1,0:T(8,128)S(1)}, f32[12,512,512]{1,2,0:T(8,128)}) fusion(f32[12,512]{1,0:T(8,128)} %log_add_fusion, f32[12,512,512]{1,2,0:T(8,128)} %copy-done.1, pred[512,512]{0,1:T(8,128)(4,1)} %copy-done.13, bf16[512,12,64]{0,2,1:T(8,128)(2,1)} %bitcast.176, f32[512,3,12,64]{0,3,2,1:T(8,128)} %bitcast.175), kind=kOutput, calls=%fused_computation.6 | convolution fusion | flops 418375680 | bytes 27058176 | tf_op jit(solution)/shard_map/qhd,khd->hqk/dot_general | solution.py:245
  338.0 7.2 multiply_convert_fusion
  350.2 3.1 fusion.53
  355.0 5.1 fusion.65
  360.3 8.9 convolution_bitcast_fusion.2
  369.3 13.3 %convolution_bitcast_fusion.1 = f32[1,768,4096]{2,1,0:T(8,128)} fusion(bf16[4,256,768]{2,1,0:T(8,128)(2,1)} %all-to-all-done, bf16[4,256,2048]{2,1,0:T(8,128)(2,1)} %get-tuple-element.31, bf16[4,256,2048]{2,1,0:T(8,128)(2,1)} %get-tuple-element.30), kind=kOutput, calls=%fused_computation.24 | convolution fusion | flops 6459228160 | bytes 22544384 | tf_op jit(solution)/shard_map/sjcd,sjcf->jdf/dot_general | solution.py:215
  382.6 3.6 fusion.25
  386.9 3.1 fusion.104
  391.5 5.6 fusion.42
  397.1 43.3 %all-reduce.9 = (f32[768]{0:T(1024)}, f32[768]{0:T(1024)}, f32[768,8]{0,1:T(8,128)}, f32[768,4]{0,1:T(4,128)}, f32[768,2]{0,1:T(2,128)}) all-reduce(f32[768]{0:T(1024)} %get-tuple-element.18, f32[768]{0:T(1024)} %get-tuple-element.11, f32[768,8]{0,1:T(8,128)} %fusion.103, ...), channel_id=2, replica_groups=mesh['dp'=8,'expert'=4] {'dp','expert'}, use_global_device_ids=true, to_apply=%region_27.28.clone | all-reduce | flops 12288 | bytes 98304
  447.6 3.6 fusion.39
  451.2 100.1 %reduce-scatter.8.cloned.1.call-done = f32[24,2304]{1,0:T(8,128)} async-done(((f32[768,2304]{1,0:T(8,128)}), f32[24,2304]{1,0:T(8,128)}) %reduce-scatter.8.cloned.1.call-update) | async-done | bytes 221200 | tf_op jit(solution)/shard_map/reduce_scatter | solution.py:282
  551.3 121.4 %reduce-scatter.14.cloned.1.call-done = f32[1,256,768]{2,1,0:T(8,128)} async-done(((f32[1,2048,768]{2,1,0:T(8,128)}), f32[1,256,768]{2,1,0:T(8,128)}) %reduce-scatter.14.cloned.1.call-update) | async-done | bytes 786448 | tf_op jit(solution)/shard_map/reduce_scatter | solution.py:223
  672.7 210.5 %reduce-scatter.12.cloned.1.call-done = f32[1,96,4096]{2,1,0:T(8,128)} async-done(((f32[1,768,4096]{2,1,0:T(8,128)}), f32[1,96,4096]{2,1,0:T(8,128)}) %reduce-scatter.12.cloned.1.call-update) | async-done | bytes 1572880 | tf_op jit(solution)/shard_map/reduce_scatter | solution.py:222
  (225 shorter events, 95.2 us)
Async XLA Ops:
  7.2 6.5 copy-start
  13.7 3.3 copy-start.48
  17.0 3.0 copy-start.56
  20.8 2.3 copy-start.16
  23.1 4.5 copy-start.1
  23.1 4.5 copy-start.33
  27.7 17.1 %copy-start.34 = (f32[12,512]{1,0:T(8,128)}, f32[12,512]{1,0:T(8,128)S(1)}, u32[]{:S(2)}) copy-start(f32[12,512]{1,0:T(8,128)S(1)} %fusion) | copy-start | bytes 73732
  27.7 17.2 %copy-start.9 = (bf16[512,768]{1,0:T(8,128)(2,1)S(1)}, bf16[512,768]{1,0:T(8,128)(2,1)}, u32[]{:S(2)}) copy-start(bf16[512,768]{1,0:T(8,128)(2,1)} %param.14) | copy-start | bytes 2359300
  27.7 17.2 %copy-start.59 = (bf16[768,768]{1,0:T(8,128)(2,1)S(1)}, bf16[768,768]{1,0:T(8,128)(2,1)}, u32[]{:S(2)}) copy-start(bf16[768,768]{1,0:T(8,128)(2,1)} %param.20) | copy-start | bytes 3538948
  44.8 2.6 copy-start.54
  44.9 15.4 %copy-start.35 = (s32[512,2]{0,1:T(2,128)S(1)}, s32[512,2]{0,1:T(2,128)}, u32[]{:S(2)}) copy-start(s32[512,2]{0,1:T(2,128)} %param.16) | copy-start | bytes 12292
  44.9 25.6 %copy-start.46 = (f32[768]{0:T(1024)S(1)}, f32[768]{0:T(1024)}, u32[]{:S(2)}) copy-start(f32[768]{0:T(1024)} %param.21) | copy-start | bytes 9220
  47.5 25.8 %copy-start.51 = (f32[512]{0:T(512)}, f32[512]{0:T(512)S(1)}, u32[]{:S(2)}) copy-start(f32[512]{0:T(512)S(1)} %get-tuple-element.56) | copy-start | bytes 6148
  81.1 82.0 %all-to-all-start = ((bf16[4,256,768]{2,1,0:T(8,128)(2,1)}), bf16[4,256,768]{2,1,0:T(8,128)(2,1)}, u32[]{:S(2)}, u32[]{:S(2)}) async-start(bf16[4,256,768]{2,1,0:T(8,128)(2,1)} %bitcast.171), calls=%async_computation | async-start | bytes 3145728 | tf_op jit(solution)/shard_map/all_to_all | solution.py:120
  89.0 8.9 copy-start.42
  89.1 8.9 copy-start.53
  92.9 2.5 copy-start.7
  152.5 7.9 copy-start.55
  163.1 25.1 %all-to-all-start.2 = ((bf16[4,256,768]{2,1,0:T(8,128)(2,1)}), bf16[4,256,768]{2,1,0:T(8,128)(2,1)}, u32[]{:S(2)}, u32[]{:S(2)}) async-start(bf16[4,256,768]{2,1,0:T(8,128)(2,1)} %bitcast.172), calls=%async_computation.2 | async-start | bytes 3145728 | tf_op jit(solution)/shard_map/all_to_all | solution.py:185
  188.2 16.4 %copy-start.58 = (bf16[1,2048,768]{2,1,0:T(8,128)(2,1)S(1)}, bf16[1,2048,768]{2,1,0:T(8,128)(2,1)}, u32[]{:S(2)}) copy-start(bf16[1,2048,768]{2,1,0:T(8,128)(2,1)} %param.26) | copy-start | bytes 9437188
  209.1 24.5 %all-to-all-start.1 = ((bf16[4,256,768]{2,1,0:T(8,128)(2,1)}), bf16[4,256,768]{2,1,0:T(8,128)(2,1)}, u32[]{:S(2)}, u32[]{:S(2)}) async-start(bf16[4,256,768]{2,1,0:T(8,128)(2,1)} %fusion.31), calls=%async_computation.1 | async-start | bytes 3145728 | tf_op jit(solution)/shard_map/all_to_all | solution.py:131
  233.6 55.2 %all-to-all-start.3 = ((bf16[4,256,768]{2,1,0:T(8,128)(2,1)}), bf16[4,256,768]{2,1,0:T(8,128)(2,1)}, u32[]{:S(2)}, u32[]{:S(2)}) async-start(bf16[4,256,768]{2,1,0:T(8,128)(2,1)} %fusion.28), calls=%async_computation.3 | async-start | bytes 3145728 | tf_op jit(solution)/shard_map/all_to_all | solution.py:203
  238.0 213.2 %reduce-scatter.10.cloned.1.call-start = ((), (), s32[]{:S(2)}) async-start(), calls=%async_computation.9 | async-start | bytes 2433024 | tf_op jit(solution)/shard_map/reduce_scatter | solution.py:283
  252.9 30.5 %copy-start.43 = (f32[512]{0:T(512)S(1)}, f32[512]{0:T(512)}, u32[]{:S(2)}) copy-start(f32[512]{0:T(512)} %copy-done.42) | copy-start | bytes 6148
  303.6 6.8 copy-start.39
  303.6 6.8 copy-start.47
  303.6 6.8 copy-start.52
  310.4 6.0 copy-start.4
  310.4 6.0 copy-start.8
  310.4 6.0 copy-start.20
  310.4 6.0 copy-start.57
  324.1 227.2 %reduce-scatter.8.cloned.1.call-start = ((), (), s32[]{:S(2)}) async-start(), calls=%async_computation.8 | async-start | bytes 7299072 | tf_op jit(solution)/shard_map/reduce_scatter | solution.py:282
  324.6 13.4 %slice-start = ((s8[12582912]{0:T(1024)(128)(4,1)}), s8[4194304]{0:T(1024)(128)(4,1)S(1)}, s32[]{:S(2)}) async-start(s8[12582912]{0:T(1024)(128)(4,1)} %bitcast.167), calls=%async_computation.12 | async-start | bytes 8388608
  324.6 13.4 %slice-start.1 = ((s8[12582912]{0:T(1024)(128)(4,1)}), s8[4194304]{0:T(1024)(128)(4,1)S(1)}, s32[]{:S(2)}) async-start(s8[12582912]{0:T(1024)(128)(4,1)} %bitcast.167), calls=%async_computation.13 | async-start | bytes 8388608
  324.6 13.3 %slice-start.2 = ((s8[12582912]{0:T(1024)(128)(4,1)}), s8[4194304]{0:T(1024)(128)(4,1)S(1)}, s32[]{:S(2)}) async-start(s8[12582912]{0:T(1024)(128)(4,1)} %bitcast.167), calls=%async_computation.14 | async-start | bytes 8388608
  324.6 13.3 %copy-start.14 = (pred[512,512]{0,1:T(8,128)(4,1)S(1)}, pred[512,512]{0,1:T(8,128)(4,1)}, u32[]{:S(2)}) copy-start(pred[512,512]{0,1:T(8,128)(4,1)} %copy-done.13) | copy-start | bytes 786436
  324.7 13.3 %copy-start.29 = (f32[12,512]{1,0:T(8,128)S(1)}, f32[12,512]{1,0:T(8,128)}, u32[]{:S(2)}) copy-start(f32[12,512]{1,0:T(8,128)} %log_add_fusion) | copy-start | bytes 73732
  338.0 7.2 copy-start.17
  338.0 7.2 copy-start.19
  360.1 312.6 %reduce-scatter.14.cloned.1.call-start = ((), (), s32[]{:S(2)}) async-start(), calls=%async_computation.11 | async-start | bytes 7077888 | tf_op jit(solution)/shard_map/reduce_scatter | solution.py:223
  369.2 514.0 %reduce-scatter.12.cloned.1.call-start = ((), (), s32[]{:S(2)}) async-start(), calls=%async_computation.10 | async-start | bytes 14155776 | tf_op jit(solution)/shard_map/reduce_scatter | solution.py:222
  382.6 7.3 copy-start.32
  386.9 3.1 copy-start.3
  386.9 4.6 copy-start.11
  386.9 4.6 copy-start.37
  386.9 4.6 copy-start.50
  391.5 5.6 copy-start.45
  391.5 56.1 %copy-start.38 = (f32[768]{0:T(1024)S(1)}, f32[768]{0:T(1024)}, u32[]{:S(2)}) copy-start(f32[768]{0:T(1024)} %param.18) | copy-start | bytes 9220
  (25 other events, 40.4 us)
Sparse Core Ops, SparseCore 0:
  324.2 101.4 reduce-scatter.9
  433.0 118.2 reduce-scatter.7
  555.5 117.2 reduce-scatter.13
  676.7 206.4 reduce-scatter.11
where the time goes:
time: 894 us; the launch traced here: 890 us
  waiting for transfers between devices  449 us (50%)
  matrix products  194 us (22%)
  local copies, waits for them, and re-layouts  113 us (13%)
  other arithmetic  57.3 us (6%)
  blocking collectives  43.3 us (5%)
  starting transfers between devices  18.2 us (2%)
  between operations  14.7 us (2%)
    reduce_scatter x1, waiting for transfers between devices, body(): lax.psum_scatter(in_terms, 'dp', scatter_dimension=1, tiled=True)  210 us
    reduce_scatter x1, waiting for transfers between devices, body(): lax.psum_scatter(out_terms, 'dp', scatter_dimension=1, tiled=True)  121 us
    reduce_scatter x1, waiting for transfers between devices, body(): lax.psum_scatter(qkv_local, ('dp', 'expert'), scatter_dimension=0, tiled=...  100 us
    unnamed x1, blocking collectives  43.3 us
    dot_general x1, matrix products, body(): jnp.einsum('lkj,ljd->lkd', const_mask, const_out, precision=precise)  28.8 us
    dot_general x1, matrix products, body(): jnp.einsum('lkj,lkd->ljd', const_mask, d_expert, precision=precise)  19.1 us
  transfers between devices with their start and end apart: 8, of which 5 were waited for; matrix products, arithmetic and copies ran while one was open for 26% of the time, Pallas kernels for 0%

commit v1 on v0

v1 whole, which is shorter than its diff:
```python
import functools
import math

import jax
import jax.numpy as jnp
import numpy as np
from jax import lax
from jax.experimental import pallas as pl
from jax.experimental.pallas import tpu as pltpu
from jax.sharding import PartitionSpec as P

HEAD_DIM = 64
EPS = 1e-06
MASKED = -1e30
F32 = jnp.float32
BF16 = jnp.bfloat16
VMEM_LIMIT = 62 * 1024 * 1024


def dot(a, b):
    return lax.dot_general(a, b, (((1,), (0,)), ((), ())), preferred_element_type=F32)


def dot_nt(a, b):
    return lax.dot_general(a, b, (((1,), (1,)), ((), ())), preferred_element_type=F32)


def dot_tn(a, b):
    return lax.dot_general(a, b, (((0,), (0,)), ((), ())), preferred_element_type=F32)


def tile(i, size):
    return pl.ds(pl.multiple_of(i * size, size), size)


def rotary_tables(length):
    half = HEAD_DIM // 2
    inverse = np.exp(np.arange(half, dtype=np.float32) * np.float32(-2.0 * math.log(10000.0) / HEAD_DIM))
    angles = np.arange(length, dtype=np.float32)[:, None] * inverse.astype(np.float32)[None, :]
    cos, sin = np.cos(angles), np.sin(angles)
    return (
        np.concatenate([cos] * 4, axis=1).astype(np.float32),
        np.concatenate([-sin, sin] * 2, axis=1).astype(np.float32),
    )


def rotate(x, cos, sin):
    lane = lax.broadcasted_iota(jnp.int32, x.shape, 1)
    front = (lane % HEAD_DIM) < HEAD_DIM // 2
    other = jnp.where(front, pltpu.roll(x, 96, 1), pltpu.roll(x, 32, 1))
    return x * cos + other * sin


def row_mean(x):
    return jnp.mean(x, axis=-1, keepdims=True)


def pick(x, lane, index):
    return jnp.sum(jnp.where(lane == index, x, 0.0), axis=-1, keepdims=True)


def half_mask(x, lane, which):
    keep = (lane < HEAD_DIM) if which == 0 else (lane >= HEAD_DIM)
    return jnp.where(keep, x, jnp.zeros_like(x))


def fwd_kernel(
    tok, seg, rT, pT, ln1, wqkv, wattn, ln2, wrT, cmT, cot, cos, sin,
    q, k, v, pw, att, n1, res, meta, send,
    proj, bias, wcat, rb, pb, n2b, n2l, gd,
):
    length, width = tok.shape
    capacity = length // 2
    experts = send.shape[0]

    @pl.loop(0, length // 64)
    def _(i):
        rows = tile(i, 64)
        x = tok[rows].astype(F32)
        r = lax.rsqrt(row_mean(x * x) + EPS)
        n1[rows] = (x * r * ln1[...]).astype(BF16)

    for kind, dst in enumerate((q, k, v)):

        @pl.loop(0, width // 256)
        def _(j):
            cols = pl.ds(pl.multiple_of(kind * width + j * 256, 256), 256)
            proj[...] = dot(n1[...], wqkv[:, cols])

            @pl.loop(0, length // 128)
            def _(i):
                rows = tile(i, 128)
                for part in range(2):
                    x = proj[rows, part * 128 : part * 128 + 128]
                    if kind < 2:
                        x = rotate(x, cos[rows], sin[rows])
                    if kind == 0:
                        x = x * 0.125
                    dst[rows, pl.ds(pl.multiple_of(j * 256 + part * 128, 128), 128)] = x.astype(BF16)

    seg_f = seg[...].astype(F32)
    rb[0] = jnp.transpose(jnp.broadcast_to(seg_f, (128, length)))

    @pl.loop(0, length // 128)
    def _(i):
        rows = tile(i, 128)
        row_id = lax.broadcasted_iota(jnp.int32, (128, length), 0) + i * 128
        col_id = lax.broadcasted_iota(jnp.int32, (128, length), 1)
        same = rb[0, rows, 0:1] == seg_f
        bias[rows] = jnp.where(same & (row_id >= col_id), 0.0, MASKED)

    block = length // 2

    @pl.loop(0, width // 128)
    def _(j):
        cols = tile(j, 128)
        for b in range(2):
            rows = slice(b * block, (b + 1) * block)
            nk = (b + 1) * block
            qlane = lax.broadcasted_iota(jnp.int32, (block, 128), 1)
            klane = lax.broadcasted_iota(jnp.int32, (nk, 128), 1)
            acc = jnp.zeros((block, 128), F32)
            for h in range(2):
                s = dot_nt(half_mask(q[rows, cols], qlane, h), k[0:nk, cols]) + bias[rows, 0:nk]
                m = jnp.max(s, axis=-1, keepdims=True)
                e = jnp.exp(s - m)
                w = (e * (1.0 / jnp.sum(e, axis=-1, keepdims=True))).astype(BF16)
                pw[2 * j + h, rows, 0:nk] = w
                acc = acc + dot(w, half_mask(v[0:nk, cols], klane, h))
            att[rows, cols] = acc.astype(BF16)

    @pl.loop(0, width // 256)
    def _(j):
        cols = tile(j, 256)
        res[:, cols] = tok[:, cols].astype(F32) + dot(att[...], wattn[:, cols])

    @pl.loop(0, length // 64)
    def _(i):
        rows = tile(i, 64)
        x = res[rows]
        n2 = x * lax.rsqrt(row_mean(x * x) + EPS) * ln2[...]
        high = n2.astype(BF16)
        n2b[rows] = high
        n2l[rows] = (n2 - high.astype(F32)).astype(BF16)

    wcat[...] = jnp.zeros_like(wcat)
    wcat[0:8] = wrT[...]
    wcat[8:12] = cmT[...]
    w_high = wcat[...].astype(BF16)
    w_low = (wcat[...] - w_high.astype(F32)).astype(BF16)

    for kk in range(2):
        rb[kk] = jnp.transpose(jnp.broadcast_to(rT[kk : kk + 1, :].astype(F32), (128, length)))
    pb[...] = jnp.zeros_like(pb)
    pb[0:8] = pT[...]
    rb[2] = jnp.transpose(pb[...])

    @pl.loop(0, length // 128)
    def _(i):
        rows = tile(i, 128)
        lane = lax.broadcasted_iota(jnp.int32, (128, 128), 1)
        lane_f = lane.astype(F32)
        high = n2b[rows]
        mixed = dot_nt(high, w_high) + dot_nt(high, w_low) + dot_nt(n2l[rows], w_high)
        logits = mixed + rb[2, rows]
        hits = [(rb[kk, rows] == lane_f).astype(F32) for kk in range(2)]
        chosen = [jnp.sum(h * logits, axis=-1, keepdims=True) for h in hits]
        top = jnp.maximum(chosen[0], chosen[1])
        e = [jnp.exp(c - top) for c in chosen]
        inv = 1.0 / (e[0] + e[1])
        gates = [v_ * inv for v_ in e]
        shares = []
        for j in range(2):
            a0, a1 = pick(mixed, lane, 8 + 2 * j), pick(mixed, lane, 9 + 2 * j)
            mx = jnp.maximum(a0, a1)
            b0, b1 = jnp.exp(a0 - mx), jnp.exp(a1 - mx)
            binv = 1.0 / (b0 + b1)
            shares.append((b0 * binv, b1 * binv))
        t_id = lax.broadcasted_iota(jnp.int32, (128, length), 0) + i * 128
        before = (t_id > lax.broadcasted_iota(jnp.int32, (128, length), 1)).astype(F32).astype(BF16)
        all_lane = lax.broadcasted_iota(jnp.int32, (length, 128), 1).astype(F32)
        count = ((rb[0] == all_lane).astype(F32) + (rb[1] == all_lane).astype(F32)).astype(BF16)
        place = dot(before, count) + lane_f * float(capacity) + 1.0
        target = [
            jnp.sum(jnp.where(lane < experts, h * place, 0.0), axis=-1, keepdims=True) - 1.0
            for h in hits
        ]
        gate_sum = gates[0] * hits[0] + gates[1] * hits[1]
        cg = [pick(gate_sum, lane, 6), pick(gate_sum, lane, 7)]
        keep = pick(gate_sum, lane, 5) + cg[0] * shares[0][0] + cg[1] * shares[1][0]
        values = (
            target[0], target[1], gates[0], gates[1], keep, cg[0], cg[1],
            shares[0][0], shares[0][1], shares[1][0], shares[1][1],
        )
        out = jnp.zeros((128, 128), F32)
        for n, value in enumerate(values):
            out = jnp.where(lane == n, value, out)
        meta[rows] = out
        g = cot[rows].astype(F32)
        for kk in range(2):
            gd[pl.ds(pl.multiple_of(kk * length + i * 128, 128), 128)] = (g * gates[kk]).astype(BF16)

    meta_t = jnp.transpose(meta[...])

    @pl.loop(0, experts)
    def _(e):
        s_id = (lax.broadcasted_iota(jnp.int32, (capacity, length), 0) + e * capacity).astype(F32)
        first = (meta_t[0:1] == s_id).astype(F32).astype(BF16)
        second = (meta_t[1:2] == s_id).astype(F32).astype(BF16)
        send[e, 0:capacity] = dot(first + second, n2b[...]).astype(BF16)
        send[e, capacity : 2 * capacity] = (
            dot(first, gd[0:length]) + dot(second, gd[length : 2 * length])
        ).astype(BF16)


def expert_kernel(arr, win, wout, ret, d_in, d_out, x, dy, hid, dgu, ffn, dsent):
    groups, both, width = arr.shape
    capacity = both // 2
    hidden = wout.shape[1]
    ft = hid.shape[1]
    for s in range(groups):
        x[s * capacity : (s + 1) * capacity] = arr[s, 0:capacity]
        dy[s * capacity : (s + 1) * capacity] = arr[s, capacity:both]

    @pl.loop(0, hidden // ft)
    def _(f):
        gate_cols = tile(f, ft)
        up_cols = pl.ds(pl.multiple_of(hidden + f * ft, ft), ft)

        @pl.loop(0, groups)
        def _(s):
            rows = tile(s, capacity)
            gate = dot(x[rows], win[0, :, gate_cols])
            up = dot(x[rows], win[0, :, up_cols])
            dh = dot_nt(dy[rows], wout[0, gate_cols, :])
            sig = 1.0 / (1.0 + jnp.exp(-gate))
            silu = gate * sig
            hid[rows] = (silu * up).astype(BF16)
            dgu[rows, 0:ft] = (dh * up * sig * (1.0 + gate * (1.0 - sig))).astype(BF16)
            dgu[rows, ft : 2 * ft] = (dh * silu).astype(BF16)

        d_in[:, gate_cols] = dot_tn(x[...], dgu[:, 0:ft]).astype(BF16)
        d_in[:, up_cols] = dot_tn(x[...], dgu[:, ft : 2 * ft]).astype(BF16)
        d_out[gate_cols] = dot_tn(hid[...], dy[...]).astype(BF16)

        @pl.loop(0, groups)
        def _(s):
            rows = tile(s, capacity)
            y = dot(hid[rows], wout[0, gate_cols, :])
            d = dot_nt(dgu[rows, 0:ft], win[0, :, gate_cols]) + dot_nt(
                dgu[rows, ft : 2 * ft], win[0, :, up_cols]
            )

            @pl.when(f == 0)
            def _():
                ffn[rows] = y
                dsent[rows] = d

            @pl.when(f > 0)
            def _():
                ffn[rows] += y
                dsent[rows] += d

    for s in range(groups):
        ret[s, 0:capacity] = ffn[s * capacity : (s + 1) * capacity].astype(BF16)
        ret[s, capacity:both] = dsent[s * capacity : (s + 1) * capacity].astype(BF16)


def bwd_kernel(
    tok, cot, res, meta, rT, ret, q, k, v, pw, att, n1, ln1, wqkv, wattn, ln2, wrT, cmT, cvT, cos, sin,
    out, igrad, d_qkv, d_attn, d_small,
    wcat, rb, fk0, fk1, dsn, dcat, n2b, dres, dbr, dproj, datt, dkv, lnacc, rr,
):
    length, width = tok.shape
    experts, both, _ = ret.shape
    capacity = both // 2

    wcat[...] = jnp.zeros_like(wcat)
    wcat[0:8] = wrT[...]
    wcat[8:12] = cmT[...]
    for kk in range(2):
        rb[kk] = jnp.transpose(jnp.broadcast_to(rT[kk : kk + 1, :].astype(F32), (128, length)))

    for s in range(experts):
        rr[s * capacity : (s + 1) * capacity] = ret[s, 0:capacity]
        rr[(experts + s) * capacity : (experts + s + 1) * capacity] = ret[s, capacity:both]
    slots = experts * capacity

    @pl.loop(0, length // 256)
    def _(i):
        rows = tile(i, 256)
        s_id = lax.broadcasted_iota(jnp.int32, (256, slots), 1).astype(F32)
        first = (meta[rows, 0:1] == s_id).astype(F32).astype(BF16)
        second = (meta[rows, 1:2] == s_id).astype(F32).astype(BF16)
        fk0[rows] = dot(first, rr[0:slots])
        fk1[rows] = dot(second, rr[0:slots])
        dsn[rows] = dot(first + second, rr[slots : 2 * slots])

    w_high = wcat[...].astype(BF16)
    lnacc[...] = jnp.zeros_like(lnacc)

    @pl.loop(0, length // 64)
    def _(i):
        rows = tile(i, 64)
        lane = lax.broadcasted_iota(jnp.int32, (64, 128), 1)
        lane_f = lane.astype(F32)
        m = meta[rows]
        g0, g1, keep = m[:, 2:3], m[:, 3:4], m[:, 4:5]
        cg = (m[:, 5:6], m[:, 6:7])
        shares = ((m[:, 7:8], m[:, 8:9]), (m[:, 9:10], m[:, 10:11]))
        g = cot[rows].astype(F32)
        x = res[rows]
        r2 = lax.rsqrt(row_mean(x * x) + EPS)
        xr = x * r2
        n2 = xr * ln2[...]
        n2b[rows] = n2.astype(BF16)
        f0, f1 = fk0[rows], fk1[rows]
        cv = (cvT[0:1, :], cvT[1:2, :])
        out[rows] = (
            x + g0 * f0 + g1 * f1 + keep * n2 + (cg[0] * shares[0][1]) * cv[0] + (cg[1] * shares[1][1]) * cv[1]
        ).astype(BF16)
        gn2 = jnp.sum(g * n2, axis=-1, keepdims=True)
        gcv = [jnp.sum(g * c, axis=-1, keepdims=True) for c in cv]
        hits = [(rb[kk, rows] == lane_f).astype(F32) for kk in range(2)]
        special = jnp.where(lane == 5, gn2, 0.0)
        for j in range(2):
            special = jnp.where(lane == 6 + j, shares[j][0] * gn2 + shares[j][1] * gcv[j], special)
        dg = [
            jnp.sum(g * f, axis=-1, keepdims=True) + jnp.sum(h * special, axis=-1, keepdims=True)
            for f, h in zip((f0, f1), hits)
        ]
        mean_dg = g0 * dg[0] + g1 * dg[1]
        dc0, dc1 = g0 * (dg[0] - mean_dg), g1 * (dg[1] - mean_dg)
        cat = hits[0] * dc0 + hits[1] * dc1
        for j in range(2):
            dm0, dm1 = cg[j] * gn2, cg[j] * gcv[j]
            mean_dm = shares[j][0] * dm0 + shares[j][1] * dm1
            cat = jnp.where(lane == 8 + 2 * j, shares[j][0] * (dm0 - mean_dm), cat)
            cat = jnp.where(lane == 9 + 2 * j, shares[j][1] * (dm1 - mean_dm), cat)
        dcat[rows, 0:128] = cat.astype(BF16)
        vecs = jnp.where(lane == 12, cg[0] * shares[0][1], 0.0)
        vecs = jnp.where(lane == 13, cg[1] * shares[1][1], vecs)
        dcat[rows, 128:256] = vecs.astype(BF16)
        dn2 = keep * g + dsn[rows] + dot(cat.astype(BF16), w_high)
        lnacc[0:8] += jnp.sum((dn2 * xr).reshape(8, 8, width), axis=0)
        dn = dn2 * ln2[...]
        dr = g + r2 * dn - xr * (r2 * r2) * row_mean(dn * x)
        dres[rows] = dr
        dbr[rows] = dr.astype(BF16)

    d_small[...] = dot_tn(n2b[...], dcat[:, 0:128]) + dot_tn(cot[...], dcat[:, 128:256])

    @pl.loop(0, width // 256)
    def _(j):
        cols = tile(j, 256)
        datt[:, cols] = dot_nt(dbr[...], wattn[cols, :]).astype(BF16)
        d_attn[:, cols] = dot_tn(att[...], dbr[:, cols])

    block = length // 2

    @pl.loop(0, width // 128)
    def _(j):
        cols = tile(j, 128)
        dkv[...] = jnp.zeros_like(dkv)
        for b in range(2):
            rows = slice(b * block, (b + 1) * block)
            nk = (b + 1) * block
            qlane = lax.broadcasted_iota(jnp.int32, (block, 128), 1)
            klane = lax.broadcasted_iota(jnp.int32, (nk, 128), 1)
            do = datt[rows, cols]
            prod = do.astype(F32) * att[rows, cols].astype(F32)
            dq = jnp.zeros((block, 128), F32)
            for h in range(2):
                delta = jnp.sum(half_mask(prod, qlane, h), axis=-1, keepdims=True)
                dom = half_mask(do, qlane, h)
                dp = dot_nt(dom, v[0:nk, cols])
                w = pw[2 * j + h, rows, 0:nk]
                ds = (w.astype(F32) * (dp - delta)).astype(BF16)
                dq = dq + dot(ds, half_mask(k[0:nk, cols], klane, h))
                dkv[0, 0:nk] += dot_tn(ds, half_mask(q[rows, cols], qlane, h))
                dkv[1, 0:nk] += dot_tn(w, dom)
            dproj[rows, cols] = rotate(dq * 0.125, cos[rows], -sin[rows]).astype(BF16)
        dproj[:, pl.ds(pl.multiple_of(width + j * 128, 128), 128)] = rotate(dkv[0], cos[...], -sin[...]).astype(BF16)
        dproj[:, pl.ds(pl.multiple_of(2 * width + j * 128, 128), 128)] = dkv[1].astype(BF16)

    @pl.loop(0, 3 * width // 256)
    def _(j):
        cols = tile(j, 256)
        d_qkv[:, cols] = dot_tn(n1[...], dproj[:, cols])

    @pl.loop(0, width // 256)
    def _(j):
        cols = tile(j, 256)
        fk0[:, cols] = dot_nt(dproj[...], wqkv[cols, :])

    @pl.loop(0, length // 64)
    def _(i):
        rows = tile(i, 64)
        x = tok[rows].astype(F32)
        r1 = lax.rsqrt(row_mean(x * x) + EPS)
        xr = x * r1
        d = fk0[rows]
        dn = d * ln1[...]
        lnacc[8:16] += jnp.sum((d * xr).reshape(8, 8, width), axis=0)
        igrad[rows] = (dres[rows] + r1 * dn - xr * (r1 * r1) * row_mean(dn * x)).astype(BF16)

    ln = jnp.zeros((128, width), F32)
    row = lax.broadcasted_iota(jnp.int32, (128, width), 0)
    ln = jnp.where(row == 14, jnp.sum(lnacc[8:16], axis=0, keepdims=True), ln)
    ln = jnp.where(row == 15, jnp.sum(lnacc[0:8], axis=0, keepdims=True), ln)
    d_small[...] += jnp.transpose(ln)


def shape(*s, dtype=BF16):
    return jax.ShapeDtypeStruct(s, dtype)


def call(kernel, outs, scratch, args, name):
    return pl.pallas_call(
        kernel,
        out_shape=outs,
        in_specs=[pl.BlockSpec(memory_space=pltpu.VMEM)] * len(args),
        out_specs=[pl.BlockSpec(memory_space=pltpu.VMEM)] * len(outs),
        scratch_shapes=scratch,
        compiler_params=pltpu.CompilerParams(vmem_limit_bytes=VMEM_LIMIT),
        name=name,
    )(*args)


def body(
    tokens, segments, routes, prev_logits, ln1_gain, w_qkv, w_attn, ln2_gain, w_router, const_mix, const_vec,
    expert_in, expert_out, cotangent,
):
    length, width = tokens.shape
    heads = width // HEAD_DIM
    experts = lax.axis_size("expert") * expert_in.shape[0]
    hidden = expert_out.shape[1]
    capacity = length // 2
    slots = experts * capacity
    V = pltpu.VMEM
    cos, sin = (jnp.asarray(t) for t in rotary_tables(length))
    rT, pT = routes.T, prev_logits.T
    wrT, cmT, cvT = w_router.T, const_mix.T, const_vec.T
    ln1, ln2 = ln1_gain.reshape(1, width), ln2_gain.reshape(1, width)

    q, k, v, pw, att, n1, res, meta, send = call(
        fwd_kernel,
        [
            shape(length, width), shape(length, width), shape(length, width), shape(heads, length, length),
            shape(length, width), shape(length, width), shape(length, width, dtype=F32),
            shape(length, 128, dtype=F32), shape(experts, length, width),
        ],
        [
            V((length, 256), F32), V((length, length), F32), V((128, width), F32), V((3, length, 128), F32),
            V((128, length), F32), V((length, width), BF16), V((length, width), BF16), V((2 * length, width), BF16),
        ],
        (tokens, segments, rT, pT, ln1, w_qkv, w_attn, ln2, wrT, cmT, cotangent, cos, sin),
        "attention",
    )
    arr = lax.all_to_all(send, "expert", split_axis=0, concat_axis=0, tiled=True)
    ft = 256
    ret, d_in, d_out = call(
        expert_kernel,
        [shape(experts, length, width), shape(width, 2 * hidden), shape(hidden, width)],
        [
            V((slots, width), BF16), V((slots, width), BF16), V((slots, ft), BF16), V((slots, 2 * ft), BF16),
            V((slots, width), F32), V((slots, width), F32),
        ],
        (arr, expert_in, expert_out),
        "experts",
    )
    back = lax.all_to_all(ret, "expert", split_axis=0, concat_axis=0, tiled=True)
    g_in = lax.psum_scatter(d_in, "dp", scatter_dimension=0, tiled=True).astype(F32)[None]
    g_out = lax.psum_scatter(d_out, "dp", scatter_dimension=0, tiled=True).astype(F32)[None]
    out, igrad, d_qkv, d_attn, d_small = call(
        bwd_kernel,
        [
            shape(length, width), shape(length, width), shape(width, 3 * width, dtype=F32),
            shape(width, width, dtype=F32), shape(width, 128, dtype=F32),
        ],
        [
            V((128, width), F32), V((2, length, 128), F32), V((length, width), F32), V((length, width), F32),
            V((length, width), F32), V((length, 256), BF16), V((length, width), BF16), V((length, width), F32),
            V((length, width), BF16), V((length, 3 * width), BF16), V((length, width), BF16),
            V((2, length, 128), F32), V((16, width), F32), V((2 * slots, width), BF16),
        ],
        (
            tokens, cotangent, res, meta, rT, back, q, k, v, pw, att, n1, ln1, w_qkv, w_attn, ln2, wrT, cmT, cvT,
            cos, sin,
        ),
        "backward",
    )
    both = ("dp", "expert")
    d_qkv = lax.psum_scatter(d_qkv, both, scatter_dimension=0, tiled=True)
    d_attn = lax.psum_scatter(d_attn, both, scatter_dimension=0, tiled=True)
    small = lax.psum_scatter(d_small, both, scatter_dimension=0, tiled=True)
    return (
        out, igrad, small[:, 14], d_qkv, d_attn, small[:, 15], small[:, 0:8], small[:, 8:12], small[:, 12:14],
        g_in, g_out,
    )


def solution(mesh):
    rows = P(("dp", "expert"), None)
    return jax.shard_map(
        body,
        mesh=mesh,
        in_specs=(
            rows, rows, rows, rows, P(), P(), P(), P(), P(), P(), P(),
            P("expert", None, None), P("expert", None, None), rows,
        ),
        out_specs=(
            rows, rows, P(("dp", "expert")), rows, rows, P(("dp", "expert")), rows, rows, rows,
            P("expert", "dp", None), P("expert", "dp", None),
        ),
        check_vma=False,
    )
```

time: 894 us -> 667 us (0.75)
  matrix products: 194 us -> 0 us
  Pallas kernels: 0 us -> 132 us
  local copies, waits for them, and re-layouts: 113 us -> 8.24 us
  other arithmetic: 57.3 us -> 4.34 us
  blocking collectives: 43.3 us -> 85.2 us
  waiting for transfers between devices: 449 us -> 421 us
  starting transfers between devices: 18.2 us -> 0.2 us
    dot_general x27 -> x0, matrix products: 194 us -> none  [the longest x1 28.8 us: body(): jnp.einsum('lkj,ljd->lkd', const_mask, const_out, precision=precise)]
    reduce_scatter x4, waiting for transfers between devices: 432 us -> 256 us  [the longest x1 124 us: body(): d_qkv = lax.psum_scatter(d_qkv, both, scatter_dimension=0, tiled=True)]
    unnamed x4 -> x6, waiting for transfers between devices: 0.07 us -> 166 us
    pallas_call x0 -> x3, Pallas kernels: none -> 132 us  [call(): pl.pallas_call(kernel, out_shape=outs, in_specs=[pl.BlockSpec(memory_spac...]
    all_to_all x0 -> x2, blocking collectives: none -> 85.2 us  [the longest x1 42.9 us: body(): lax.all_to_all(send, 'expert', split_axis=0, concat_axis=0, tiled=True)]
    unnamed x1 -> x0, blocking collectives: 43.3 us -> none
    gather x4 -> x0, local copies, waits for them, and re-layouts: 29.2 us -> none  [the longest x1 7.85 us: body(): d_pairs[pair_source]]
    convert_element_type x6 -> x0, other arithmetic: 18.7 us -> none  [the longest x1 7.17 us: body(): d_scores = (weights * (d_weights - row_delta)).astype(jnp.bfloat16)]
  transfers between devices with their start and end apart: 8 -> 5, of which waited for: 5 -> 4; matrix products, arithmetic and copies ran while one was open for 26% -> 2% of each run, Pallas kernels for 0% -> 0%
where the time goes in v1:
time: 667 us
  waiting for transfers between devices  421 us (63%)
  Pallas kernels  132 us (20%)
  blocking collectives  85.2 us (13%)
  between operations  15.7 us (2%)
  local copies, waits for them, and re-layouts  8.24 us (1%)
    unnamed x6, waiting for transfers between devices  166 us
    pallas_call x3, Pallas kernels, call(): pl.pallas_call(kernel, out_shape=outs, in_specs=[pl.BlockSpec(memory_spac...  132 us
    reduce_scatter x1, waiting for transfers between devices, body(): d_qkv = lax.psum_scatter(d_qkv, both, scatter_dimension=0, tiled=True)  124 us
    reduce_scatter x1, waiting for transfers between devices, body(): d_attn = lax.psum_scatter(d_attn, both, scatter_dimension=0, tiled=True)  102 us
    all_to_all x1, blocking collectives, body(): lax.all_to_all(send, 'expert', split_axis=0, concat_axis=0, tiled=True)  42.9 us
    all_to_all x1, blocking collectives, body(): lax.all_to_all(ret, 'expert', split_axis=0, concat_axis=0, tiled=True)  42.3 us
    reduce_scatter x1, waiting for transfers between devices, body(): lax.psum_scatter(d_in, 'dp', scatter_dimension=0, tiled=True).astype(F32)  29.1 us
  transfers between devices with their start and end apart: 5, of which 4 were waited for; matrix products, arithmetic and copies ran while one was open for 2% of the time, Pallas kernels for 0%

profile of v1, /device:TPU:0, one launch (start us, length us, event | category | flops | bytes accessed | tf_op | source)
XLA Modules:
  0.0 666.7 jit_solution(8618670321954372353)
XLA Ops:
  8.0 0.0 all-reduce.3.cloned.1.call-start
  8.1 1.3 reshape.28.ln1
  9.3 1.3 reshape.29.ln2
  10.6 31.7 %attention.1 = (bf16[512,768]{1,0:T(8,128)(2,1)}, bf16[512,768]{1,0:T(8,128)(2,1)}, bf16[512,768]{1,0:T(8,128)(2,1)}, bf16[12,512,512]{2,1,0:T(8,128)(2,1)}, bf1...) custom-call(bf16[512,768]{1,0:T(8,128)(2,1)} %tok.3, ...), custom_call_target="tpu_custom_call" | custom-call | tf_op jit(solution)/shard_map/attention/pallas_call | solution.py:419
  42.3 42.9 %all_to_all.10.arr = bf16[4,512,768]{2,1,0:T(8,128)(2,1)} all-to-all(bf16[4,512,768]{2,1,0:T(8,128)(2,1)} %get-tuple-element.30), channel_id=1, replica_groups=mesh['dp'=8,'expert'=4] {'expert'}, dimensions={0} | all-to-all | bytes 6291456 | tf_op jit(solution)/shard_map/all_to_all | solution.py:460
  85.2 56.9 %experts.1 = (bf16[4,512,768]{2,1,0:T(8,128)(2,1)}, bf16[768,4096]{1,0:T(8,128)(2,1)}, bf16[2048,768]{1,0:T(8,128)(2,1)}) custom-call(bf16[4,512,768]{2,1,0:T(8,128)(2,1)} %all_to_all.10.arr, bf16[1,768,4096]{2,1,0:T(8,128)(2,1)} %win.1, bf16[1,2048,768]{2,1,0:T(8,128)(2,1)} %wout.1), custom_call_target="tpu_custom_call" | custom-call | tf_op jit(solution)/shard_map/experts/pallas_call | solution.py:419
  142.0 42.3 %all_to_all.11.ret = bf16[4,512,768]{2,1,0:T(8,128)(2,1)} all-to-all(bf16[4,512,768]{2,1,0:T(8,128)(2,1)} %get-tuple-element.31), channel_id=1, replica_groups=mesh['dp'=8,'expert'=4] {'expert'}, dimensions={0} | all-to-all | bytes 6291456 | tf_op jit(solution)/shard_map/all_to_all | solution.py:472
  184.3 43.4 %backward.1 = (bf16[512,768]{1,0:T(8,128)(2,1)}, bf16[512,768]{1,0:T(8,128)(2,1)}, f32[768,2304]{1,0:T(8,128)}, f32[768,768]{1,0:T(8,128)}, f32[768,128]{1,0:T(8,128)}) custom-call(bf16[512,768]{1,0:T(8,128)(2,1)} %tok.3, bf16[512,768]{1,0:T(8,128)(2,1)} %cot.3, f32[512,768]{1,0:T(8,128)} %get-tuple-element.28.res, f32[512,128]{1,0:T(8,128)} %get-tuple-element.29.meta, ...), custom_call_target="tpu_custom_call" | custom-call | tf_op jit(solution)/shard_map/backward/pallas_call | solution.py:419
  227.7 0.0 all-reduce.3.cloned.1.call-update
  227.8 0.0 reduce-scatter.11.cloned.1.call-start
  227.8 0.5 reduce-scatter.11.cloned.1.call-update
  228.3 0.0 reduce-scatter.9.cloned.1.call-start
  228.4 0.5 reduce-scatter.9.cloned.1.call-update
  228.9 0.0 reduce-scatter.7.cloned.1.call-start
  229.0 0.5 reduce-scatter.7.cloned.1.call-update
  229.5 0.0 reduce-scatter.5.cloned.1.call-start
  229.6 0.7 reduce-scatter.5.cloned.1.call-update
  230.2 163.3 %all-reduce.3.cloned.1.call-done = f32[768,128]{1,0:T(8,128)} async-done(((f32[768,128]{1,0:T(8,128)}), f32[768,128]{1,0:T(8,128)}) %all-reduce.3.cloned.1.call-update) | async-done | bytes 393232
  393.5 0.8 dynamic-slice.4
  394.3 0.7 copy.34
  395.0 0.8 dynamic-slice.5
  395.8 0.6 copy.35
  396.4 0.7 constant_dynamic-slice_fusion
  397.1 0.7 copy.33
  397.8 1.5 dynamic-slice_reduce_fusion
  399.3 0.0 reduce-scatter.11.cloned.1.call-done
  399.3 1.9 bitcast_convert_fusion.1
  401.2 29.1 %reduce-scatter.9.cloned.1.call-done = bf16[96,4096]{1,0:T(8,128)(2,1)} async-done(((bf16[768,4096]{1,0:T(8,128)(2,1)}), bf16[96,4096]{1,0:T(8,128)(2,1)}) %reduce-scatter.9.cloned.1.call-update) | async-done | bytes 786448 | tf_op jit(solution)/shard_map/reduce_scatter | solution.py:473
  430.2 2.4 bitcast_convert_fusion
  432.7 102.3 %reduce-scatter.7.cloned.1.call-done = f32[24,768]{1,0:T(8,128)} async-done(((f32[768,768]{1,0:T(8,128)}), f32[24,768]{1,0:T(8,128)}) %reduce-scatter.7.cloned.1.call-update) | async-done | bytes 73744 | tf_op jit(solution)/shard_map/reduce_scatter | solution.py:495
  535.0 124.1 %reduce-scatter.5.cloned.1.call-done = f32[24,2304]{1,0:T(8,128)} async-done(((f32[768,2304]{1,0:T(8,128)}), f32[24,2304]{1,0:T(8,128)}) %reduce-scatter.5.cloned.1.call-update) | async-done | bytes 221200 | tf_op jit(solution)/shard_map/reduce_scatter | solution.py:494
Async XLA Ops:
  8.0 385.5 %all-reduce.3.cloned.1.call-start = ((), (), s32[]{:S(2)}) async-start(), calls=%async_computation.10 | async-start | bytes 786432
  227.8 171.5 %reduce-scatter.11.cloned.1.call-start = ((), (), s32[]{:S(2)}) async-start(), calls=%async_computation.9 | async-start | bytes 3538944 | tf_op jit(solution)/shard_map/reduce_scatter | solution.py:474
  228.3 201.9 %reduce-scatter.9.cloned.1.call-start = ((), (), s32[]{:S(2)}) async-start(), calls=%async_computation.8 | async-start | bytes 7077888 | tf_op jit(solution)/shard_map/reduce_scatter | solution.py:473
  228.9 306.0 %reduce-scatter.7.cloned.1.call-start = ((), (), s32[]{:S(2)}) async-start(), calls=%async_computation.7 | async-start | bytes 2433024 | tf_op jit(solution)/shard_map/reduce_scatter | solution.py:495
  229.5 429.6 %reduce-scatter.5.cloned.1.call-start = ((), (), s32[]{:S(2)}) async-start(), calls=%async_computation.6 | async-start | bytes 7299072 | tf_op jit(solution)/shard_map/reduce_scatter | solution.py:494
Sparse Core Ops, SparseCore 0:
  227.9 165.6 all-reduce.2
Sparse Core Ops, SparseCore 1:
  232.2 76.6 reduce-scatter.10
  312.8 117.4 reduce-scatter.8
  436.8 98.1 reduce-scatter.6
  541.2 117.8 reduce-scatter.4

commit v2 on v1

v2 whole, which is shorter than its diff:
```python
import functools
import math

import jax
import jax.numpy as jnp
import numpy as np
from jax import lax
from jax.experimental import pallas as pl
from jax.experimental.pallas import tpu as pltpu
from jax.sharding import PartitionSpec as P

HEAD_DIM = 64
EPS = 1e-06
MASKED = -1e30
F32 = jnp.float32
BF16 = jnp.bfloat16
VMEM_LIMIT = 62 * 1024 * 1024


def dot(a, b):
    return lax.dot_general(a, b, (((1,), (0,)), ((), ())), preferred_element_type=F32)


def dot_nt(a, b):
    return lax.dot_general(a, b, (((1,), (1,)), ((), ())), preferred_element_type=F32)


def dot_tn(a, b):
    return lax.dot_general(a, b, (((0,), (0,)), ((), ())), preferred_element_type=F32)


def tile(i, size):
    return pl.ds(pl.multiple_of(i * size, size), size)


def rotary_tables(length):
    half = HEAD_DIM // 2
    inverse = np.exp(np.arange(half, dtype=np.float32) * np.float32(-2.0 * math.log(10000.0) / HEAD_DIM))
    angles = np.arange(length, dtype=np.float32)[:, None] * inverse.astype(np.float32)[None, :]
    cos, sin = np.cos(angles), np.sin(angles)
    return (
        np.concatenate([cos] * 4, axis=1).astype(np.float32),
        np.concatenate([-sin, sin] * 2, axis=1).astype(np.float32),
    )


def rotate(x, cos, sin):
    lane = lax.broadcasted_iota(jnp.int32, x.shape, 1)
    front = (lane % HEAD_DIM) < HEAD_DIM // 2
    other = jnp.where(front, pltpu.roll(x, 96, 1), pltpu.roll(x, 32, 1))
    return x * cos + other * sin


def row_mean(x):
    return jnp.mean(x, axis=-1, keepdims=True)


def pick(x, lane, index):
    return jnp.sum(jnp.where(lane == index, x, 0.0), axis=-1, keepdims=True)


def half_mask(x, lane, which):
    keep = (lane < HEAD_DIM) if which == 0 else (lane >= HEAD_DIM)
    return jnp.where(keep, x, jnp.zeros_like(x))


MESH = pl.DeviceIdType.MESH


def flip(i, m):
    return i + m * (1 - 2 * ((i // m) % 2))


def side(mask):
    axis, m = mask
    return (lax.axis_index(axis) // m) % 2


def partner(mask):
    axis, m = mask
    return {axis: flip(lax.axis_index(axis), m)}


def greet(masks, shifts=0):
    barrier = pltpu.get_barrier_semaphore()
    for mask in masks:
        pl.semaphore_signal(barrier, inc=1, device_id=partner(mask), device_id_type=MESH)
    n = lax.axis_size("expert")
    for o in range(1, shifts + 1):
        dest = lax.rem(lax.axis_index("expert") + o, n)
        pl.semaphore_signal(barrier, inc=1, device_id={"expert": dest}, device_id_type=MESH)
    pl.semaphore_wait(barrier, len(masks) + shifts)


def exchange(src, dst, send_sem, recv_sem):
    n = lax.axis_size("expert")
    me = lax.axis_index("expert")
    copies = []
    for o in range(1, n):
        dest = lax.rem(me + o, n)
        copies.append(
            pltpu.make_async_remote_copy(
                src.at[dest], dst.at[me], send_sem.at[o - 1], recv_sem.at[o - 1],
                device_id={"expert": dest}, device_id_type=MESH,
            )
        )
    return copies


def half_copy(src, dst, mask, rows, send_sem, recv_sem):
    start = pl.multiple_of((1 - side(mask)) * rows, 8)
    return pltpu.make_async_remote_copy(
        src.at[pl.ds(start, rows)], dst, send_sem, recv_sem, device_id=partner(mask), device_id_type=MESH
    )


def half_add(src, dst, mask, rows, out=None):
    start = side(mask) * rows
    step = 48 if rows % 48 == 0 else 64 if rows % 64 == 0 else 24
    out = dst if out is None else out

    @pl.loop(0, rows // step)
    def _(i):
        here = pl.ds(pl.multiple_of(i * step, 8), step)
        mine = src[pl.ds(pl.multiple_of(start + i * step, 8), step)].astype(F32)
        out[here] = (mine + dst[here].astype(F32)).astype(out.dtype)


def place_of(shard, masks):
    place = 0
    for m in masks:
        place = 2 * place + (shard // m) % 2
    return place


def fwd_kernel(
    tok, seg, rT, pT, ln1, wqkv, wattn, ln2, wrT, cmT, cot, cos, sin,
    q, k, v, pw, att, n1, res, meta, send, g_rows,
    proj, bias, wcat, rb, pb, n2b, n2l, gl, tg, onehot, g_out, send_sem, recv_sem,
):
    length, width = tok.shape
    capacity = length // 2
    experts = send.shape[0]

    greet((), experts - 1)
    for kk in range(2):
        rb[kk] = jnp.transpose(jnp.broadcast_to(rT[kk : kk + 1, :].astype(F32), (128, length)))
    all_lane = lax.broadcasted_iota(jnp.int32, (length, 128), 1).astype(F32)
    count = ((rb[0] == all_lane).astype(F32) + (rb[1] == all_lane).astype(F32)).astype(BF16)

    @pl.loop(0, length // 128)
    def _(i):
        rows = tile(i, 128)
        lane = lax.broadcasted_iota(jnp.int32, (128, 128), 1)
        lane_f = lane.astype(F32)
        t_id = lax.broadcasted_iota(jnp.int32, (128, length), 0) + i * 128
        before = (t_id > lax.broadcasted_iota(jnp.int32, (128, length), 1)).astype(F32).astype(BF16)
        place = dot(before, count) + lane_f * float(capacity) + 1.0
        out = jnp.zeros((128, 128), F32)
        for kk in range(2):
            hit = (rb[kk, rows] == lane_f) & (lane < experts)
            out = jnp.where(lane == kk, jnp.sum(jnp.where(hit, place, 0.0), axis=-1, keepdims=True) - 1.0, out)
        tg[rows] = out

    target = jnp.transpose(tg[...])
    pb[...] = target

    @pl.loop(0, experts)
    def _(e):
        s_id = (lax.broadcasted_iota(jnp.int32, (capacity, length), 0) + e * capacity).astype(F32)
        here = (pb[0:1] == s_id).astype(F32) + (pb[1:2] == s_id).astype(F32)
        onehot[tile(e, capacity)] = here.astype(BF16)
        g_out[e] = dot(here.astype(BF16), cot[...]).astype(BF16)

    copies = exchange(g_out, g_rows, send_sem, recv_sem)
    for c in copies:
        c.start()
    me = lax.axis_index("expert")
    g_rows[me] = g_out[me]

    @pl.loop(0, length // 64)
    def _(i):
        rows = tile(i, 64)
        x = tok[rows].astype(F32)
        r = lax.rsqrt(row_mean(x * x) + EPS)
        n1[rows] = (x * r * ln1[...]).astype(BF16)

    for kind, dst in enumerate((q, k, v)):

        @pl.loop(0, width // 256)
        def _(j):
            cols = pl.ds(pl.multiple_of(kind * width + j * 256, 256), 256)
            proj[...] = dot(n1[...], wqkv[:, cols])

            @pl.loop(0, length // 128)
            def _(i):
                rows = tile(i, 128)
                for part in range(2):
                    x = proj[rows, part * 128 : part * 128 + 128]
                    if kind < 2:
                        x = rotate(x, cos[rows], sin[rows])
                    if kind == 0:
                        x = x * 0.125
                    dst[rows, pl.ds(pl.multiple_of(j * 256 + part * 128, 128), 128)] = x.astype(BF16)

    seg_f = seg[...].astype(F32)
    rb[2] = jnp.transpose(jnp.broadcast_to(seg_f, (128, length)))

    @pl.loop(0, length // 128)
    def _(i):
        rows = tile(i, 128)
        row_id = lax.broadcasted_iota(jnp.int32, (128, length), 0) + i * 128
        col_id = lax.broadcasted_iota(jnp.int32, (128, length), 1)
        same = rb[2, rows, 0:1] == seg_f
        bias[rows] = jnp.where(same & (row_id >= col_id), 0.0, MASKED)

    block = length // 2

    @pl.loop(0, width // 128)
    def _(j):
        cols = tile(j, 128)
        for b in range(2):
            rows = slice(b * block, (b + 1) * block)
            nk = (b + 1) * block
            qlane = lax.broadcasted_iota(jnp.int32, (block, 128), 1)
            klane = lax.broadcasted_iota(jnp.int32, (nk, 128), 1)
            acc = jnp.zeros((block, 128), F32)
            for h in range(2):
                s = dot_nt(half_mask(q[rows, cols], qlane, h), k[0:nk, cols]) + bias[rows, 0:nk]
                m = jnp.max(s, axis=-1, keepdims=True)
                e = jnp.exp(s - m)
                w = (e * (1.0 / jnp.sum(e, axis=-1, keepdims=True))).astype(BF16)
                pw[2 * j + h, rows, 0:nk] = w
                acc = acc + dot(w, half_mask(v[0:nk, cols], klane, h))
            att[rows, cols] = acc.astype(BF16)

    @pl.loop(0, width // 256)
    def _(j):
        cols = tile(j, 256)
        res[:, cols] = tok[:, cols].astype(F32) + dot(att[...], wattn[:, cols])

    @pl.loop(0, length // 64)
    def _(i):
        rows = tile(i, 64)
        x = res[rows]
        n2 = x * lax.rsqrt(row_mean(x * x) + EPS) * ln2[...]
        high = n2.astype(BF16)
        n2b[rows] = high
        n2l[rows] = (n2 - high.astype(F32)).astype(BF16)

    wcat[...] = jnp.zeros_like(wcat)
    wcat[0:8] = wrT[...]
    wcat[8:12] = cmT[...]
    w_high = wcat[...].astype(BF16)
    w_low = (wcat[...] - w_high.astype(F32)).astype(BF16)

    pb[8:16] = pT[...]
    rb[2] = jnp.transpose(jnp.concatenate([pb[8:16], jnp.zeros((120, length), F32)], axis=0))

    @pl.loop(0, length // 128)
    def _(i):
        rows = tile(i, 128)
        lane = lax.broadcasted_iota(jnp.int32, (128, 128), 1)
        lane_f = lane.astype(F32)
        high = n2b[rows]
        mixed = dot_nt(high, w_high) + dot_nt(high, w_low) + dot_nt(n2l[rows], w_high)
        logits = mixed + rb[2, rows]
        hits = [(rb[kk, rows] == lane_f).astype(F32) for kk in range(2)]
        chosen = [jnp.sum(h * logits, axis=-1, keepdims=True) for h in hits]
        top = jnp.maximum(chosen[0], chosen[1])
        e = [jnp.exp(c - top) for c in chosen]
        inv = 1.0 / (e[0] + e[1])
        gates = [v_ * inv for v_ in e]
        shares = []
        for j in range(2):
            a0, a1 = pick(mixed, lane, 8 + 2 * j), pick(mixed, lane, 9 + 2 * j)
            mx = jnp.maximum(a0, a1)
            b0, b1 = jnp.exp(a0 - mx), jnp.exp(a1 - mx)
            binv = 1.0 / (b0 + b1)
            shares.append((b0 * binv, b1 * binv))
        gate_sum = gates[0] * hits[0] + gates[1] * hits[1]
        cg = [pick(gate_sum, lane, 6), pick(gate_sum, lane, 7)]
        keep = pick(gate_sum, lane, 5) + cg[0] * shares[0][0] + cg[1] * shares[1][0]
        values = (
            gates[0], gates[1], keep, cg[0], cg[1], shares[0][0], shares[0][1], shares[1][0], shares[1][1],
        )
        out = tg[rows]
        for n, value in enumerate(values):
            out = jnp.where(lane == n + 2, value, out)
        meta[rows] = out
        for kk in range(2):
            g_high = gates[kk].astype(BF16).astype(F32)
            both = jnp.where(lane == 0, g_high, jnp.where(lane == 1, gates[kk] - g_high, 0.0))
            gl[pl.ds(pl.multiple_of(kk * length + i * 128, 128), 128)] = both.astype(BF16)

    @pl.loop(0, experts)
    def _(e):
        s_id = (lax.broadcasted_iota(jnp.int32, (capacity, length), 0) + e * capacity).astype(F32)
        gate = jnp.zeros((capacity, 128), F32)
        for kk in range(2):
            here = (pb[kk : kk + 1] == s_id).astype(F32).astype(BF16)
            gate = gate + dot(here, gl[kk * length : (kk + 1) * length])
        send[e, :, 0:width] = dot(onehot[tile(e, capacity)], n2b[...]).astype(BF16)
        send[e, :, width : width + 128] = gate.astype(BF16)

    for c in copies:
        c.wait()


def expert_kernel(stages, xs, g_rows, win, wout, *refs):
    if stages:
        f_back, d_back, p_in, p_out = refs[:4]
        refs = refs[4:]
    else:
        f_back, d_back, gi, go = refs[:4]
        refs = refs[4:]
    xr, dy, hid, fa, fb, dgu, acc, stage = refs[:8]
    refs = refs[8:]
    if stages:
        gi, go, in_send, in_recv, out_send, out_recv = refs[:6]
        refs = refs[6:]
    x_send, x_recv, f_send, f_recv, d_send, d_recv = refs
    groups, capacity, wide = xs.shape
    hidden, width = wout.shape[1:]
    tiles, _, ft = hid.shape
    slabs = go.shape[0]
    me = lax.axis_index("expert")

    greet([s[0] for s in stages[:2]], groups - 1)
    copies = exchange(xs, xr, x_send, x_recv)
    for c in copies:
        c.start()
    xr[me] = xs[me]
    for c in copies:
        c.wait()
    for s in range(groups):
        pair = xr[s, :, width:wide].astype(F32)
        lane = lax.broadcasted_iota(jnp.int32, pair.shape, 1)
        gate = jnp.sum(jnp.where(lane < 2, pair, 0.0), axis=-1, keepdims=True)
        dy[s] = (g_rows[s].astype(F32) * gate).astype(BF16)

    @pl.loop(0, tiles)
    def _(f):
        gate_cols = tile(f, ft)
        up_cols = pl.ds(pl.multiple_of(hidden + f * ft, ft), ft)

        @pl.loop(0, groups)
        def _(s):
            rows = tile(s, capacity)
            gate = dot(xr[s, :, 0:width], win[0, :, gate_cols])
            up = dot(xr[s, :, 0:width], win[0, :, up_cols])
            sig = 1.0 / (1.0 + jnp.exp(-gate))
            silu = gate * sig
            h = (silu * up).astype(BF16)
            hid[f, rows] = h
            fa[f, rows] = (up * sig * (1.0 + gate * (1.0 - sig))).astype(BF16)
            fb[f, rows] = silu.astype(BF16)
            y = dot(h, wout[0, gate_cols, :])

            @pl.when(f == 0)
            def _():
                acc[s] = y

            @pl.when(f > 0)
            def _():
                acc[s] += y

    stage[0] = acc[...].astype(BF16)
    f_copies = exchange(stage.at[0], f_back, f_send, f_recv)
    for c in f_copies:
        c.start()
    f_back[me] = stage[0, me]

    shards = 2 ** len(stages[0]) if stages else 0
    in_rows, out_rows = width // 2, hidden // 2
    half = tiles // 2
    for part in range(2):
        masks = stages[part] if stages else ()

        @pl.loop(part * half, (part + 1) * half)
        def _(f):
            gate_cols = tile(f, ft)
            up_cols = pl.ds(pl.multiple_of(hidden + f * ft, ft), ft)

            @pl.loop(0, groups)
            def _(s):
                rows = tile(s, capacity)
                dh = dot_nt(dy[s], wout[0, gate_cols, :])
                da = (dh * fa[f, rows].astype(F32)).astype(BF16)
                db = (dh * fb[f, rows].astype(F32)).astype(BF16)
                dgu[rows, 0:ft] = da
                dgu[rows, ft : 2 * ft] = db
                d = dot_nt(da, win[0, :, gate_cols]) + dot_nt(db, win[0, :, up_cols])

                @pl.when(f == 0)
                def _():
                    acc[s] = d

                @pl.when(f > 0)
                def _():
                    acc[s] += d

            for p in range(2):
                cols = slice(p * ft, (p + 1) * ft)
                d = dot_tn(xr[:, :, 0:width].reshape(groups * capacity, width), dgu[:, cols])
                if not stages:
                    gi[f, :, cols] = d.astype(BF16)
                    continue
                size = width // shards
                for j in range(shards):
                    at = place_of(j, [m for _, m in masks]) * size
                    gi[f, at : at + size, cols] = d[j * size : (j + 1) * size].astype(BF16)
            if stages:
                half_copy(gi.at[f], p_in.at[f], masks[0], in_rows, in_send.at[f], in_recv.at[f]).start()

    stage[1] = acc[...].astype(BF16)
    d_copies = exchange(stage.at[1], d_back, d_send, d_recv)
    for c in d_copies:
        c.start()
    d_back[me] = stage[1, me]

    out_copies = []
    size = hidden // tiles
    for c in range(slabs):
        cols = slice(c * (width // slabs), (c + 1) * (width // slabs))
        masks = stages[c % 2] if stages else ()

        @pl.loop(0, tiles)
        def _(t):
            at = place_of(t, [m for _, m in masks]) if stages else t
            go[c, tile(at, size)] = dot_tn(hid[t], dy[:, :, cols].reshape(groups * capacity, width // slabs)).astype(BF16)

        if stages:
            out_copies.append(half_copy(go.at[c], p_out.at[c], masks[0], out_rows, out_send.at[c], out_recv.at[c]))
            out_copies[-1].start()

    if stages:
        for part in range(2):
            masks = stages[part]

            @pl.loop(part * half, (part + 1) * half)
            def _(f):
                half_copy(gi.at[f], p_in.at[f], masks[0], in_rows, in_send.at[f], in_recv.at[f]).wait()
                half_add(gi.at[f], p_in.at[f], masks[0], in_rows)

        for c in range(slabs):
            out_copies[c].wait()
            half_add(go.at[c], p_out.at[c], stages[c % 2][0], out_rows)
    for c in f_copies + d_copies:
        c.wait()


def bwd_kernel(plan, *refs):
    (
        tok, cot, res, meta, rT, f_back, d_back, q, k, v, pw, att, n1, ln1, wqkv, wattn, ln2, wrT, cmT, cvT, cos, sin,
    ) = refs[:22]
    refs = refs[22:]
    if plan:
        stages, order = plan
        p_in, p_out, out, igrad, d_qkv, d_attn, d_small, g_in, g_out = refs[:9]
        refs = refs[9:]
    else:
        out, igrad, d_qkv, d_attn, d_small = refs[:5]
        refs = refs[5:]
    wcat, rb, fk0, fk1, dsn, dcat, n2b, dres, dbr, dproj, datt, dkv, lnacc = refs[:13]
    refs = refs[13:]
    length, width = tok.shape
    experts, capacity, _ = f_back.shape
    slots = experts * capacity
    block = length // 2

    halves = []
    if plan:
        in1, in2, out1, out2, in_send, in_recv, out_send, out_recv, gq, ga = refs[:10]
        gq_recv, ga_recv, g_last, r_last, fin, q_send, q_recv = (
            refs[10:14], refs[14:18], refs[18], refs[19], refs[20], refs[21], refs[22],
        )
        greet(order, 0)
        slabs_in, slabs_out = p_in.shape[0], p_out.shape[0]
        in_rows, out_rows = in1.shape[1], out1.shape[1]

        def in_copy(i, s):
            masks = stages[i * 2 // slabs_in]
            src, dst = ((p_in, in1), (in1, in2))[s]
            return half_copy(
                src.at[i], dst.at[i], masks[s + 1], dst.shape[1], in_send.at[s, i], in_recv.at[s, i]
            )

        def out_copy(i, s):
            masks = stages[i % 2]
            src, dst = ((p_out, out1), (out1, out2))[s]
            return half_copy(
                src.at[i], dst.at[i], masks[s + 1], dst.shape[1], out_send.at[s, i], out_recv.at[s, i]
            )

        ft = p_in.shape[2] // 2
        hidden = g_in.shape[1] // 2

        def in_done(i, s):
            masks = stages[i * 2 // slabs_in]
            in_copy(i, s).wait()
            if s == 0:
                half_add(p_in.at[i], in1.at[i], masks[1], in1.shape[1])
                in_copy(i, 1).start()
            else:
                for part in range(2):
                    cols = slice(part * ft, (part + 1) * ft)
                    to = slice(part * hidden + i * ft, part * hidden + (i + 1) * ft)
                    half_add(in1.at[i, :, cols], in2.at[i, :, cols], masks[2], in2.shape[1], g_in.at[:, to])

        def out_done(i, s):
            masks = stages[i % 2]
            out_copy(i, s).wait()
            if s == 0:
                half_add(p_out.at[i], out1.at[i], masks[1], out1.shape[1])
                out_copy(i, 1).start()
            else:
                wide = out2.shape[2]
                half_add(out1.at[i], out2.at[i], masks[2], out2.shape[1], g_out.at[:, i * wide : (i + 1) * wide])

        for i in range(slabs_in):
            in_copy(i, 0).start()
        for i in range(slabs_out):
            out_copy(i, 0).start()
        for s in range(2):
            for i in range(slabs_in // 2):
                halves.append((in_done, i, s))
                halves.append((in_done, slabs_in // 2 + i, s))
            for i in range(slabs_out):
                halves.append((out_done, i, s))

    def tick(n):
        for _ in range(min(n, len(halves))):
            f, i, s = halves.pop(0)
            f(i, s)

    total = lax.axis_size("dp") * lax.axis_size("expert") if plan else 0

    def slab_store(dst, s, value, cols):
        size = value.shape[0] // total
        low = order[-1]
        bits = [m * (1 if a == "expert" else lax.axis_size("expert")) for a, m in order]
        for j in range(total):
            if (j // bits[-1]) % 2:
                continue
            at = place_of(j, bits[:-1]) * 2 * size
            other = j + bits[-1]
            both = jnp.concatenate(
                [value[j * size : (j + 1) * size], value[other * size : (other + 1) * size]], axis=0
            )
            dst[s, at : at + 2 * size, cols] = both.astype(BF16)

    def slab_copy(src, bufs, s, stage, base):
        if stage < 4:
            return half_copy(
                (src if stage == 0 else bufs[stage - 1]).at[s], bufs[stage].at[s], order[stage],
                bufs[stage].shape[1], q_send.at[base + s, stage], q_recv.at[base + s, stage],
            )
        wide = src.shape[2]
        return half_copy(
            g_last.at[base + s, :, 0:wide], r_last.at[base + s, :, 0:wide], order[4],
            r_last.shape[1], q_send.at[base + s, 4], q_recv.at[base + s, 4],
        )

    def slab_done(src, bufs, s, stage, base):
        slab_copy(src, bufs, s, stage, base).wait()
        if stage < 4:
            before = (src if stage == 0 else bufs[stage - 1]).at[s]
            wide = src.shape[2]
            into = g_last.at[base + s, :, 0:wide] if stage == 3 else None
            half_add(before, bufs[stage].at[s], order[stage], bufs[stage].shape[1], into)
            slab_copy(src, bufs, s, stage + 1, base).start()
        else:
            wide = src.shape[2]
            half_add(
                g_last.at[base + s, :, 0:wide], r_last.at[base + s, :, 0:wide], order[4], r_last.shape[1],
                fin.at[base + s, :, 0:wide],
            )

    wcat[...] = jnp.zeros_like(wcat)
    wcat[0:8] = wrT[...]
    wcat[8:12] = cmT[...]
    for kk in range(2):
        rb[kk] = jnp.transpose(jnp.broadcast_to(rT[kk : kk + 1, :].astype(F32), (128, length)))

    @pl.loop(0, length // 256)
    def _(i):
        rows = tile(i, 256)
        s_id = lax.broadcasted_iota(jnp.int32, (256, slots), 1).astype(F32)
        first = (meta[rows, 0:1] == s_id).astype(F32).astype(BF16)
        second = (meta[rows, 1:2] == s_id).astype(F32).astype(BF16)
        fk0[rows] = dot(first, f_back[...].reshape(slots, width))
        fk1[rows] = dot(second, f_back[...].reshape(slots, width))
        dsn[rows] = dot(first + second, d_back[...].reshape(slots, width))

    w_high = wcat[...].astype(BF16)
    lnacc[...] = jnp.zeros_like(lnacc)

    @pl.loop(0, length // 64)
    def _(i):
        rows = tile(i, 64)
        lane = lax.broadcasted_iota(jnp.int32, (64, 128), 1)
        lane_f = lane.astype(F32)
        m = meta[rows]
        g0, g1, keep = m[:, 2:3], m[:, 3:4], m[:, 4:5]
        cg = (m[:, 5:6], m[:, 6:7])
        shares = ((m[:, 7:8], m[:, 8:9]), (m[:, 9:10], m[:, 10:11]))
        g = cot[rows].astype(F32)
        x = res[rows]
        r2 = lax.rsqrt(row_mean(x * x) + EPS)
        xr = x * r2
        n2 = xr * ln2[...]
        n2b[rows] = n2.astype(BF16)
        f0, f1 = fk0[rows], fk1[rows]
        cv = (cvT[0:1, :], cvT[1:2, :])
        out[rows] = (
            x + g0 * f0 + g1 * f1 + keep * n2 + (cg[0] * shares[0][1]) * cv[0] + (cg[1] * shares[1][1]) * cv[1]
        ).astype(BF16)
        gn2 = jnp.sum(g * n2, axis=-1, keepdims=True)
        gcv = [jnp.sum(g * c, axis=-1, keepdims=True) for c in cv]
        hits = [(rb[kk, rows] == lane_f).astype(F32) for kk in range(2)]
        special = jnp.where(lane == 5, gn2, 0.0)
        for j in range(2):
            special = jnp.where(lane == 6 + j, shares[j][0] * gn2 + shares[j][1] * gcv[j], special)
        dg = [
            jnp.sum(g * f, axis=-1, keepdims=True) + jnp.sum(h * special, axis=-1, keepdims=True)
            for f, h in zip((f0, f1), hits)
        ]
        mean_dg = g0 * dg[0] + g1 * dg[1]
        dc0, dc1 = g0 * (dg[0] - mean_dg), g1 * (dg[1] - mean_dg)
        cat = hits[0] * dc0 + hits[1] * dc1
        for j in range(2):
            dm0, dm1 = cg[j] * gn2, cg[j] * gcv[j]
            mean_dm = shares[j][0] * dm0 + shares[j][1] * dm1
            cat = jnp.where(lane == 8 + 2 * j, shares[j][0] * (dm0 - mean_dm), cat)
            cat = jnp.where(lane == 9 + 2 * j, shares[j][1] * (dm1 - mean_dm), cat)
        dcat[rows, 0:128] = cat.astype(BF16)
        vecs = jnp.where(lane == 12, cg[0] * shares[0][1], 0.0)
        vecs = jnp.where(lane == 13, cg[1] * shares[1][1], vecs)
        dcat[rows, 128:256] = vecs.astype(BF16)
        dn2 = keep * g + dsn[rows] + dot(cat.astype(BF16), w_high)
        lnacc[0:8] += jnp.sum((dn2 * xr).reshape(8, 8, width), axis=0)
        dn = dn2 * ln2[...]
        dr = g + r2 * dn - xr * (r2 * r2) * row_mean(dn * x)
        dres[rows] = dr
        dbr[rows] = dr.astype(BF16)

    tick(6)

    @pl.loop(0, width // 256)
    def _(j):
        cols = tile(j, 256)
        datt[:, cols] = dot_nt(dbr[...], wattn[cols, :]).astype(BF16)

    for j in range(width // 256):
        cols = slice(j * 256, (j + 1) * 256)
        d = dot_tn(att[...], dbr[:, cols])
        if plan:
            slab_store(ga, 0, d, cols)
        else:
            d_attn[:, cols] = d
    tick(4)

    for part in range(3):

        @pl.loop(2 * part, 2 * part + 2)
        def _(j):
            cols = tile(j, 128)
            dkv[...] = jnp.zeros_like(dkv)
            for b in range(2):
                rows = slice(b * block, (b + 1) * block)
                nk = (b + 1) * block
                qlane = lax.broadcasted_iota(jnp.int32, (block, 128), 1)
                klane = lax.broadcasted_iota(jnp.int32, (nk, 128), 1)
                do = datt[rows, cols]
                prod = do.astype(F32) * att[rows, cols].astype(F32)
                dq = jnp.zeros((block, 128), F32)
                for h in range(2):
                    delta = jnp.sum(half_mask(prod, qlane, h), axis=-1, keepdims=True)
                    dom = half_mask(do, qlane, h)
                    dp = dot_nt(dom, v[0:nk, cols])
                    w = pw[2 * j + h, rows, 0:nk]
                    ds = (w.astype(F32) * (dp - delta)).astype(BF16)
                    dq = dq + dot(ds, half_mask(k[0:nk, cols], klane, h))
                    dkv[0, 0:nk] += dot_tn(ds, half_mask(q[rows, cols], qlane, h))
                    dkv[1, 0:nk] += dot_tn(w, dom)
                dproj[rows, cols] = rotate(dq * 0.125, cos[rows], -sin[rows]).astype(BF16)
            dproj[:, pl.ds(pl.multiple_of(width + j * 128, 128), 128)] = rotate(dkv[0], cos[...], -sin[...]).astype(BF16)
            dproj[:, pl.ds(pl.multiple_of(2 * width + j * 128, 128), 128)] = dkv[1].astype(BF16)

        for kind in range(3):
            cols = slice(kind * width + part * 256, kind * width + part * 256 + 256)
            d = dot_tn(n1[...], dproj[:, cols])
            if plan:
                slab_store(gq, part, d, slice(kind * 256, kind * 256 + 256))
            else:
                d_qkv[:, cols] = d
        if plan:
            slab_copy(gq, gq_recv, part, 0, 0).start()
            for stage in range(part):
                slab_done(gq, gq_recv, part - 1 - stage, stage, 0)
        tick(3)

    @pl.loop(0, width // 256)
    def _(j):
        cols = tile(j, 256)
        fk0[:, cols] = dot_nt(dproj[...], wqkv[cols, :])

    @pl.loop(0, length // 64)
    def _(i):
        rows = tile(i, 64)
        x = tok[rows].astype(F32)
        r1 = lax.rsqrt(row_mean(x * x) + EPS)
        xr = x * r1
        d = fk0[rows]
        dn = d * ln1[...]
        lnacc[8:16] += jnp.sum((d * xr).reshape(8, 8, width), axis=0)
        igrad[rows] = (dres[rows] + r1 * dn - xr * (r1 * r1) * row_mean(dn * x)).astype(BF16)

    ln = jnp.zeros((128, width), F32)
    row = lax.broadcasted_iota(jnp.int32, (128, width), 0)
    ln = jnp.where(row == 14, jnp.sum(lnacc[8:16], axis=0, keepdims=True), ln)
    ln = jnp.where(row == 15, jnp.sum(lnacc[0:8], axis=0, keepdims=True), ln)
    small = dot_tn(n2b[...], dcat[:, 0:128]) + dot_tn(cot[...], dcat[:, 128:256]) + jnp.transpose(ln)
    if not plan:
        d_small[...] = small
        return
    slab_store(ga, 0, small, slice(width, width + 128))
    slab_copy(ga, ga_recv, 0, 0, 3).start()
    live = [(gq, gq_recv, 0, 2, 0), (gq, gq_recv, 1, 1, 0), (gq, gq_recv, 2, 0, 0), (ga, ga_recv, 0, 0, 3)]
    while live:
        for src, bufs, s, stage, base in live:
            slab_done(src, bufs, s, stage, base)
        live = [(a, b, s, stage + 1, base) for a, b, s, stage, base in live if stage < 4]
        tick(4)
    tick(100)
    for s in range(3):
        for kind in range(3):
            at = kind * width + s * 256
            d_qkv[:, at : at + 256] = fin[s, :, kind * 256 : kind * 256 + 256]
    d_attn[...] = fin[3, :, 0:width]
    d_small[...] = fin[3, :, width : width + 128]


def shape(*s, dtype=BF16):
    return jax.ShapeDtypeStruct(s, dtype)


def call(kernel, outs, scratch, args, name, collective_id):
    return pl.pallas_call(
        kernel,
        out_shape=outs,
        in_specs=[pl.BlockSpec(memory_space=pltpu.VMEM)] * len(args),
        out_specs=[pl.BlockSpec(memory_space=pltpu.VMEM)] * len(outs),
        scratch_shapes=scratch,
        compiler_params=pltpu.CompilerParams(
            vmem_limit_bytes=VMEM_LIMIT, has_side_effects=True, collective_id=collective_id
        ),
        name=name,
    )(*args)


def body(
    tokens, segments, routes, prev_logits, ln1_gain, w_qkv, w_attn, ln2_gain, w_router, const_mix, const_vec,
    expert_in, expert_out, cotangent,
):
    length, width = tokens.shape
    heads = width // HEAD_DIM
    experts = lax.axis_size("expert") * expert_in.shape[0]
    hidden = expert_out.shape[1]
    capacity = length // 2
    slots = experts * capacity
    n_dp = lax.axis_size("dp")
    V = pltpu.VMEM
    DMA = pltpu.SemaphoreType.DMA
    cos, sin = (jnp.asarray(t) for t in rotary_tables(length))
    rT, pT = routes.T, prev_logits.T
    wrT, cmT, cvT = w_router.T, const_mix.T, const_vec.T
    ln1, ln2 = ln1_gain.reshape(1, width), ln2_gain.reshape(1, width)
    peers = experts - 1

    q, k, v, pw, att, n1, res, meta, send, g_rows = call(
        fwd_kernel,
        [
            shape(length, width), shape(length, width), shape(length, width), shape(heads, length, length),
            shape(length, width), shape(length, width), shape(length, width, dtype=F32),
            shape(length, 128, dtype=F32), shape(experts, capacity, width + 128), shape(experts, capacity, width),
        ],
        [
            V((length, 256), F32), V((length, length), F32), V((128, width), F32), V((3, length, 128), F32),
            V((128, length), F32), V((length, width), BF16), V((length, width), BF16), V((2 * length, 128), BF16),
            V((length, 128), F32), V((slots, length), BF16), V((experts, capacity, width), BF16),
            DMA((peers,)), DMA((peers,)),
        ],
        (tokens, segments, rT, pT, ln1, w_qkv, w_attn, ln2, wrT, cmT, cotangent, cos, sin),
        "attention", 0,
    )

    tiles, slabs = 8, 3
    ft = hidden // tiles
    within = n_dp == tiles and experts == 4
    stages = ((("dp", 1), ("dp", 2), ("dp", 4)), (("dp", 2), ("dp", 1), ("dp", 4))) if within else ()
    order = (("expert", 1), ("expert", 2), ("dp", 1), ("dp", 2), ("dp", 4))
    slab_in, slab_out = (tiles, width, 2 * ft), (slabs, hidden, width // slabs)
    back = [shape(experts, capacity, width)] * 2

    def part_of(s, n):
        return (s[0], s[1] // n, s[2])

    in_half, out_half = part_of(slab_in, 2), part_of(slab_out, 2)
    f_back, d_back, g_in, g_out = call(
        functools.partial(expert_kernel, stages),
        back + ([shape(*in_half), shape(*out_half)] if within else [shape(*slab_in), shape(*slab_out)]),
        [
            V((experts, capacity, width + 128), BF16), V((experts, capacity, width), BF16), V((tiles, slots, ft), BF16),
            V((tiles, slots, ft), BF16), V((tiles, slots, ft), BF16), V((slots, 2 * ft), BF16),
            V((experts, capacity, width), F32), V((2, experts, capacity, width), BF16),
        ]
        + ([V(slab_in, BF16), V(slab_out, BF16)] + [DMA((tiles,))] * 2 + [DMA((slabs,))] * 2 if within else [])
        + [DMA((peers,))] * 6,
        (send, g_rows, expert_in, expert_out),
        "experts", 1,
    )

    args = (
        tokens, cotangent, res, meta, rT, f_back, d_back, q, k, v, pw, att, n1, ln1, w_qkv, w_attn, ln2, wrT, cmT, cvT,
        cos, sin,
    )
    n_all = n_dp * experts
    rows = width // n_all if within else width
    outs = [
        shape(length, width), shape(length, width), shape(rows, 3 * width, dtype=F32), shape(rows, width, dtype=F32),
        shape(rows, 128, dtype=F32),
    ]
    scratch = [
        V((128, width), F32), V((2, length, 128), F32), V((length, width), F32), V((length, width), F32),
        V((length, width), F32), V((length, 256), BF16), V((length, width), BF16), V((length, width), F32),
        V((length, width), BF16), V((length, 3 * width), BF16), V((length, width), BF16),
        V((2, length, 128), F32), V((16, width), F32),
    ]
    if within:
        args += (g_in, g_out)
        outs += [shape(width // n_dp, 2 * hidden, dtype=F32), shape(hidden // n_dp, width, dtype=F32)]
        wide = width + 128
        scratch += [
            V(part_of(slab_in, 4), BF16), V(part_of(slab_in, 8), BF16), V(part_of(slab_out, 4), BF16),
            V(part_of(slab_out, 8), BF16), DMA((2, tiles)), DMA((2, tiles)), DMA((2, slabs)), DMA((2, slabs)),
            V((3, width, width), BF16), V((1, width, wide), BF16),
        ]
        scratch += [V((3, width >> s, width), BF16) for s in range(1, 5)]
        scratch += [V((1, width >> s, wide), BF16) for s in range(1, 5)]
        scratch += [
            V((4, 2 * rows, wide), F32), V((4, rows, wide), F32), V((4, rows, wide), F32), DMA((4, 5)), DMA((4, 5)),
        ]
    plan = (stages, order) if within else ()
    done = call(functools.partial(bwd_kernel, plan), outs, scratch, args, "backward", 2 if within else None)
    out, igrad, d_qkv, d_attn, small = done[:5]
    if within:
        g_in, g_out = done[5:]
    else:
        g_in = jnp.moveaxis(g_in.reshape(tiles, width, 2, ft), 0, 2).reshape(width, 2 * hidden)
        g_out = jnp.moveaxis(g_out, 0, 1).reshape(hidden, width)
        g_in = lax.psum_scatter(g_in, "dp", scatter_dimension=0, tiled=True).astype(F32)
        g_out = lax.psum_scatter(g_out, "dp", scatter_dimension=0, tiled=True).astype(F32)
        d_qkv, d_attn, small = (
            lax.psum_scatter(d, ("dp", "expert"), scatter_dimension=0, tiled=True) for d in (d_qkv, d_attn, small)
        )
    return (
        out, igrad, small[:, 14], d_qkv, d_attn, small[:, 15], small[:, 0:8], small[:, 8:12], small[:, 12:14],
        g_in[None], g_out[None],
    )


def solution(mesh):
    rows = P(("dp", "expert"), None)
    return jax.shard_map(
        body,
        mesh=mesh,
        in_specs=(
            rows, rows, rows, rows, P(), P(), P(), P(), P(), P(), P(),
            P("expert", None, None), P("expert", None, None), rows,
        ),
        out_specs=(
            rows, rows, P(("dp", "expert")), rows, rows, P(("dp", "expert")), rows, rows, rows,
            P("expert", "dp", None), P("expert", "dp", None),
        ),
        check_vma=False,
    )
```

time: 667 us -> 283 us (0.42)
  waiting for transfers between devices: 421 us -> 0 us
  Pallas kernels: 132 us -> 267 us
  blocking collectives: 85.2 us -> 0 us
  between operations: 15.7 us -> 0.69 us
  local copies, waits for them, and re-layouts: 8.24 us -> 15.2 us
    reduce_scatter x4 -> x0, waiting for transfers between devices: 256 us -> none  [the longest x1 124 us: body(): d_qkv = lax.psum_scatter(d_qkv, both, scatter_dimension=0, tiled=True)]
    unnamed x6 -> x0, waiting for transfers between devices: 166 us -> none
    pallas_call x3, Pallas kernels: 132 us -> 267 us  [call(): pl.pallas_call(kernel, out_shape=outs, in_specs=[pl.BlockSpec(memory_spac...]
    all_to_all x2 -> x0, blocking collectives: 85.2 us -> none  [the longest x1 42.9 us: body(): lax.all_to_all(send, 'expert', split_axis=0, concat_axis=0, tiled=True)]
    unnamed x3 -> x19, local copies, waits for them, and re-layouts: 1.95 us -> 9.62 us
  transfers between devices with their start and end apart: 5 -> 0, of which waited for: 4 -> 0; matrix products, arithmetic and copies ran while one was open for 2% -> 0% of each run, Pallas kernels for 0% -> 0%
where the time goes in v2:
time: 283 us
  Pallas kernels  267 us (94%)
  local copies, waits for them, and re-layouts  15.2 us (5%)
    pallas_call x3, Pallas kernels, call(): pl.pallas_call(kernel, out_shape=outs, in_specs=[pl.BlockSpec(memory_spac...  267 us
    unnamed x19, local copies, waits for them, and re-layouts  9.62 us

profile of v2, /device:TPU:0, one launch (start us, length us, event | category | flops | bytes accessed | tf_op | source)
XLA Modules:
  0.0 282.9 jit_solution(6395017048853559984)
XLA Ops:
  0.6 1.3 reshape.28.ln1.refs_13_
  1.9 1.3 reshape.29.ln2.refs_16_
  3.2 36.8 %attention.1 = (bf16[512,768]{1,0:T(8,128)(2,1)}, bf16[512,768]{1,0:T(8,128)(2,1)}, bf16[512,768]{1,0:T(8,128)(2,1)}, bf16[12,512,512]{2,1,0:T(8,128)(2,1)}, bf1...) custom-call(bf16[512,768]{1,0:T(8,128)(2,1)} %refs_0_.1, ...), custom_call_target="tpu_custom_call" | custom-call | tf_op jit(solution)/shard_map/attention/pallas_call | solution.py:750
  40.0 122.9 %experts.1 = (bf16[4,256,768]{2,1,0:T(8,128)(2,1)}, bf16[4,256,768]{2,1,0:T(8,128)(2,1)}, bf16[8,384,512]{2,1,0:T(8,128)(2,1)}, bf16[3,1024,256]{2,1,0:T(8,128)(2,1)}) custom-call(bf16[4,256,896]{2,1,0:T(8,128)(2,1)} %get-tuple-element.34.xs, bf16[4,256,768]{2,1,0:T(8,128)(2,1)} %get-tuple-element.35.g_rows, bf16[1,768,4096]{2,1,0:T(8,128)(2,1)} %win.1, ...), custom_call_target="tpu_custom_call" | custom-call | tf_op jit(solution)/shard_map/experts/pallas_call | solution.py:750
  162.9 107.3 %backward.1 = (bf16[512,768]{1,0:T(8,128)(2,1)}, bf16[512,768]{1,0:T(8,128)(2,1)}, f32[24,2304]{1,0:T(8,128)}, f32[24,768]{1,0:T(8,128)}, f32[24,128]{1,0:T(8,12...) custom-call(bf16[512,768]{1,0:T(8,128)(2,1)} %refs_0_.1, bf16[512,768]{1,0:T(8,128)(2,1)} %refs_1_.1, ...), custom_call_target="tpu_custom_call" | custom-call | tf_op jit(solution)/shard_map/backward/pallas_call | solution.py:750
  270.2 0.0 copy-start.2
  270.2 1.5 slice_reduce_fusion
  271.7 1.4 copy.30
  273.1 0.8 slice.18
  273.9 0.7 copy.31
  274.5 0.8 slice.19
  275.3 0.6 copy.32
  275.9 0.0 copy-start.3
  275.9 0.0 copy-start.4
  275.9 0.0 copy-start
  275.9 2.2 copy.39
  278.1 0.0 copy-done.2
  278.1 0.9 copy.40
  279.0 0.0 copy-done.3
  279.0 0.7 copy.41
  279.7 0.0 copy-done.4
  279.7 0.6 copy.42
  280.3 0.0 copy-done
  280.3 0.0 copy-start.1
  280.3 1.1 copy.43
  281.5 0.5 copy-done.1
  282.0 0.9 copy.44
Async XLA Ops:
  270.2 7.9 %copy-start.2 = (bf16[512,768]{1,0:T(8,128)(2,1)S(1)}, bf16[512,768]{1,0:T(8,128)(2,1)}, u32[]{:S(2)}) copy-start(bf16[512,768]{1,0:T(8,128)(2,1)} %get-tuple-element.89) | copy-start | bytes 2359300
  275.9 3.1 %copy-start.3 = (f32[24,2304]{1,0:T(8,128)S(1)}, f32[24,2304]{1,0:T(8,128)}, u32[]{:S(2)}) copy-start(f32[24,2304]{1,0:T(8,128)} %get-tuple-element.91) | copy-start | bytes 663556
  275.9 3.8 %copy-start.4 = (f32[24,768]{1,0:T(8,128)S(1)}, f32[24,768]{1,0:T(8,128)}, u32[]{:S(2)}) copy-start(f32[24,768]{1,0:T(8,128)} %get-tuple-element.92) | copy-start | bytes 221188
  275.9 4.4 %copy-start = (f32[96,4096]{1,0:T(8,128)S(1)}, f32[96,4096]{1,0:T(8,128)}, u32[]{:S(2)}) copy-start(f32[96,4096]{1,0:T(8,128)} %get-tuple-element.51) | copy-start | bytes 4718596
  280.3 1.7 copy-start.1

commit v3 on v2

--- a/solution.py
+++ b/solution.py
@@ -81,30 +81,31 @@
     return {axis: flip(lax.axis_index(axis), m)}
 
 
-def greet(masks, shifts=0):
+def across(r):
+    e = lax.axis_index("expert")
+    for m in (1, 2):
+        if r & m:
+            e = flip(e, m)
+    return e
+
+
+def greet(masks, peers=0):
     barrier = pltpu.get_barrier_semaphore()
     for mask in masks:
         pl.semaphore_signal(barrier, inc=1, device_id=partner(mask), device_id_type=MESH)
-    n = lax.axis_size("expert")
-    for o in range(1, shifts + 1):
-        dest = lax.rem(lax.axis_index("expert") + o, n)
-        pl.semaphore_signal(barrier, inc=1, device_id={"expert": dest}, device_id_type=MESH)
-    pl.semaphore_wait(barrier, len(masks) + shifts)
+    for r in range(1, peers + 1):
+        pl.semaphore_signal(barrier, inc=1, device_id={"expert": across(r)}, device_id_type=MESH)
+    pl.semaphore_wait(barrier, len(masks) + peers)
 
 
 def exchange(src, dst, send_sem, recv_sem):
-    n = lax.axis_size("expert")
-    me = lax.axis_index("expert")
-    copies = []
-    for o in range(1, n):
-        dest = lax.rem(me + o, n)
-        copies.append(
-            pltpu.make_async_remote_copy(
-                src.at[dest], dst.at[me], send_sem.at[o - 1], recv_sem.at[o - 1],
-                device_id={"expert": dest}, device_id_type=MESH,
-            )
+    return {
+        r: pltpu.make_async_remote_copy(
+            src.at[r], dst.at[r], send_sem.at[r - 1], recv_sem.at[r - 1],
+            device_id={"expert": across(r)}, device_id_type=MESH,
         )
-    return copies
+        for r in range(src.shape[0] - 1, 0, -1)
+    }
 
 
 def half_copy(src, dst, mask, rows, send_sem, recv_sem):
@@ -165,18 +166,17 @@
     target = jnp.transpose(tg[...])
     pb[...] = target
 
-    @pl.loop(0, experts)
-    def _(e):
-        s_id = (lax.broadcasted_iota(jnp.int32, (capacity, length), 0) + e * capacity).astype(F32)
+    copies = exchange(g_out, g_rows, send_sem, recv_sem)
+    for r in range(experts - 1, -1, -1):
+        s_id = (lax.broadcasted_iota(jnp.int32, (capacity, length), 0) + across(r) * capacity).astype(F32)
         here = (pb[0:1] == s_id).astype(F32) + (pb[1:2] == s_id).astype(F32)
-        onehot[tile(e, capacity)] = here.astype(BF16)
-        g_out[e] = dot(here.astype(BF16), cot[...]).astype(BF16)
-
-    copies = exchange(g_out, g_rows, send_sem, recv_sem)
-    for c in copies:
-        c.start()
-    me = lax.axis_index("expert")
-    g_rows[me] = g_out[me]
+        onehot[r * capacity : (r + 1) * capacity] = here.astype(BF16)
+        rows_r = dot(here.astype(BF16), cot[...]).astype(BF16)
+        if r:
+            g_out[r] = rows_r
+            copies[r].start()
+        else:
+            g_rows[0] = rows_r
 
     @pl.loop(0, length // 64)
     def _(i):
@@ -295,7 +295,10 @@
 
     @pl.loop(0, experts)
     def _(e):
-        s_id = (lax.broadcasted_iota(jnp.int32, (capacity, length), 0) + e * capacity).astype(F32)
+        owner = flip(lax.axis_index("expert"), 1)
+        owner = jnp.where(e % 2 == 1, owner, lax.axis_index("expert"))
+        owner = jnp.where(e // 2 == 1, flip(owner, 2), owner)
+        s_id = (lax.broadcasted_iota(jnp.int32, (capacity, length), 0) + owner * capacity).astype(F32)
         gate = jnp.zeros((capacity, 128), F32)
         for kk in range(2):
             here = (pb[kk : kk + 1] == s_id).astype(F32).astype(BF16)
@@ -303,156 +306,148 @@
         send[e, :, 0:width] = dot(onehot[tile(e, capacity)], n2b[...]).astype(BF16)
         send[e, :, width : width + 128] = gate.astype(BF16)
 
-    for c in copies:
+    for c in copies.values():
         c.wait()
 
 
 def expert_kernel(stages, xs, g_rows, win, wout, *refs):
+    f_rows, d_back, go = refs[:3]
     if stages:
-        f_back, d_back, p_in, p_out = refs[:4]
-        refs = refs[4:]
+        p_in = refs[3]
     else:
-        f_back, d_back, gi, go = refs[:4]
-        refs = refs[4:]
-    xr, dy, hid, fa, fb, dgu, acc, stage = refs[:8]
-    refs = refs[8:]
+        gi = refs[3]
+    xr, dy, hid, dgu, f_acc, d_acc, d_out = refs[4:11]
+    refs = refs[11:]
     if stages:
-        gi, go, in_send, in_recv, out_send, out_recv = refs[:6]
-        refs = refs[6:]
-    x_send, x_recv, f_send, f_recv, d_send, d_recv = refs
+        gi, in_send, in_recv = refs[:3]
+        refs = refs[3:]
+    x_send, x_recv, d_send, d_recv = refs
     groups, capacity, wide = xs.shape
     hidden, width = wout.shape[1:]
-    tiles, _, ft = hid.shape
+    tiles, rows_all, ft = hid.shape
     slabs = go.shape[0]
-    me = lax.axis_index("expert")
-
-    greet([s[0] for s in stages[:2]], groups - 1)
+    shards = 2 ** len(stages[0]) if stages else 0
+    near = rows_all // 2
+
+    greet([s[0] for s in stages], groups - 1)
     copies = exchange(xs, xr, x_send, x_recv)
-    for c in copies:
+    for c in copies.values():
         c.start()
-    xr[me] = xs[me]
-    for c in copies:
-        c.wait()
-    for s in range(groups):
-        pair = xr[s, :, width:wide].astype(F32)
+    xr[0] = xs[0]
+
+    def gated(r):
+        pair = xr[r, :, width:wide].astype(F32)
         lane = lax.broadcasted_iota(jnp.int32, pair.shape, 1)
         gate = jnp.sum(jnp.where(lane < 2, pair, 0.0), axis=-1, keepdims=True)
-        dy[s] = (g_rows[s].astype(F32) * gate).astype(BF16)
+        dy[r * capacity : (r + 1) * capacity] = (g_rows[r].astype(F32) * gate).astype(BF16)
+
+    def cols_of(f):
+        return tile(f, ft), pl.ds(pl.multiple_of(hidden + f * ft, ft), ft)
+
+    def work(f, part):
+        gate_cols, up_cols = cols_of(f)
+        rows = slice(part * near, (part + 1) * near)
+        x = xr[2 * part : 2 * part + 2, :, 0:width].reshape(near, width)
+        gate = dot(x, win[0, :, gate_cols])
+        up = dot(x, win[0, :, up_cols])
+        dh = dot_nt(dy[rows], wout[0, gate_cols, :])
+        sig = 1.0 / (1.0 + jnp.exp(-gate))
+        silu = gate * sig
+        h = (silu * up).astype(BF16)
+        da = (dh * up * (sig + silu * (1.0 - sig))).astype(BF16)
+        db = (dh * silu).astype(BF16)
+        hid[f, rows] = h
+        dgu[f, rows, 0:ft] = da
+        dgu[f, rows, ft : 2 * ft] = db
+        y = dot(h, wout[0, gate_cols, :])
+        d = dot_nt(da, win[0, :, gate_cols]) + dot_nt(db, win[0, :, up_cols])
+
+        @pl.when(f == 0)
+        def _():
+            f_acc[rows] = y
+            d_acc[rows] = d
+
+        @pl.when(f > 0)
+        def _():
+            f_acc[rows] += y
+            d_acc[rows] += d
+
+    def in_copy(slab, p):
+        return half_copy(
+            gi.at[slab], p_in.at[slab], stages[p][0], width // 2, in_send.at[slab], in_recv.at[slab]
+        )
+
+    copies[1].wait()
+    gated(0)
+    gated(1)
 
     @pl.loop(0, tiles)
     def _(f):
-        gate_cols = tile(f, ft)
-        up_cols = pl.ds(pl.multiple_of(hidden + f * ft, ft), ft)
-
-        @pl.loop(0, groups)
-        def _(s):
-            rows = tile(s, capacity)
-            gate = dot(xr[s, :, 0:width], win[0, :, gate_cols])
-            up = dot(xr[s, :, 0:width], win[0, :, up_cols])
-            sig = 1.0 / (1.0 + jnp.exp(-gate))
-            silu = gate * sig
-            h = (silu * up).astype(BF16)
-            hid[f, rows] = h
-            fa[f, rows] = (up * sig * (1.0 + gate * (1.0 - sig))).astype(BF16)
-            fb[f, rows] = silu.astype(BF16)
-            y = dot(h, wout[0, gate_cols, :])
-
-            @pl.when(f == 0)
-            def _():
-                acc[s] = y
-
-            @pl.when(f > 0)
-            def _():
-                acc[s] += y
-
-    stage[0] = acc[...].astype(BF16)
-    f_copies = exchange(stage.at[0], f_back, f_send, f_recv)
-    for c in f_copies:
-        c.start()
-    f_back[me] = stage[0, me]
-
-    shards = 2 ** len(stages[0]) if stages else 0
-    in_rows, out_rows = width // 2, hidden // 2
-    half = tiles // 2
-    for part in range(2):
-        masks = stages[part] if stages else ()
-
-        @pl.loop(part * half, (part + 1) * half)
-        def _(f):
-            gate_cols = tile(f, ft)
-            up_cols = pl.ds(pl.multiple_of(hidden + f * ft, ft), ft)
-
-            @pl.loop(0, groups)
-            def _(s):
-                rows = tile(s, capacity)
-                dh = dot_nt(dy[s], wout[0, gate_cols, :])
-                da = (dh * fa[f, rows].astype(F32)).astype(BF16)
-                db = (dh * fb[f, rows].astype(F32)).astype(BF16)
-                dgu[rows, 0:ft] = da
-                dgu[rows, ft : 2 * ft] = db
-                d = dot_nt(da, win[0, :, gate_cols]) + dot_nt(db, win[0, :, up_cols])
-
-                @pl.when(f == 0)
-                def _():
-                    acc[s] = d
-
-                @pl.when(f > 0)
-                def _():
-                    acc[s] += d
-
-            for p in range(2):
-                cols = slice(p * ft, (p + 1) * ft)
-                d = dot_tn(xr[:, :, 0:width].reshape(groups * capacity, width), dgu[:, cols])
-                if not stages:
-                    gi[f, :, cols] = d.astype(BF16)
-                    continue
-                size = width // shards
-                for j in range(shards):
-                    at = place_of(j, [m for _, m in masks]) * size
-                    gi[f, at : at + size, cols] = d[j * size : (j + 1) * size].astype(BF16)
-            if stages:
-                half_copy(gi.at[f], p_in.at[f], masks[0], in_rows, in_send.at[f], in_recv.at[f]).start()
-
-    stage[1] = acc[...].astype(BF16)
-    d_copies = exchange(stage.at[1], d_back, d_send, d_recv)
-    for c in d_copies:
-        c.start()
-    d_back[me] = stage[1, me]
-
-    out_copies = []
-    size = hidden // tiles
+        work(f, 0)
+
+    copies[3].wait()
+    copies[2].wait()
+    gated(2)
+    gated(3)
+
+    @pl.loop(0, tiles)
+    def _(f):
+        work(f, 1)
+        for p in range(2):
+            d = dot_tn(xr[:, :, 0:width].reshape(rows_all, width), dgu[f, :, p * ft : (p + 1) * ft])
+            if not stages:
+                gi[2 * f + p] = d.astype(BF16)
+                continue
+            size = width // shards
+            for j in range(shards):
+                at = place_of(j, [m for _, m in stages[p]]) * size
+                gi[2 * f + p, at : at + size] = d[j * size : (j + 1) * size].astype(BF16)
+            in_copy(2 * f + p, p).start()
+
+    d_copies = exchange(d_out, d_back, d_send, d_recv)
+    for r in range(groups - 1, -1, -1):
+        rows = slice(r * capacity, (r + 1) * capacity)
+        y = f_acc[rows]
+        f_rows[r] = y.astype(BF16)
+        dots = jnp.sum(y * g_rows[r].astype(F32), axis=-1, keepdims=True)
+        high = dots.astype(BF16).astype(F32)
+        lane = lax.broadcasted_iota(jnp.int32, (capacity, 128), 1)
+        extra = jnp.where(lane == 0, high, jnp.where(lane == 1, dots - high, 0.0)).astype(BF16)
+        dst = d_out if r else d_back
+        dst[r, :, 0:width] = d_acc[rows].astype(BF16)
+        dst[r, :, width:wide] = extra
+        if r:
+            d_copies[r].start()
+
     for c in range(slabs):
         cols = slice(c * (width // slabs), (c + 1) * (width // slabs))
-        masks = stages[c % 2] if stages else ()
 
         @pl.loop(0, tiles)
         def _(t):
-            at = place_of(t, [m for _, m in masks]) if stages else t
-            go[c, tile(at, size)] = dot_tn(hid[t], dy[:, :, cols].reshape(groups * capacity, width // slabs)).astype(BF16)
-
-        if stages:
-            out_copies.append(half_copy(go.at[c], p_out.at[c], masks[0], out_rows, out_send.at[c], out_recv.at[c]))
-            out_copies[-1].start()
+            d = dot_tn(hid[t], dy[:, cols]).astype(BF16)
+            if not stages:
+                go[c, tile(t, ft)] = d
+                return
+            size = hidden // shards
+            for i in range(ft // size):
+                at = place_of(t * (ft // size) + i, [m for _, m in stages[0]])
+                go[c, tile(at, size)] = d[i * size : (i + 1) * size]
 
     if stages:
-        for part in range(2):
-            masks = stages[part]
-
-            @pl.loop(part * half, (part + 1) * half)
-            def _(f):
-                half_copy(gi.at[f], p_in.at[f], masks[0], in_rows, in_send.at[f], in_recv.at[f]).wait()
-                half_add(gi.at[f], p_in.at[f], masks[0], in_rows)
-
-        for c in range(slabs):
-            out_copies[c].wait()
-            half_add(go.at[c], p_out.at[c], stages[c % 2][0], out_rows)
-    for c in f_copies + d_copies:
+
+        @pl.loop(0, tiles)
+        def _(f):
+            for p in range(2):
+                in_copy(2 * f + p, p).wait()
+                half_add(gi.at[2 * f + p], p_in.at[2 * f + p], stages[p][0], width // 2)
+
+    for c in d_copies.values():
         c.wait()
 
 
 def bwd_kernel(plan, *refs):
     (
-        tok, cot, res, meta, rT, f_back, d_back, q, k, v, pw, att, n1, ln1, wqkv, wattn, ln2, wrT, cmT, cvT, cos, sin,
+        tok, cot, res, meta, rT, f_rows, d_back, q, k, v, pw, att, n1, ln1, wqkv, wattn, ln2, wrT, cmT, cvT, cos, sin,
     ) = refs[:22]
     refs = refs[22:]
     if plan:
@@ -462,77 +457,84 @@
     else:
         out, igrad, d_qkv, d_attn, d_small = refs[:5]
         refs = refs[5:]
-    wcat, rb, fk0, fk1, dsn, dcat, n2b, dres, dbr, dproj, datt, dkv, lnacc = refs[:13]
-    refs = refs[13:]
+    wcat, rb, fk0, dsn, dots, dcat, n2b, dres, dbr, dproj, datt, dkv, lnacc, f_back, f_send, f_recv = refs[:16]
+    refs = refs[16:]
     length, width = tok.shape
-    experts, capacity, _ = f_back.shape
+    experts, capacity, _ = f_rows.shape
     slots = experts * capacity
     block = length // 2
 
-    halves = []
+    greet(order[2:] if plan else (), experts - 1)
+    f_copies = exchange(f_rows, f_back, f_send, f_recv)
+
+    events = []
     if plan:
-        in1, in2, out1, out2, in_send, in_recv, out_send, out_recv, gq, ga = refs[:10]
+        in1, in2, out0, out1, out2, in_send, in_recv, out_send, out_recv, gq, ga = refs[:11]
         gq_recv, ga_recv, g_last, r_last, fin, q_send, q_recv = (
-            refs[10:14], refs[14:18], refs[18], refs[19], refs[20], refs[21], refs[22],
+            refs[11:15], refs[15:19], refs[19], refs[20], refs[21], refs[22], refs[23],
         )
-        greet(order, 0)
         slabs_in, slabs_out = p_in.shape[0], p_out.shape[0]
-        in_rows, out_rows = in1.shape[1], out1.shape[1]
+        ft = p_in.shape[2]
+        hidden = g_in.shape[1] // 2
 
         def in_copy(i, s):
-            masks = stages[i * 2 // slabs_in]
             src, dst = ((p_in, in1), (in1, in2))[s]
             return half_copy(
-                src.at[i], dst.at[i], masks[s + 1], dst.shape[1], in_send.at[s, i], in_recv.at[s, i]
+                src.at[i], dst.at[i], stages[i % 2][s + 1], dst.shape[1], in_send.at[s, i], in_recv.at[s, i]
             )
 
         def out_copy(i, s):
+            src, dst = ((p_out, out0), (out0, out1), (out1, out2))[s]
+            return half_copy(
+                src.at[i], dst.at[i], stages[0][s], dst.shape[1], out_send.at[s, i], out_recv.at[s, i]
+            )
+
+        def in_done(i, s):
             masks = stages[i % 2]
-            src, dst = ((p_out, out1), (out1, out2))[s]
-            return half_copy(
-                src.at[i], dst.at[i], masks[s + 1], dst.shape[1], out_send.at[s, i], out_recv.at[s, i]
-            )
-
-        ft = p_in.shape[2] // 2
-        hidden = g_in.shape[1] // 2
-
-        def in_done(i, s):
-            masks = stages[i * 2 // slabs_in]
             in_copy(i, s).wait()
             if s == 0:
                 half_add(p_in.at[i], in1.at[i], masks[1], in1.shape[1])
                 in_copy(i, 1).start()
             else:
-                for part in range(2):
-                    cols = slice(part * ft, (part + 1) * ft)
-                    to = slice(part * hidden + i * ft, part * hidden + (i + 1) * ft)
-                    half_add(in1.at[i, :, cols], in2.at[i, :, cols], masks[2], in2.shape[1], g_in.at[:, to])
+                to = (i % 2) * hidden + (i // 2) * ft
+                half_add(in1.at[i], in2.at[i], masks[2], in2.shape[1], g_in.at[:, to : to + ft])
 
         def out_done(i, s):
-            masks = stages[i % 2]
             out_copy(i, s).wait()
-            if s == 0:
-                half_add(p_out.at[i], out1.at[i], masks[1], out1.shape[1])
-                out_copy(i, 1).start()
+            src, dst = ((p_out, out0), (out0, out1), (out1, out2))[s]
+            if s < 2:
+                half_add(src.at[i], dst.at[i], stages[0][s], dst.shape[1])
+                out_copy(i, s + 1).start()
             else:
                 wide = out2.shape[2]
-                half_add(out1.at[i], out2.at[i], masks[2], out2.shape[1], g_out.at[:, i * wide : (i + 1) * wide])
-
-        for i in range(slabs_in):
+                half_add(out1.at[i], out2.at[i], stages[0][2], out2.shape[1], g_out.at[:, i * wide : (i + 1) * wide])
+
+        out_copy(0, 0).start()
+        for i in range(0, slabs_in, 2):
             in_copy(i, 0).start()
-        for i in range(slabs_out):
-            out_copy(i, 0).start()
-        for s in range(2):
-            for i in range(slabs_in // 2):
-                halves.append((in_done, i, s))
-                halves.append((in_done, slabs_in // 2 + i, s))
-            for i in range(slabs_out):
-                halves.append((out_done, i, s))
+
+        def odd_start():
+            for i in range(1, slabs_in, 2):
+                in_copy(i, 0).start()
+
+        def last_start():
+            out_copy(1, 0).start()
+
+        events = [
+            (in_done, 0, 0), (in_done, 2, 0), (odd_start,),
+            (in_done, 4, 0), (in_done, 6, 0), (out_done, 0, 0),
+            (last_start,), (in_done, 1, 0), (in_done, 3, 0), (in_done, 0, 1),
+            (in_done, 5, 0), (in_done, 7, 0), (in_done, 2, 1), (out_done, 0, 1),
+            (in_done, 4, 1), (in_done, 6, 1), (out_done, 1, 0), (in_done, 1, 1), (in_done, 3, 1),
+            (in_done, 5, 1), (in_done, 7, 1), (out_done, 0, 2), (out_done, 1, 1), (out_done, 1, 2),
+        ]
+    for c in f_copies.values():
+        c.start()
 
     def tick(n):
-        for _ in range(min(n, len(halves))):
-            f, i, s = halves.pop(0)
-            f(i, s)
+        for _ in range(min(n, len(events))):
+            f, *a = events.pop(0)
+            f(*a)
 
     total = lax.axis_size("dp") * lax.axis_size("expert") if plan else 0
 
@@ -577,21 +579,29 @@
                 fin.at[base + s, :, 0:wide],
             )
 
+    f_back[0] = f_rows[0]
     wcat[...] = jnp.zeros_like(wcat)
     wcat[0:8] = wrT[...]
     wcat[8:12] = cmT[...]
     for kk in range(2):
         rb[kk] = jnp.transpose(jnp.broadcast_to(rT[kk : kk + 1, :].astype(F32), (128, length)))
 
+    def chosen(rows, wide):
+        slot = lax.broadcasted_iota(jnp.int32, (wide, slots), 1)
+        r = slot // capacity
+        e = jnp.zeros_like(slot)
+        for n in range(experts):
+            e = jnp.where(r == n, across(n), e)
+        s_id = (slot - r * capacity + e * capacity).astype(F32)
+        return meta[rows, 0:1] == s_id, meta[rows, 1:2] == s_id
+
     @pl.loop(0, length // 256)
     def _(i):
         rows = tile(i, 256)
-        s_id = lax.broadcasted_iota(jnp.int32, (256, slots), 1).astype(F32)
-        first = (meta[rows, 0:1] == s_id).astype(F32).astype(BF16)
-        second = (meta[rows, 1:2] == s_id).astype(F32).astype(BF16)
-        fk0[rows] = dot(first, f_back[...].reshape(slots, width))
-        fk1[rows] = dot(second, f_back[...].reshape(slots, width))
-        dsn[rows] = dot(first + second, d_back[...].reshape(slots, width))
+        first, second = (c.astype(F32).astype(BF16) for c in chosen(rows, 256))
+        dsn[rows] = dot(first + second, d_back[:, :, 0:width].reshape(slots, width))
+        for n, c in enumerate((first, second)):
+            dots[n, rows] = dot(c, d_back[:, :, width : width + 128].reshape(slots, 128))
 
     w_high = wcat[...].astype(BF16)
     lnacc[...] = jnp.zeros_like(lnacc)
@@ -611,11 +621,8 @@
         xr = x * r2
         n2 = xr * ln2[...]
         n2b[rows] = n2.astype(BF16)
-        f0, f1 = fk0[rows], fk1[rows]
         cv = (cvT[0:1, :], cvT[1:2, :])
-        out[rows] = (
-            x + g0 * f0 + g1 * f1 + keep * n2 + (cg[0] * shares[0][1]) * cv[0] + (cg[1] * shares[1][1]) * cv[1]
-        ).astype(BF16)
+        fk0[rows] = x + keep * n2 + (cg[0] * shares[0][1]) * cv[0] + (cg[1] * shares[1][1]) * cv[1]
         gn2 = jnp.sum(g * n2, axis=-1, keepdims=True)
         gcv = [jnp.sum(g * c, axis=-1, keepdims=True) for c in cv]
         hits = [(rb[kk, rows] == lane_f).astype(F32) for kk in range(2)]
@@ -623,8 +630,8 @@
         for j in range(2):
             special = jnp.where(lane == 6 + j, shares[j][0] * gn2 + shares[j][1] * gcv[j], special)
         dg = [
-            jnp.sum(g * f, axis=-1, keepdims=True) + jnp.sum(h * special, axis=-1, keepdims=True)
-            for f, h in zip((f0, f1), hits)
+            jnp.sum(h * special + jnp.where(lane < 2, dots[n, rows], 0.0), axis=-1, keepdims=True)
+            for n, h in enumerate(hits)
         ]
         mean_dg = g0 * dg[0] + g1 * dg[1]
         dc0, dc1 = g0 * (dg[0] - mean_dg), g1 * (dg[1] - mean_dg)
@@ -645,7 +652,7 @@
         dres[rows] = dr
         dbr[rows] = dr.astype(BF16)
 
-    tick(6)
+    tick(3)
 
     @pl.loop(0, width // 256)
     def _(j):
@@ -659,7 +666,7 @@
             slab_store(ga, 0, d, cols)
         else:
             d_attn[:, cols] = d
-    tick(4)
+    tick(3)
 
     for part in range(3):
 
@@ -699,7 +706,19 @@
             slab_copy(gq, gq_recv, part, 0, 0).start()
             for stage in range(part):
                 slab_done(gq, gq_recv, part - 1 - stage, stage, 0)
-        tick(3)
+        tick(4)
+
+    for c in f_copies.values():
+        c.wait()
+
+    @pl.loop(0, length // 256)
+    def _(i):
+        rows = tile(i, 256)
+        first, second = chosen(rows, 256)
+        mix = jnp.where(first, meta[rows, 2:3], jnp.where(second, meta[rows, 3:4], 0.0)).astype(BF16)
+        out[rows] = (fk0[rows] + dot(mix, f_back[...].reshape(slots, width))).astype(BF16)
+
+    tick(2)
 
     @pl.loop(0, width // 256)
     def _(j):
@@ -796,34 +815,36 @@
         "attention", 0,
     )
 
-    tiles, slabs = 8, 3
+    tiles, slabs = 4, 2
     ft = hidden // tiles
-    within = n_dp == tiles and experts == 4
+    within = n_dp == 8 and experts == 4
     stages = ((("dp", 1), ("dp", 2), ("dp", 4)), (("dp", 2), ("dp", 1), ("dp", 4))) if within else ()
     order = (("expert", 1), ("expert", 2), ("dp", 1), ("dp", 2), ("dp", 4))
-    slab_in, slab_out = (tiles, width, 2 * ft), (slabs, hidden, width // slabs)
-    back = [shape(experts, capacity, width)] * 2
+    slab_in, slab_out = (2 * tiles, width, ft), (slabs, hidden, width // slabs)
 
     def part_of(s, n):
         return (s[0], s[1] // n, s[2])
 
-    in_half, out_half = part_of(slab_in, 2), part_of(slab_out, 2)
-    f_back, d_back, g_in, g_out = call(
+    wide = width + 128
+    f_rows, d_back, g_out, g_in = call(
         functools.partial(expert_kernel, stages),
-        back + ([shape(*in_half), shape(*out_half)] if within else [shape(*slab_in), shape(*slab_out)]),
         [
-            V((experts, capacity, width + 128), BF16), V((experts, capacity, width), BF16), V((tiles, slots, ft), BF16),
-            V((tiles, slots, ft), BF16), V((tiles, slots, ft), BF16), V((slots, 2 * ft), BF16),
-            V((experts, capacity, width), F32), V((2, experts, capacity, width), BF16),
+            shape(experts, capacity, width), shape(experts, capacity, wide), shape(*slab_out),
+            shape(*part_of(slab_in, 2 if within else 1)),
+        ],
+        [
+            V((experts, capacity, wide), BF16), V((slots, width), BF16), V((tiles, slots, ft), BF16),
+            V((tiles, slots, 2 * ft), BF16), V((slots, width), F32), V((slots, width), F32),
+            V((experts, capacity, wide), BF16),
         ]
-        + ([V(slab_in, BF16), V(slab_out, BF16)] + [DMA((tiles,))] * 2 + [DMA((slabs,))] * 2 if within else [])
-        + [DMA((peers,))] * 6,
+        + ([V(slab_in, BF16)] + [DMA((2 * tiles,))] * 2 if within else [])
+        + [DMA((peers,))] * 4,
         (send, g_rows, expert_in, expert_out),
         "experts", 1,
     )
 
     args = (
-        tokens, cotangent, res, meta, rT, f_back, d_back, q, k, v, pw, att, n1, ln1, w_qkv, w_attn, ln2, wrT, cmT, cvT,
+        tokens, cotangent, res, meta, rT, f_rows, d_back, q, k, v, pw, att, n1, ln1, w_qkv, w_attn, ln2, wrT, cmT, cvT,
         cos, sin,
     )
     n_all = n_dp * experts
@@ -834,17 +855,17 @@
     ]
     scratch = [
         V((128, width), F32), V((2, length, 128), F32), V((length, width), F32), V((length, width), F32),
-        V((length, width), F32), V((length, 256), BF16), V((length, width), BF16), V((length, width), F32),
+        V((2, length, 128), F32), V((length, 256), BF16), V((length, width), BF16), V((length, width), F32),
         V((length, width), BF16), V((length, 3 * width), BF16), V((length, width), BF16),
-        V((2, length, 128), F32), V((16, width), F32),
+        V((2, length, 128), F32), V((16, width), F32), V((experts, capacity, width), BF16), DMA((peers,)), DMA((peers,)),
     ]
     if within:
         args += (g_in, g_out)
         outs += [shape(width // n_dp, 2 * hidden, dtype=F32), shape(hidden // n_dp, width, dtype=F32)]
-        wide = width + 128
         scratch += [
-            V(part_of(slab_in, 4), BF16), V(part_of(slab_in, 8), BF16), V(part_of(slab_out, 4), BF16),
-            V(part_of(slab_out, 8), BF16), DMA((2, tiles)), DMA((2, tiles)), DMA((2, slabs)), DMA((2, slabs)),
+            V(part_of(slab_in, 4), BF16), V(part_of(slab_in, 8), BF16), V(part_of(slab_out, 2), BF16),
+            V(part_of(slab_out, 4), BF16), V(part_of(slab_out, 8), BF16), DMA((2, 2 * tiles)), DMA((2, 2 * tiles)),
+            DMA((3, slabs)), DMA((3, slabs)),
             V((3, width, width), BF16), V((1, width, wide), BF16),
         ]
         scratch += [V((3, width >> s, width), BF16) for s in range(1, 5)]
@@ -853,12 +874,12 @@
             V((4, 2 * rows, wide), F32), V((4, rows, wide), F32), V((4, rows, wide), F32), DMA((4, 5)), DMA((4, 5)),
         ]
     plan = (stages, order) if within else ()
-    done = call(functools.partial(bwd_kernel, plan), outs, scratch, args, "backward", 2 if within else None)
+    done = call(functools.partial(bwd_kernel, plan), outs, scratch, args, "backward", 2)
     out, igrad, d_qkv, d_attn, small = done[:5]
     if within:
         g_in, g_out = done[5:]
     else:
-        g_in = jnp.moveaxis(g_in.reshape(tiles, width, 2, ft), 0, 2).reshape(width, 2 * hidden)
+        g_in = jnp.moveaxis(g_in.reshape(tiles, 2, width, ft), 2, 0).transpose(0, 2, 1, 3).reshape(width, 2 * hidden)
         g_out = jnp.moveaxis(g_out, 0, 1).reshape(hidden, width)
         g_in = lax.psum_scatter(g_in, "dp", scatter_dimension=0, tiled=True).astype(F32)
         g_out = lax.psum_scatter(g_out, "dp", scatter_dimension=0, tiled=True).astype(F32)

time: 283 us -> 237 us (0.84)
  Pallas kernels: 267 us -> 221 us
    pallas_call x3, Pallas kernels: 267 us -> 221 us  [call(): pl.pallas_call(kernel, out_shape=outs, in_specs=[pl.BlockSpec(memory_spac...]
where the time goes in v3:
time: 237 us
  Pallas kernels  221 us (93%)
  local copies, waits for them, and re-layouts  14.7 us (6%)
    pallas_call x3, Pallas kernels, call(): pl.pallas_call(kernel, out_shape=outs, in_specs=[pl.BlockSpec(memory_spac...  221 us
    unnamed x19, local copies, waits for them, and re-layouts  9.08 us

profile of v3, /device:TPU:0, one launch (start us, length us, event | category | flops | bytes accessed | tf_op | source)
XLA Modules:
  0.0 236.9 jit_solution(14768339526120083718)
XLA Ops:
  0.6 1.3 reshape.28.ln1.refs_13_
  1.9 1.3 reshape.29.ln2.refs_16_
  3.2 36.7 %attention.1 = (bf16[512,768]{1,0:T(8,128)(2,1)}, bf16[512,768]{1,0:T(8,128)(2,1)}, bf16[512,768]{1,0:T(8,128)(2,1)}, bf16[12,512,512]{2,1,0:T(8,128)(2,1)}, bf1...) custom-call(bf16[512,768]{1,0:T(8,128)(2,1)} %refs_0_.1, ...), custom_call_target="tpu_custom_call" | custom-call | tf_op jit(solution)/shard_map/attention/pallas_call | solution.py:769
  39.9 72.9 %experts.1 = (bf16[4,256,768]{2,1,0:T(8,128)(2,1)}, bf16[4,256,896]{2,1,0:T(8,128)(2,1)}, bf16[2,2048,384]{2,1,0:T(8,128)(2,1)}, bf16[8,384,512]{2,1,0:T(8,128)(2,1)}) custom-call(bf16[4,256,896]{2,1,0:T(8,128)(2,1)} %get-tuple-element.34.xs, bf16[4,256,768]{2,1,0:T(8,128)(2,1)} %get-tuple-element.35.g_rows, bf16[1,768,4096]{2,1,0:T(8,128)(2,1)} %win.1, ...), custom_call_target="tpu_custom_call" | custom-call | tf_op jit(solution)/shard_map/experts/pallas_call | solution.py:769
  112.7 111.9 %backward.1 = (bf16[512,768]{1,0:T(8,128)(2,1)}, bf16[512,768]{1,0:T(8,128)(2,1)}, f32[24,2304]{1,0:T(8,128)}, f32[24,768]{1,0:T(8,128)}, f32[24,128]{1,0:T(8,12...) custom-call(bf16[512,768]{1,0:T(8,128)(2,1)} %refs_0_.1, bf16[512,768]{1,0:T(8,128)(2,1)} %refs_1_.1, ...), custom_call_target="tpu_custom_call" | custom-call | tf_op jit(solution)/shard_map/backward/pallas_call | solution.py:769
  224.7 0.0 copy-start.2
  224.7 0.0 copy-start.3
  224.7 1.5 slice_reduce_fusion
  226.2 1.4 copy.30
  227.6 0.0 copy-start.4
  227.6 0.8 slice.18
  228.4 0.7 copy.31
  229.0 0.8 slice.19
  229.8 0.6 copy.32
  230.4 0.0 copy-start
  230.4 2.2 copy.39
  232.6 0.0 copy-done.2
  232.6 0.9 copy.40
  233.5 0.0 copy-done.3
  233.5 0.0 copy-start.1
  233.5 0.7 copy.41
  234.2 0.0 copy-done.4
  234.2 0.6 copy.42
  234.8 0.0 copy-done
  234.8 1.1 copy.43
  236.0 0.0 copy-done.1
  236.0 0.9 copy.44
Async XLA Ops:
  224.7 8.0 %copy-start.2 = (bf16[512,768]{1,0:T(8,128)(2,1)S(1)}, bf16[512,768]{1,0:T(8,128)(2,1)}, u32[]{:S(2)}) copy-start(bf16[512,768]{1,0:T(8,128)(2,1)} %get-tuple-element.89) | copy-start | bytes 2359300
  224.7 8.8 %copy-start.3 = (f32[24,2304]{1,0:T(8,128)S(1)}, f32[24,2304]{1,0:T(8,128)}, u32[]{:S(2)}) copy-start(f32[24,2304]{1,0:T(8,128)} %get-tuple-element.91) | copy-start | bytes 663556
  227.6 6.6 %copy-start.4 = (f32[24,768]{1,0:T(8,128)S(1)}, f32[24,768]{1,0:T(8,128)}, u32[]{:S(2)}) copy-start(f32[24,768]{1,0:T(8,128)} %get-tuple-element.92) | copy-start | bytes 221188
  230.4 4.4 %copy-start = (f32[96,4096]{1,0:T(8,128)S(1)}, f32[96,4096]{1,0:T(8,128)}, u32[]{:S(2)}) copy-start(f32[96,4096]{1,0:T(8,128)} %get-tuple-element.51) | copy-start | bytes 4718596
  233.5 2.5 %copy-start.1 = (f32[256,768]{1,0:T(8,128)S(1)}, f32[256,768]{1,0:T(8,128)}, u32[]{:S(2)}) copy-start(f32[256,768]{1,0:T(8,128)} %get-tuple-element.52) | copy-start | bytes 2359300

commit v4 on v3

--- a/solution.py
+++ b/solution.py
@@ -136,13 +136,16 @@
 
 def fwd_kernel(
     tok, seg, rT, pT, ln1, wqkv, wattn, ln2, wrT, cmT, cot, cos, sin,
-    q, k, v, pw, att, n1, res, meta, send, g_rows,
-    proj, bias, wcat, rb, pb, n2b, n2l, gl, tg, onehot, g_out, send_sem, recv_sem,
+    q_out, k_out, v_out, pw_out, att_out, n1_out, res_out, meta, send_out, g_rows,
+    proj, bias, wcat, rb, pb, n2b, n2l, gl, tg, onehot, g_out, send_sem, recv_sem, pw, send, pw_sem, row_sem,
 ):
-    length, width = tok.shape
+    length, width = tok.near.shape
     capacity = length // 2
     experts = send.shape[0]
 
+    for ref in (cot, tok, wqkv, cos, sin, wattn):
+        ref.start()
+    q, k, v, att, n1, res = (ref.near for ref in (q_out, k_out, v_out, att_out, n1_out, res_out))
     greet((), experts - 1)
     for kk in range(2):
         rb[kk] = jnp.transpose(jnp.broadcast_to(rT[kk : kk + 1, :].astype(F32), (128, length)))
@@ -166,17 +169,16 @@
     target = jnp.transpose(tg[...])
     pb[...] = target
 
+    cot = cot.wait()
     copies = exchange(g_out, g_rows, send_sem, recv_sem)
+    own_rows = pltpu.make_async_copy(g_out.at[0], g_rows.at[0], row_sem.at[experts])
     for r in range(experts - 1, -1, -1):
         s_id = (lax.broadcasted_iota(jnp.int32, (capacity, length), 0) + across(r) * capacity).astype(F32)
         here = (pb[0:1] == s_id).astype(F32) + (pb[1:2] == s_id).astype(F32)
         onehot[r * capacity : (r + 1) * capacity] = here.astype(BF16)
-        rows_r = dot(here.astype(BF16), cot[...]).astype(BF16)
-        if r:
-            g_out[r] = rows_r
-            copies[r].start()
-        else:
-            g_rows[0] = rows_r
+        g_out[r] = dot(here.astype(BF16), cot[...]).astype(BF16)
+        (copies[r] if r else own_rows).start()
+    tok = tok.wait()
 
     @pl.loop(0, length // 64)
     def _(i):
@@ -185,7 +187,9 @@
         r = lax.rsqrt(row_mean(x * x) + EPS)
         n1[rows] = (x * r * ln1[...]).astype(BF16)
 
-    for kind, dst in enumerate((q, k, v)):
+    n1_out.start()
+    wqkv, cos, sin = wqkv.wait(), cos.wait(), sin.wait()
+    for kind, (dst, done) in enumerate(((q, q_out), (k, k_out), (v, v_out))):
 
         @pl.loop(0, width // 256)
         def _(j):
@@ -203,6 +207,8 @@
                         x = x * 0.125
                     dst[rows, pl.ds(pl.multiple_of(j * 256 + part * 128, 128), 128)] = x.astype(BF16)
 
+        done.start()
+
     seg_f = seg[...].astype(F32)
     rb[2] = jnp.transpose(jnp.broadcast_to(seg_f, (128, length)))
 
@@ -215,6 +221,10 @@
         bias[rows] = jnp.where(same & (row_id >= col_id), 0.0, MASKED)
 
     block = length // 2
+
+    def weights_copy(j, b):
+        at = (pl.ds(2 * j, 2), slice(b * block, (b + 1) * block), slice(0, (b + 1) * block))
+        return pltpu.make_async_copy(pw.at[at], pw_out.at[at], pw_sem.at[j, b])
 
     @pl.loop(0, width // 128)
     def _(j):
@@ -233,11 +243,17 @@
                 pw[2 * j + h, rows, 0:nk] = w
                 acc = acc + dot(w, half_mask(v[0:nk, cols], klane, h))
             att[rows, cols] = acc.astype(BF16)
+            weights_copy(j, b).start()
+
+    att_out.start()
+    wattn = wattn.wait()
 
     @pl.loop(0, width // 256)
     def _(j):
         cols = tile(j, 256)
         res[:, cols] = tok[:, cols].astype(F32) + dot(att[...], wattn[:, cols])
+
+    res_out.start()
 
     @pl.loop(0, length // 64)
     def _(i):
@@ -305,25 +321,44 @@
             gate = gate + dot(here, gl[kk * length : (kk + 1) * length])
         send[e, :, 0:width] = dot(onehot[tile(e, capacity)], n2b[...]).astype(BF16)
         send[e, :, width : width + 128] = gate.astype(BF16)
-
+        pltpu.make_async_copy(send.at[e], send_out.at[e], row_sem.at[e]).start()
+
+    for ref in (q_out, k_out, v_out, att_out, n1_out, res_out):
+        ref.wait()
+
+    @pl.loop(0, width // 128)
+    def _(j):
+        for b in range(2):
+            weights_copy(j, b).wait()
+
+    @pl.loop(0, experts)
+    def _(e):
+        pltpu.make_async_copy(send.at[e], send_out.at[e], row_sem.at[e]).wait()
+
+    own_rows.wait()
     for c in copies.values():
         c.wait()
 
 
 def expert_kernel(stages, xs, g_rows, win, wout, *refs):
-    f_rows, d_back, go = refs[:3]
+    f_out, d_back, go_out = refs[:3]
+    f_rows, go = f_out.near, go_out.near
     if stages:
-        p_in = refs[3]
+        late_out, early_out = refs[3:5]
+        p_late, p_early = late_out.near, early_out.near
+        refs = refs[5:]
     else:
-        gi = refs[3]
-    xr, dy, hid, dgu, f_acc, d_acc, d_out = refs[4:11]
-    refs = refs[11:]
+        gi_out = refs[3]
+        gi = gi_out.near
+        refs = refs[4:]
+    xr, dy, hid, dgu, f_acc, d_acc, d_out = refs[:7]
+    refs = refs[7:]
     if stages:
-        gi, in_send, in_recv = refs[:3]
-        refs = refs[3:]
-    x_send, x_recv, d_send, d_recv = refs
+        gi, p_first, in_send, in_recv, e_send, e_recv = refs[:6]
+        refs = refs[6:]
+    x_send, x_recv, d_send, d_recv, own_sem = refs
     groups, capacity, wide = xs.shape
-    hidden, width = wout.shape[1:]
+    hidden, width = wout.near.shape[1:]
     tiles, rows_all, ft = hid.shape
     slabs = go.shape[0]
     shards = 2 ** len(stages[0]) if stages else 0
@@ -333,7 +368,10 @@
     copies = exchange(xs, xr, x_send, x_recv)
     for c in copies.values():
         c.start()
-    xr[0] = xs[0]
+    own_x = pltpu.make_async_copy(xs.at[0], xr.at[0], own_sem.at[0])
+    own_x.start()
+    for ref in (g_rows, win, wout):
+        ref.start()
 
     def gated(r):
         pair = xr[r, :, width:wide].astype(F32)
@@ -372,14 +410,23 @@
             f_acc[rows] += y
             d_acc[rows] += d
 
-    def in_copy(slab, p):
+    def in_copy(part, f, p):
+        dst = (p_first if part == 0 else p_late).at[2 * (f - part * tiles // 2) + p]
+        slab = 2 * f + p
+        return half_copy(gi.at[slab], dst, stages[p][0], width // 2, in_send.at[slab], in_recv.at[slab]), dst
+
+    def early_copy(slab):
         return half_copy(
-            gi.at[slab], p_in.at[slab], stages[p][0], width // 2, in_send.at[slab], in_recv.at[slab]
+            p_first.at[slab], p_early.at[slab], stages[slab % 2][1], width // 4, e_send.at[slab], e_recv.at[slab]
         )
 
+    own_x.wait()
+    g_rows = g_rows.wait()
     copies[1].wait()
     gated(0)
     gated(1)
+
+    win, wout = win.wait(), wout.wait()
 
     @pl.loop(0, tiles)
     def _(f):
@@ -390,21 +437,24 @@
     gated(2)
     gated(3)
 
-    @pl.loop(0, tiles)
-    def _(f):
-        work(f, 1)
-        for p in range(2):
-            d = dot_tn(xr[:, :, 0:width].reshape(rows_all, width), dgu[f, :, p * ft : (p + 1) * ft])
-            if not stages:
-                gi[2 * f + p] = d.astype(BF16)
-                continue
-            size = width // shards
-            for j in range(shards):
-                at = place_of(j, [m for _, m in stages[p]]) * size
-                gi[2 * f + p, at : at + size] = d[j * size : (j + 1) * size].astype(BF16)
-            in_copy(2 * f + p, p).start()
+    for part in range(2):
+
+        @pl.loop(part * (tiles // 2), (part + 1) * (tiles // 2))
+        def _(f):
+            work(f, 1)
+            for p in range(2):
+                d = dot_tn(xr[:, :, 0:width].reshape(rows_all, width), dgu[f, :, p * ft : (p + 1) * ft])
+                if not stages:
+                    gi[2 * f + p] = d.astype(BF16)
+                    continue
+                size = width // shards
+                for j in range(shards):
+                    at = place_of(j, [m for _, m in stages[p]]) * size
+                    gi[2 * f + p, at : at + size] = d[j * size : (j + 1) * size].astype(BF16)
+                in_copy(part, f, p)[0].start()
 
     d_copies = exchange(d_out, d_back, d_send, d_recv)
+    own_d = pltpu.make_async_copy(d_out.at[0], d_back.at[0], own_sem.at[1])
     for r in range(groups - 1, -1, -1):
         rows = slice(r * capacity, (r + 1) * capacity)
         y = f_acc[rows]
@@ -413,11 +463,10 @@
         high = dots.astype(BF16).astype(F32)
         lane = lax.broadcasted_iota(jnp.int32, (capacity, 128), 1)
         extra = jnp.where(lane == 0, high, jnp.where(lane == 1, dots - high, 0.0)).astype(BF16)
-        dst = d_out if r else d_back
-        dst[r, :, 0:width] = d_acc[rows].astype(BF16)
-        dst[r, :, width:wide] = extra
-        if r:
-            d_copies[r].start()
+        d_out[r, :, 0:width] = d_acc[rows].astype(BF16)
+        d_out[r, :, width:wide] = extra
+        (d_copies[r] if r else own_d).start()
+    f_out.start()
 
     for c in range(slabs):
         cols = slice(c * (width // slabs), (c + 1) * (width // slabs))
@@ -433,153 +482,219 @@
                 at = place_of(t * (ft // size) + i, [m for _, m in stages[0]])
                 go[c, tile(at, size)] = d[i * size : (i + 1) * size]
 
+    go_out.start()
     if stages:
-
-        @pl.loop(0, tiles)
-        def _(f):
-            for p in range(2):
-                in_copy(2 * f + p, p).wait()
-                half_add(gi.at[2 * f + p], p_in.at[2 * f + p], stages[p][0], width // 2)
-
+        for part in range(2):
+            for f in range(part * (tiles // 2), (part + 1) * (tiles // 2)):
+                for p in range(2):
+                    copy, dst = in_copy(part, f, p)
+                    copy.wait()
+                    half_add(gi.at[2 * f + p], dst, stages[p][0], width // 2)
+                    if part == 0:
+                        early_copy(2 * f + p).start()
+        late_out.start()
+        for slab in range(tiles):
+            early_copy(slab).wait()
+            half_add(p_first.at[slab], p_early.at[slab], stages[slab % 2][1], width // 4)
+        early_out.start()
+        late_out.wait()
+        early_out.wait()
+    else:
+        gi_out.start()
+        gi_out.wait()
+    f_out.wait()
+    go_out.wait()
+    own_d.wait()
     for c in d_copies.values():
         c.wait()
 
 
+def out_start(copy, i):
+    copy(i, 0).start()
+
+
+def as_columns(x):
+    row = jnp.sum(x, axis=0, keepdims=True)
+    return jnp.transpose(jnp.broadcast_to(row, (128, row.shape[1])))
+
+
+class Slab:
+    def __init__(self, order, refs):
+        self.order = order
+        self.bufs, (self.pair, self.got, self.send, self.recv) = refs[:5], refs[5:]
+        self.bits = [m * (1 if a == "expert" else lax.axis_size("expert")) for a, m in order]
+        self.out = ()
+
+    def store(self, value, at):
+        total = 2 ** len(self.order)
+        size, cols = value.shape[0] // total, slice(at, at + value.shape[1])
+        for j in range(total):
+            other = j + self.bits[-1]
+            if (j // self.bits[-1]) % 2:
+                continue
+            row = place_of(j, self.bits[:-1]) * 2 * size
+            both = jnp.concatenate([value[j * size : (j + 1) * size], value[other * size : (other + 1) * size]], axis=0)
+            self.bufs[0][row : row + 2 * size, cols] = both.astype(BF16)
+
+    def copy(self, s):
+        src, dst = (self.bufs[s], self.bufs[s + 1]) if s < 4 else (self.pair, self.got)
+        return half_copy(src, dst, self.order[s], dst.shape[0], self.send.at[s], self.recv.at[s])
+
+    def start(self):
+        self.copy(0).start()
+
+    def done(self, s):
+        self.copy(s).wait()
+        if s < 4:
+            into = self.pair if s == 3 else None
+            half_add(self.bufs[s], self.bufs[s + 1], self.order[s], self.bufs[s + 1].shape[0], into)
+            self.copy(s + 1).start()
+            return
+        rows = self.got.shape[0]
+        mine = self.pair[pl.ds(pl.multiple_of(side(self.order[4]) * rows, 8), rows)]
+        total = mine + self.got[...]
+        for ref, at, col, n in self.out:
+            ref[:, at : at + n] = total[:, col : col + n]
+
+
 def bwd_kernel(plan, *refs):
     (
-        tok, cot, res, meta, rT, f_rows, d_back, q, k, v, pw, att, n1, ln1, wqkv, wattn, ln2, wrT, cmT, cvT, cos, sin,
+        tok, cot, res, meta, rT, f_rows, d_back, q, k, v, pw_far, att, n1, ln1, wqkv, wattn, ln2, wrT, cmT, cvT, cos, sin,
     ) = refs[:22]
     refs = refs[22:]
     if plan:
         stages, order = plan
-        p_in, p_out, out, igrad, d_qkv, d_attn, d_small, g_in, g_out = refs[:9]
-        refs = refs[9:]
+        p_early, p_late, p_out, out_s, igrad_s, d_qkv, d_attn, d_small, d_ln, g_in_s, g_out_s = refs[:11]
+        g_in, g_out = g_in_s.near, g_out_s.near
+        refs = refs[11:]
     else:
-        out, igrad, d_qkv, d_attn, d_small = refs[:5]
+        out_s, igrad_s, d_qkv, d_attn, d_small = refs[:5]
         refs = refs[5:]
-    wcat, rb, fk0, dsn, dots, dcat, n2b, dres, dbr, dproj, datt, dkv, lnacc, f_back, f_send, f_recv = refs[:16]
-    refs = refs[16:]
-    length, width = tok.shape
+    out, igrad = out_s.near, igrad_s.near
+    wcat, rb, fk0, dsn, dots, dcat, n2b, dres, dbr, dproj, datt, dkv, lnacc, f_back, f_send, f_recv, pw, own_sem = refs[:18]
+    refs = refs[18:]
+    length, width = tok.near.shape
     experts, capacity, _ = f_rows.shape
     slots = experts * capacity
     block = length // 2
 
+    weights = []
+    for b in range(2):
+        at = (slice(0, pw.shape[0]), slice(b * block, (b + 1) * block), slice(0, (b + 1) * block))
+        weights.append(pltpu.make_async_copy(pw_far.at[at], pw.at[at], own_sem.at[b]))
+    own_f = pltpu.make_async_copy(f_rows.at[0], f_back.at[0], own_sem.at[2])
+    for ref in (d_back, cot, res):
+        ref.start()
     greet(order[2:] if plan else (), experts - 1)
     f_copies = exchange(f_rows, f_back, f_send, f_recv)
 
-    events = []
+    acts = {}
     if plan:
-        in1, in2, out0, out1, out2, in_send, in_recv, out_send, out_recv, gq, ga = refs[:11]
-        gq_recv, ga_recv, g_last, r_last, fin, q_send, q_recv = (
-            refs[11:15], refs[15:19], refs[19], refs[20], refs[21], refs[22], refs[23],
-        )
-        slabs_in, slabs_out = p_in.shape[0], p_out.shape[0]
-        ft = p_in.shape[2]
+        in1, in2, out0, out1, out2, in_send, in_recv, out_send, out_recv = refs[:9]
+        slab_refs = [refs[9 + 9 * n : 18 + 9 * n] for n in range(6)]
+        late = p_late.near.shape[0]
+        slabs_in = late + p_early.near.shape[0]
+        ft = p_late.near.shape[2]
         hidden = g_in.shape[1] // 2
 
+        def in_refs(i, s, far=False):
+            n = i - (slabs_in - late)
+            p = "far" if far else "near"
+            first = getattr(p_early, p).at[i] if n < 0 else in1.at[n]
+            return (getattr(p_late, p).at[n], first) if s == 0 else (first, in2.at[i])
+
         def in_copy(i, s):
-            src, dst = ((p_in, in1), (in1, in2))[s]
-            return half_copy(
-                src.at[i], dst.at[i], stages[i % 2][s + 1], dst.shape[1], in_send.at[s, i], in_recv.at[s, i]
-            )
+            src, dst = in_refs(i, s, True)
+            return half_copy(src, dst, stages[i % 2][s + 1], dst.shape[0], in_send.at[s, i], in_recv.at[s, i])
+
+        def in_done(i, s):
+            in_copy(i, s).wait()
+            src, dst = in_refs(i, s)
+            if s == 0:
+                half_add(src, dst, stages[i % 2][1], dst.shape[0])
+                in_copy(i, 1).start()
+            else:
+                to = (i % 2) * hidden + (i // 2) * ft
+                half_add(src, dst, stages[i % 2][2], dst.shape[0], g_in.at[:, to : to + ft])
+
+        def out_refs(i, s, far=False):
+            return ((p_out.far if far else p_out.near, out0), (out0, out1), (out1, out2))[s]
 
         def out_copy(i, s):
-            src, dst = ((p_out, out0), (out0, out1), (out1, out2))[s]
+            src, dst = out_refs(i, s, True)
             return half_copy(
                 src.at[i], dst.at[i], stages[0][s], dst.shape[1], out_send.at[s, i], out_recv.at[s, i]
             )
 
-        def in_done(i, s):
-            masks = stages[i % 2]
-            in_copy(i, s).wait()
-            if s == 0:
-                half_add(p_in.at[i], in1.at[i], masks[1], in1.shape[1])
-                in_copy(i, 1).start()
-            else:
-                to = (i % 2) * hidden + (i // 2) * ft
-                half_add(in1.at[i], in2.at[i], masks[2], in2.shape[1], g_in.at[:, to : to + ft])
-
         def out_done(i, s):
             out_copy(i, s).wait()
-            src, dst = ((p_out, out0), (out0, out1), (out1, out2))[s]
+            src, dst = out_refs(i, s)
+            wide = out2.shape[2]
+            into = g_out.at[:, i * wide : (i + 1) * wide] if s == 2 else None
+            half_add(src.at[i], dst.at[i], stages[0][s], dst.shape[1], into)
             if s < 2:
-                half_add(src.at[i], dst.at[i], stages[0][s], dst.shape[1])
                 out_copy(i, s + 1).start()
-            else:
-                wide = out2.shape[2]
-                half_add(out1.at[i], out2.at[i], stages[0][2], out2.shape[1], g_out.at[:, i * wide : (i + 1) * wide])
+
+        swapped = (order[0], order[2], order[1], order[3], order[4])
+        slabs = [Slab(o, r) for o, r in zip((order, order, order, order, swapped, order), slab_refs)]
+        attn_slab, q0, q1, q2a, q2b, ln_slab = slabs
+
+        def q_out(first, pairs):
+            n = 128 * pairs
+            return [(d_qkv, kind * width + first * 128, kind * n, n) for kind in range(3)]
+
+        attn_slab.out = [(d_attn, 0, 0, width), (d_small, 0, width, 128)]
+        q0.out, q1.out, q2a.out, q2b.out = q_out(0, 2), q_out(2, 2), q_out(4, 1), q_out(5, 1)
+        ln_slab.out = [(d_ln, 0, 0, 128)]
 
         out_copy(0, 0).start()
-        for i in range(0, slabs_in, 2):
+        for i in range(slabs_in - late):
+            in_copy(i, 1).start()
+        for i in range(slabs_in - late, slabs_in, 2):
             in_copy(i, 0).start()
-
-        def odd_start():
-            for i in range(1, slabs_in, 2):
-                in_copy(i, 0).start()
-
-        def last_start():
-            out_copy(1, 0).start()
-
-        events = [
-            (in_done, 0, 0), (in_done, 2, 0), (odd_start,),
-            (in_done, 4, 0), (in_done, 6, 0), (out_done, 0, 0),
-            (last_start,), (in_done, 1, 0), (in_done, 3, 0), (in_done, 0, 1),
-            (in_done, 5, 0), (in_done, 7, 0), (in_done, 2, 1), (out_done, 0, 1),
-            (in_done, 4, 1), (in_done, 6, 1), (out_done, 1, 0), (in_done, 1, 1), (in_done, 3, 1),
-            (in_done, 5, 1), (in_done, 7, 1), (out_done, 0, 2), (out_done, 1, 1), (out_done, 1, 2),
-        ]
+        a, b = slabs_in - late, slabs_in
+        acts = {
+            "token": [(in_done, i, 0) for i in range(a, b, 2)]
+            + [(in_done, i, 1) for i in range(a)]
+            + [(out_start, out_copy, 1)],
+            "attn": [(attn_slab.start,), (out_done, 0, 0)],
+            "part0": [(q0.start,), (attn_slab.done, 0)],
+            "part1": [(q1.start,), (q0.done, 0), (attn_slab.done, 1), (out_done, 0, 1)]
+            + [(out_start, in_copy, i) for i in range(a + 1, b, 2)]
+            + [(in_done, i, 1) for i in range(a, b, 2)],
+            "part2": [
+                (q2a.start,), (q2b.start,), (q1.done, 0), (q0.done, 1), (attn_slab.done, 2), (out_done, 1, 0),
+            ],
+            "norm": [(q2a.done, 0), (q2b.done, 0), (q1.done, 1), (q0.done, 2), (attn_slab.done, 3)]
+            + [(in_done, i, 0) for i in range(a + 1, b, 2)]
+            + [(out_done, 0, 2)],
+            "input": [
+                (ln_slab.start,), (q2a.done, 1), (q2b.done, 1), (q1.done, 2), (q0.done, 3), (attn_slab.done, 4),
+                (out_done, 1, 1), (ln_slab.done, 0),
+            ],
+            "output": [
+                (q2a.done, 2), (q2b.done, 2), (ln_slab.done, 1), (q1.done, 3), (q0.done, 4), (ln_slab.done, 2),
+                (q2a.done, 3), (q2b.done, 3), (q1.done, 4), (ln_slab.done, 3), (q2a.done, 4), (q2b.done, 4),
+            ]
+            + [(in_done, i, 1) for i in range(a + 1, b, 2)]
+            + [(ln_slab.done, 4), (out_done, 1, 2)],
+        }
     for c in f_copies.values():
         c.start()
-
-    def tick(n):
-        for _ in range(min(n, len(events))):
-            f, *a = events.pop(0)
+    late_refs = (wattn, att, q, k, v, cos, sin, n1, wqkv, tok)
+    for ref in ((p_early, p_late, p_out) if plan else ()) + late_refs[:5]:
+        ref.start()
+    for c in weights:
+        c.start()
+    own_f.start()
+    for ref in late_refs[5:]:
+        ref.start()
+    d_back = d_back.wait()
+
+    def act(name):
+        for f, *a in acts.get(name, ()):
             f(*a)
 
-    total = lax.axis_size("dp") * lax.axis_size("expert") if plan else 0
-
-    def slab_store(dst, s, value, cols):
-        size = value.shape[0] // total
-        low = order[-1]
-        bits = [m * (1 if a == "expert" else lax.axis_size("expert")) for a, m in order]
-        for j in range(total):
-            if (j // bits[-1]) % 2:
-                continue
-            at = place_of(j, bits[:-1]) * 2 * size
-            other = j + bits[-1]
-            both = jnp.concatenate(
-                [value[j * size : (j + 1) * size], value[other * size : (other + 1) * size]], axis=0
-            )
-            dst[s, at : at + 2 * size, cols] = both.astype(BF16)
-
-    def slab_copy(src, bufs, s, stage, base):
-        if stage < 4:
-            return half_copy(
-                (src if stage == 0 else bufs[stage - 1]).at[s], bufs[stage].at[s], order[stage],
-                bufs[stage].shape[1], q_send.at[base + s, stage], q_recv.at[base + s, stage],
-            )
-        wide = src.shape[2]
-        return half_copy(
-            g_last.at[base + s, :, 0:wide], r_last.at[base + s, :, 0:wide], order[4],
-            r_last.shape[1], q_send.at[base + s, 4], q_recv.at[base + s, 4],
-        )
-
-    def slab_done(src, bufs, s, stage, base):
-        slab_copy(src, bufs, s, stage, base).wait()
-        if stage < 4:
-            before = (src if stage == 0 else bufs[stage - 1]).at[s]
-            wide = src.shape[2]
-            into = g_last.at[base + s, :, 0:wide] if stage == 3 else None
-            half_add(before, bufs[stage].at[s], order[stage], bufs[stage].shape[1], into)
-            slab_copy(src, bufs, s, stage + 1, base).start()
-        else:
-            wide = src.shape[2]
-            half_add(
-                g_last.at[base + s, :, 0:wide], r_last.at[base + s, :, 0:wide], order[4], r_last.shape[1],
-                fin.at[base + s, :, 0:wide],
-            )
-
-    f_back[0] = f_rows[0]
     wcat[...] = jnp.zeros_like(wcat)
     wcat[0:8] = wrT[...]
     wcat[8:12] = cmT[...]
@@ -603,6 +718,7 @@
         for n, c in enumerate((first, second)):
             dots[n, rows] = dot(c, d_back[:, :, width : width + 128].reshape(slots, 128))
 
+    cot, res = cot.wait(), res.wait()
     w_high = wcat[...].astype(BF16)
     lnacc[...] = jnp.zeros_like(lnacc)
 
@@ -652,7 +768,19 @@
         dres[rows] = dr
         dbr[rows] = dr.astype(BF16)
 
-    tick(3)
+    if plan:
+        for ref in (p_early, p_late, p_out):
+            ref.wait()
+    act("token")
+    wattn, att = wattn.wait(), att.wait()
+    small = dot_tn(n2b[...], dcat[:, 0:128]) + dot_tn(cot[...], dcat[:, 128:256])
+    small = small + jnp.where(
+        lax.broadcasted_iota(jnp.int32, small.shape, 1) == 15, as_columns(lnacc[0:8]), 0.0
+    )
+    if plan:
+        attn_slab.store(small, width)
+    else:
+        d_small[...] = small
 
     @pl.loop(0, width // 256)
     def _(j):
@@ -663,10 +791,13 @@
         cols = slice(j * 256, (j + 1) * 256)
         d = dot_tn(att[...], dbr[:, cols])
         if plan:
-            slab_store(ga, 0, d, cols)
+            attn_slab.store(d, j * 256)
         else:
             d_attn[:, cols] = d
-    tick(3)
+    act("attn")
+    q, k, v, cos, sin, n1 = (ref.wait() for ref in (q, k, v, cos, sin, n1))
+    for c in weights:
+        c.wait()
 
     for part in range(3):
 
@@ -698,16 +829,47 @@
         for kind in range(3):
             cols = slice(kind * width + part * 256, kind * width + part * 256 + 256)
             d = dot_tn(n1[...], dproj[:, cols])
-            if plan:
-                slab_store(gq, part, d, slice(kind * 256, kind * 256 + 256))
+            if not plan:
+                d_qkv[:, cols] = d
+            elif part < 2:
+                (q0, q1)[part].store(d, kind * 256)
             else:
-                d_qkv[:, cols] = d
-        if plan:
-            slab_copy(gq, gq_recv, part, 0, 0).start()
-            for stage in range(part):
-                slab_done(gq, gq_recv, part - 1 - stage, stage, 0)
-        tick(4)
-
+                q2a.store(d[:, 0:128], kind * 128)
+                q2b.store(d[:, 128:256], kind * 128)
+        act(f"part{part}")
+
+    wqkv = wqkv.wait()
+
+    @pl.loop(0, width // 256)
+    def _(j):
+        cols = tile(j, 256)
+        dsn[:, cols] = dot_nt(dproj[...], wqkv[cols, :])
+
+    act("norm")
+    tok = tok.wait()
+
+    @pl.loop(0, length // 64)
+    def _(i):
+        rows = tile(i, 64)
+        x = tok[rows].astype(F32)
+        r1 = lax.rsqrt(row_mean(x * x) + EPS)
+        xr = x * r1
+        d = dsn[rows]
+        dn = d * ln1[...]
+        lnacc[8:16] += jnp.sum((d * xr).reshape(8, 8, width), axis=0)
+        igrad[rows] = (dres[rows] + r1 * dn - xr * (r1 * r1) * row_mean(dn * x)).astype(BF16)
+
+    ln1_grad = jnp.where(
+        lax.broadcasted_iota(jnp.int32, (width, 128), 1) == 0, as_columns(lnacc[8:16]), 0.0
+    )
+    if plan:
+        ln_slab.store(ln1_grad, 0)
+    else:
+        d_small[...] += jnp.where(lax.broadcasted_iota(jnp.int32, (width, 128), 1) == 14, as_columns(lnacc[8:16]), 0.0)
+    igrad_s.start()
+    act("input")
+
+    own_f.wait()
     for c in f_copies.values():
         c.wait()
 
@@ -718,60 +880,55 @@
         mix = jnp.where(first, meta[rows, 2:3], jnp.where(second, meta[rows, 3:4], 0.0)).astype(BF16)
         out[rows] = (fk0[rows] + dot(mix, f_back[...].reshape(slots, width))).astype(BF16)
 
-    tick(2)
-
-    @pl.loop(0, width // 256)
-    def _(j):
-        cols = tile(j, 256)
-        fk0[:, cols] = dot_nt(dproj[...], wqkv[cols, :])
-
-    @pl.loop(0, length // 64)
-    def _(i):
-        rows = tile(i, 64)
-        x = tok[rows].astype(F32)
-        r1 = lax.rsqrt(row_mean(x * x) + EPS)
-        xr = x * r1
-        d = fk0[rows]
-        dn = d * ln1[...]
-        lnacc[8:16] += jnp.sum((d * xr).reshape(8, 8, width), axis=0)
-        igrad[rows] = (dres[rows] + r1 * dn - xr * (r1 * r1) * row_mean(dn * x)).astype(BF16)
-
-    ln = jnp.zeros((128, width), F32)
-    row = lax.broadcasted_iota(jnp.int32, (128, width), 0)
-    ln = jnp.where(row == 14, jnp.sum(lnacc[8:16], axis=0, keepdims=True), ln)
-    ln = jnp.where(row == 15, jnp.sum(lnacc[0:8], axis=0, keepdims=True), ln)
-    small = dot_tn(n2b[...], dcat[:, 0:128]) + dot_tn(cot[...], dcat[:, 128:256]) + jnp.transpose(ln)
-    if not plan:
-        d_small[...] = small
-        return
-    slab_store(ga, 0, small, slice(width, width + 128))
-    slab_copy(ga, ga_recv, 0, 0, 3).start()
-    live = [(gq, gq_recv, 0, 2, 0), (gq, gq_recv, 1, 1, 0), (gq, gq_recv, 2, 0, 0), (ga, ga_recv, 0, 0, 3)]
-    while live:
-        for src, bufs, s, stage, base in live:
-            slab_done(src, bufs, s, stage, base)
-        live = [(a, b, s, stage + 1, base) for a, b, s, stage, base in live if stage < 4]
-        tick(4)
-    tick(100)
-    for s in range(3):
-        for kind in range(3):
-            at = kind * width + s * 256
-            d_qkv[:, at : at + 256] = fin[s, :, kind * 256 : kind * 256 + 256]
-    d_attn[...] = fin[3, :, 0:width]
-    d_small[...] = fin[3, :, width : width + 128]
+    out_s.start()
+    act("output")
+    out_s.wait()
+    igrad_s.wait()
+    if plan:
+        g_in_s.start()
+        g_out_s.start()
+        g_in_s.wait()
+        g_out_s.wait()
 
 
 def shape(*s, dtype=BF16):
     return jax.ShapeDtypeStruct(s, dtype)
 
 
-def call(kernel, outs, scratch, args, name, collective_id):
+class Staged:
+    def __init__(self, far, near, sem, out):
+        self.far, self.near = far, near
+        src, dst = (near, far) if out else (far, near)
+        self.copy = lambda: pltpu.make_async_copy(src, dst, sem)
+
+    def start(self):
+        self.copy().start()
+
+    def wait(self):
+        self.copy().wait()
+        return self.near
+
+
+def call(kernel, outs, scratch, args, name, collective_id, far, staged):
+    shapes = [jax.ShapeDtypeStruct(a.shape, a.dtype) for a in args] + list(outs)
+    specs = [
+        pl.BlockSpec(memory_space=pl.ANY if n in far or n in staged else pltpu.VMEM) for n in range(len(shapes))
+    ]
+    own = len(shapes) + len(scratch)
+    extra = [pltpu.VMEM(shapes[n].shape, shapes[n].dtype) for n in staged]
+
+    def wrapped(*refs):
+        given, rest, near, sems = list(refs[: len(shapes)]), refs[len(shapes) : own], refs[own:-1], refs[-1]
+        for i, n in enumerate(staged):
+            given[n] = Staged(given[n], near[i], sems.at[i], n >= len(args))
+        kernel(*given, *rest)
+
     return pl.pallas_call(
-        kernel,
+        wrapped,
         out_shape=outs,
-        in_specs=[pl.BlockSpec(memory_space=pltpu.VMEM)] * len(args),
-        out_specs=[pl.BlockSpec(memory_space=pltpu.VMEM)] * len(outs),
-        scratch_shapes=scratch,
+        in_specs=specs[: len(args)],
+        out_specs=specs[len(args) :],
+        scratch_shapes=list(scratch) + extra + [pltpu.SemaphoreType.DMA((len(staged),))],
         compiler_params=pltpu.CompilerParams(
             vmem_limit_bytes=VMEM_LIMIT, has_side_effects=True, collective_id=collective_id
         ),
@@ -809,10 +966,11 @@
             V((length, 256), F32), V((length, length), F32), V((128, width), F32), V((3, length, 128), F32),
             V((128, length), F32), V((length, width), BF16), V((length, width), BF16), V((2 * length, 128), BF16),
             V((length, 128), F32), V((slots, length), BF16), V((experts, capacity, width), BF16),
-            DMA((peers,)), DMA((peers,)),
+            DMA((peers,)), DMA((peers,)), V((heads, length, length), BF16), V((experts, capacity, width + 128), BF16),
+            DMA((width // 128, 2)), DMA((experts + 1,)),
         ],
         (tokens, segments, rT, pT, ln1, w_qkv, w_attn, ln2, wrT, cmT, cotangent, cos, sin),
-        "attention", 0,
+        "attention", 0, (16, 21, 22), (0, 5, 6, 10, 11, 12, 13, 14, 15, 17, 18, 19),
     )
 
     tiles, slabs = 4, 2
@@ -826,21 +984,22 @@
         return (s[0], s[1] // n, s[2])
 
     wide = width + 128
-    f_rows, d_back, g_out, g_in = call(
+    late = (tiles, width // 2, ft)
+    early = (tiles, width // 4, ft)
+    f_rows, d_back, g_out, *g_in = call(
         functools.partial(expert_kernel, stages),
-        [
-            shape(experts, capacity, width), shape(experts, capacity, wide), shape(*slab_out),
-            shape(*part_of(slab_in, 2 if within else 1)),
-        ],
+        [shape(experts, capacity, width), shape(experts, capacity, wide), shape(*slab_out)]
+        + ([shape(*late), shape(*early)] if within else [shape(*slab_in)]),
         [
             V((experts, capacity, wide), BF16), V((slots, width), BF16), V((tiles, slots, ft), BF16),
             V((tiles, slots, 2 * ft), BF16), V((slots, width), F32), V((slots, width), F32),
             V((experts, capacity, wide), BF16),
         ]
-        + ([V(slab_in, BF16)] + [DMA((2 * tiles,))] * 2 if within else [])
-        + [DMA((peers,))] * 4,
+        + ([V(slab_in, BF16), V(late, BF16)] + [DMA((2 * tiles,))] * 2 + [DMA((tiles,))] * 2 if within else [])
+        + [DMA((peers,))] * 4
+        + [DMA((2,))],
         (send, g_rows, expert_in, expert_out),
-        "experts", 1,
+        "experts", 1, (0, 5), (1, 2, 3, 4, 6) + ((7, 8) if within else (7,)),
     )
 
     args = (
@@ -858,27 +1017,32 @@
         V((2, length, 128), F32), V((length, 256), BF16), V((length, width), BF16), V((length, width), F32),
         V((length, width), BF16), V((length, 3 * width), BF16), V((length, width), BF16),
         V((2, length, 128), F32), V((16, width), F32), V((experts, capacity, width), BF16), DMA((peers,)), DMA((peers,)),
+        V((heads, length, length), BF16), DMA((3,)),
     ]
     if within:
-        args += (g_in, g_out)
-        outs += [shape(width // n_dp, 2 * hidden, dtype=F32), shape(hidden // n_dp, width, dtype=F32)]
+        args += (g_in[1], g_in[0], g_out)
+        outs += [
+            shape(rows, 128, dtype=F32),
+            shape(width // n_dp, 2 * hidden, dtype=F32), shape(hidden // n_dp, width, dtype=F32)]
         scratch += [
-            V(part_of(slab_in, 4), BF16), V(part_of(slab_in, 8), BF16), V(part_of(slab_out, 2), BF16),
+            V(early, BF16), V(part_of(slab_in, 8), BF16), V(part_of(slab_out, 2), BF16),
             V(part_of(slab_out, 4), BF16), V(part_of(slab_out, 8), BF16), DMA((2, 2 * tiles)), DMA((2, 2 * tiles)),
             DMA((3, slabs)), DMA((3, slabs)),
-            V((3, width, width), BF16), V((1, width, wide), BF16),
         ]
-        scratch += [V((3, width >> s, width), BF16) for s in range(1, 5)]
-        scratch += [V((1, width >> s, wide), BF16) for s in range(1, 5)]
-        scratch += [
-            V((4, 2 * rows, wide), F32), V((4, rows, wide), F32), V((4, rows, wide), F32), DMA((4, 5)), DMA((4, 5)),
-        ]
+        for cols in (wide, width, width, width // 2, width // 2, 128):
+            scratch += [V((width >> s, cols), BF16) for s in range(5)]
+            scratch += [V((2 * rows, cols), F32), V((rows, cols), F32), DMA((5,)), DMA((5,))]
     plan = (stages, order) if within else ()
-    done = call(functools.partial(bwd_kernel, plan), outs, scratch, args, "backward", 2)
+    n = len(args)
+    staged = (0, 1, 2, 6, 7, 8, 9, 11, 12, 14, 15, 20, 21) + tuple(range(22, n)) + (n, n + 1)
+    staged += (n + 6, n + 7) if within else ()
+    done = call(functools.partial(bwd_kernel, plan), outs, scratch, args, "backward", 2, (5, 10), staged)
     out, igrad, d_qkv, d_attn, small = done[:5]
     if within:
-        g_in, g_out = done[5:]
+        ln, g_in, g_out = done[5:]
+        ln = ln[:, 0]
     else:
+        (g_in,) = g_in
         g_in = jnp.moveaxis(g_in.reshape(tiles, 2, width, ft), 2, 0).transpose(0, 2, 1, 3).reshape(width, 2 * hidden)
         g_out = jnp.moveaxis(g_out, 0, 1).reshape(hidden, width)
         g_in = lax.psum_scatter(g_in, "dp", scatter_dimension=0, tiled=True).astype(F32)
@@ -886,8 +1050,9 @@
         d_qkv, d_attn, small = (
             lax.psum_scatter(d, ("dp", "expert"), scatter_dimension=0, tiled=True) for d in (d_qkv, d_attn, small)
         )
+        ln = small[:, 14]
     return (
-        out, igrad, small[:, 14], d_qkv, d_attn, small[:, 15], small[:, 0:8], small[:, 8:12], small[:, 12:14],
+        out, igrad, ln, d_qkv, d_attn, small[:, 15], small[:, 0:8], small[:, 8:12], small[:, 12:14],
         g_in[None], g_out[None],
     )
 

time: 237 us -> 213 us (0.90)
  Pallas kernels: 221 us -> 197 us
    pallas_call x3, Pallas kernels: 221 us -> 197 us  [call(): pl.pallas_call(wrapped, out_shape=outs, in_specs=specs[:len(args)], out_s...]
where the time goes in v4:
time: 213 us; the launch traced here: 212 us
  Pallas kernels  197 us (92%)
  local copies, waits for them, and re-layouts  14.7 us (7%)
    pallas_call x3, Pallas kernels, call(): pl.pallas_call(wrapped, out_shape=outs, in_specs=specs[:len(args)], out_s...  197 us
    unnamed x19, local copies, waits for them, and re-layouts  9.08 us

profile of v4, /device:TPU:0, one launch (start us, length us, event | category | flops | bytes accessed | tf_op | source)
XLA Modules:
  0.0 212.1 jit_solution(12848921784542205343)
XLA Ops:
  0.6 1.3 reshape.28.refs_4_.refs_13_
  1.9 1.3 reshape.29.refs_7_.refs_16_
  3.2 31.9 %attention.1 = (bf16[512,768]{1,0:T(8,128)(2,1)}, bf16[512,768]{1,0:T(8,128)(2,1)}, bf16[512,768]{1,0:T(8,128)(2,1)}, bf16[12,512,512]{2,1,0:T(8,128)(2,1)}, bf1...) custom-call(bf16[512,768]{1,0:T(8,128)(2,1)} %refs_0_.3, ...), custom_call_target="tpu_custom_call" | custom-call | tf_op jit(solution)/shard_map/attention/pallas_call | solution.py:926
  35.1 73.9 %experts.1 = (bf16[4,256,768]{2,1,0:T(8,128)(2,1)}, bf16[4,256,896]{2,1,0:T(8,128)(2,1)}, bf16[2,2048,384]{2,1,0:T(8,128)(2,1)}, bf16[4,384,512]{2,1,0:T(8,128)(2,1)}, bf16[4,192,512]{2,1,0:T(8,128)(2,1)}) custom-call(bf16[4,256,896]{2,1,0:T(8,128)(2,1)} %get-tuple-element.36.refs_0_, bf16[4,256,768]{2,1,0:T(8,128)(2,1)} %get-tuple-element.37.refs_1_, ...), custom_call_target="tpu_custom_call" | custom-call | tf_op jit(solution)/shard_map/experts/pallas_call | solution.py:926
  109.0 90.9 %backward.1 = (bf16[512,768]{1,0:T(8,128)(2,1)}, bf16[512,768]{1,0:T(8,128)(2,1)}, f32[24,2304]{1,0:T(8,128)}, f32[24,768]{1,0:T(8,128)}, f32[24,128]{1,0:T(8,12...) custom-call(bf16[512,768]{1,0:T(8,128)(2,1)} %refs_0_.3, bf16[512,768]{1,0:T(8,128)(2,1)} %refs_1_.3, ...), custom_call_target="tpu_custom_call" | custom-call | tf_op jit(solution)/shard_map/backward/pallas_call | solution.py:926
  199.9 0.0 copy-start.2
  199.9 0.0 copy-start.3
  199.9 1.5 slice_reduce_fusion
  201.4 1.4 copy.30
  202.7 0.0 copy-start.4
  202.8 0.8 slice.19
  203.6 0.6 copy.32
  204.2 0.8 slice.18
  205.0 0.7 copy.31
  205.6 0.0 copy-start
  205.6 2.2 %copy.39 = bf16[512,768]{1,0:T(8,128)(2,1)} copy(bf16[512,768]{1,0:T(8,128)(2,1)} %get-tuple-element.92) | data formatting | bytes 1572864
  207.8 0.0 copy-done.2
  207.8 0.9 copy.40
  208.7 0.0 copy-done.3
  208.7 0.0 copy-start.1
  208.7 0.7 copy.41
  209.4 0.0 copy-done.4
  209.4 0.6 copy.42
  210.0 0.0 copy-done
  210.0 1.1 copy.43
  211.2 0.0 copy-done.1
  211.2 0.9 copy.44
Async XLA Ops:
  199.9 8.0 %copy-start.2 = (bf16[512,768]{1,0:T(8,128)(2,1)S(1)}, bf16[512,768]{1,0:T(8,128)(2,1)}, u32[]{:S(2)}) copy-start(bf16[512,768]{1,0:T(8,128)(2,1)} %get-tuple-element.93) | copy-start | bytes 2359300
  199.9 8.8 %copy-start.3 = (f32[24,2304]{1,0:T(8,128)S(1)}, f32[24,2304]{1,0:T(8,128)}, u32[]{:S(2)}) copy-start(f32[24,2304]{1,0:T(8,128)} %get-tuple-element.95) | copy-start | bytes 663556
  202.7 6.6 %copy-start.4 = (f32[24,768]{1,0:T(8,128)S(1)}, f32[24,768]{1,0:T(8,128)}, u32[]{:S(2)}) copy-start(f32[24,768]{1,0:T(8,128)} %get-tuple-element.96) | copy-start | bytes 221188
  205.6 4.4 %copy-start = (f32[96,4096]{1,0:T(8,128)S(1)}, f32[96,4096]{1,0:T(8,128)}, u32[]{:S(2)}) copy-start(f32[96,4096]{1,0:T(8,128)} %get-tuple-element.55) | copy-start | bytes 4718596
  208.7 2.5 %copy-start.1 = (f32[256,768]{1,0:T(8,128)S(1)}, f32[256,768]{1,0:T(8,128)}, u32[]{:S(2)}) copy-start(f32[256,768]{1,0:T(8,128)} %get-tuple-element.56) | copy-start | bytes 2359300

commit v5 on v4

--- a/solution.py
+++ b/solution.py
@@ -109,7 +109,7 @@
 
 
 def half_copy(src, dst, mask, rows, send_sem, recv_sem):
-    start = pl.multiple_of((1 - side(mask)) * rows, 8)
+    start = pl.multiple_of((1 - side(mask)) * rows, 16)
     return pltpu.make_async_remote_copy(
         src.at[pl.ds(start, rows)], dst, send_sem, recv_sem, device_id=partner(mask), device_id_type=MESH
     )
@@ -117,13 +117,13 @@
 
 def half_add(src, dst, mask, rows, out=None):
     start = side(mask) * rows
-    step = 48 if rows % 48 == 0 else 64 if rows % 64 == 0 else 24
+    step = 48 if rows % 48 == 0 else 64
     out = dst if out is None else out
 
     @pl.loop(0, rows // step)
     def _(i):
-        here = pl.ds(pl.multiple_of(i * step, 8), step)
-        mine = src[pl.ds(pl.multiple_of(start + i * step, 8), step)].astype(F32)
+        here = pl.ds(pl.multiple_of(i * step, 16), step)
+        mine = src[pl.ds(pl.multiple_of(start + i * step, 16), step)].astype(F32)
         out[here] = (mine + dst[here].astype(F32)).astype(out.dtype)
 
 
@@ -185,7 +185,7 @@
         rows = tile(i, 64)
         x = tok[rows].astype(F32)
         r = lax.rsqrt(row_mean(x * x) + EPS)
-        n1[rows] = (x * r * ln1[...]).astype(BF16)
+        n1[rows] = (x * r * ln1[0:1]).astype(BF16)
 
     n1_out.start()
     wqkv, cos, sin = wqkv.wait(), cos.wait(), sin.wait()
@@ -259,7 +259,7 @@
     def _(i):
         rows = tile(i, 64)
         x = res[rows]
-        n2 = x * lax.rsqrt(row_mean(x * x) + EPS) * ln2[...]
+        n2 = x * lax.rsqrt(row_mean(x * x) + EPS) * ln2[1:2]
         high = n2.astype(BF16)
         n2b[rows] = high
         n2l[rows] = (n2 - high.astype(F32)).astype(BF16)
@@ -509,8 +509,8 @@
         c.wait()
 
 
-def out_start(copy, i):
-    copy(i, 0).start()
+def out_start(copy, i, s):
+    copy(i, s).start()
 
 
 def as_columns(x):
@@ -521,40 +521,39 @@
 class Slab:
     def __init__(self, order, refs):
         self.order = order
-        self.bufs, (self.pair, self.got, self.send, self.recv) = refs[:5], refs[5:]
+        self.bufs, (self.send, self.recv) = refs[:6], refs[6:]
         self.bits = [m * (1 if a == "expert" else lax.axis_size("expert")) for a, m in order]
         self.out = ()
 
-    def store(self, value, at):
+    def store(self, value, piece):
         total = 2 ** len(self.order)
-        size, cols = value.shape[0] // total, slice(at, at + value.shape[1])
+        size = value.shape[0] // total
         for j in range(total):
-            other = j + self.bits[-1]
-            if (j // self.bits[-1]) % 2:
-                continue
-            row = place_of(j, self.bits[:-1]) * 2 * size
-            both = jnp.concatenate([value[j * size : (j + 1) * size], value[other * size : (other + 1) * size]], axis=0)
-            self.bufs[0][row : row + 2 * size, cols] = both.astype(BF16)
+            row = place_of(j, self.bits) * 2 * size
+            mine = value[j * size : (j + 1) * size]
+            both = jnp.concatenate([mine[:, 0:128], mine[:, 128:256]], axis=0)
+            self.bufs[0][row : row + 2 * size, piece * 128 : piece * 128 + 128] = both.astype(BF16)
 
     def copy(self, s):
-        src, dst = (self.bufs[s], self.bufs[s + 1]) if s < 4 else (self.pair, self.got)
-        return half_copy(src, dst, self.order[s], dst.shape[0], self.send.at[s], self.recv.at[s])
+        dst = self.bufs[s + 1]
+        return half_copy(self.bufs[s], dst, self.order[s], dst.shape[0], self.send.at[s], self.recv.at[s])
 
     def start(self):
         self.copy(0).start()
 
     def done(self, s):
         self.copy(s).wait()
+        rows = self.bufs[s + 1].shape[0]
         if s < 4:
-            into = self.pair if s == 3 else None
-            half_add(self.bufs[s], self.bufs[s + 1], self.order[s], self.bufs[s + 1].shape[0], into)
+            half_add(self.bufs[s], self.bufs[s + 1], self.order[s], rows)
             self.copy(s + 1).start()
             return
-        rows = self.got.shape[0]
-        mine = self.pair[pl.ds(pl.multiple_of(side(self.order[4]) * rows, 8), rows)]
-        total = mine + self.got[...]
-        for ref, at, col, n in self.out:
-            ref[:, at : at + n] = total[:, col : col + n]
+        mine = self.bufs[4][pl.ds(pl.multiple_of(side(self.order[4]) * rows, 16), rows)]
+        total = mine.astype(F32) + self.bufs[5][...].astype(F32)
+        for piece, parts in enumerate(self.out):
+            for n, (ref, at) in enumerate(parts):
+                half = slice(n * rows // 2, (n + 1) * rows // 2)
+                ref[:, at : at + 128] = total[half, piece * 128 : piece * 128 + 128]
 
 
 def bwd_kernel(plan, *refs):
@@ -591,7 +590,7 @@
     acts = {}
     if plan:
         in1, in2, out0, out1, out2, in_send, in_recv, out_send, out_recv = refs[:9]
-        slab_refs = [refs[9 + 9 * n : 18 + 9 * n] for n in range(6)]
+        slab_refs = [refs[9 + 8 * n : 17 + 8 * n] for n in range(6)]
         late = p_late.near.shape[0]
         slabs_in = late + p_early.near.shape[0]
         ft = p_late.near.shape[2]
@@ -635,49 +634,46 @@
             if s < 2:
                 out_copy(i, s + 1).start()
 
-        swapped = (order[0], order[2], order[1], order[3], order[4])
-        slabs = [Slab(o, r) for o, r in zip((order, order, order, order, swapped, order), slab_refs)]
-        attn_slab, q0, q1, q2a, q2b, ln_slab = slabs
-
-        def q_out(first, pairs):
-            n = 128 * pairs
-            return [(d_qkv, kind * width + first * 128, kind * n, n) for kind in range(3)]
-
-        attn_slab.out = [(d_attn, 0, 0, width), (d_small, 0, width, 128)]
-        q0.out, q1.out, q2a.out, q2b.out = q_out(0, 2), q_out(2, 2), q_out(4, 1), q_out(5, 1)
-        ln_slab.out = [(d_ln, 0, 0, 128)]
-
+        attn_slab, q0, q1, q2a, q2b, ln_slab = (Slab(order, r) for r in slab_refs)
+
+        def columns(ref, at):
+            return ((ref, at), (ref, at + 128))
+
+        attn_slab.out = [columns(d_attn, 256 * n) for n in range(3)]
+        q0.out = [columns(d_qkv, kind * width) for kind in range(3)]
+        q1.out = [columns(d_qkv, kind * width + 256) for kind in range(3)]
+        q2a.out = [columns(d_qkv, kind * width + 512) for kind in range(2)]
+        q2b.out = [columns(d_qkv, 2 * width + 512)]
+        ln_slab.out = [((d_ln, 0), (d_small, 0))]
+
+        for i in (1, 2):
+            in_copy(i, 1).start()
         out_copy(0, 0).start()
-        for i in range(slabs_in - late):
-            in_copy(i, 1).start()
-        for i in range(slabs_in - late, slabs_in, 2):
-            in_copy(i, 0).start()
-        a, b = slabs_in - late, slabs_in
+        in_copy(6, 0).start()
+        in_copy(3, 1).start()
+        out_copy(1, 0).start()
         acts = {
-            "token": [(in_done, i, 0) for i in range(a, b, 2)]
-            + [(in_done, i, 1) for i in range(a)]
-            + [(out_start, out_copy, 1)],
-            "attn": [(attn_slab.start,), (out_done, 0, 0)],
-            "part0": [(q0.start,), (attn_slab.done, 0)],
-            "part1": [(q1.start,), (q0.done, 0), (attn_slab.done, 1), (out_done, 0, 1)]
-            + [(out_start, in_copy, i) for i in range(a + 1, b, 2)]
-            + [(in_done, i, 1) for i in range(a, b, 2)],
-            "part2": [
-                (q2a.start,), (q2b.start,), (q1.done, 0), (q0.done, 1), (attn_slab.done, 2), (out_done, 1, 0),
+            "token": [(out_start, in_copy, 5, 0), (in_done, 1, 1)],
+            "attn": [
+                (out_start, in_copy, 0, 1), (out_start, in_copy, 4, 0), (attn_slab.start,), (in_done, 6, 0),
+                (in_done, 2, 1),
             ],
-            "norm": [(q2a.done, 0), (q2b.done, 0), (q1.done, 1), (q0.done, 2), (attn_slab.done, 3)]
-            + [(in_done, i, 0) for i in range(a + 1, b, 2)]
-            + [(out_done, 0, 2)],
-            "input": [
-                (ln_slab.start,), (q2a.done, 1), (q2b.done, 1), (q1.done, 2), (q0.done, 3), (attn_slab.done, 4),
-                (out_done, 1, 1), (ln_slab.done, 0),
+            "part0": [(q0.start,), (in_done, 3, 1), (attn_slab.done, 0)],
+            "part1": [
+                (out_start, in_copy, 7, 0), (q1.start,), (in_done, 0, 1), (out_done, 0, 0), (in_done, 4, 0),
+                (q0.done, 0),
             ],
+            "part2": [(q2a.start,), (q2b.start,), (in_done, 6, 1), (q1.done, 0), (attn_slab.done, 1)],
+            "norm": [(q2a.done, 0), (q2b.done, 0), (q0.done, 1), (out_done, 0, 1)],
+            "input": [(ln_slab.start,), (in_done, 4, 1)],
             "output": [
-                (q2a.done, 2), (q2b.done, 2), (ln_slab.done, 1), (q1.done, 3), (q0.done, 4), (ln_slab.done, 2),
-                (q2a.done, 3), (q2b.done, 3), (q1.done, 4), (ln_slab.done, 3), (q2a.done, 4), (q2b.done, 4),
-            ]
-            + [(in_done, i, 1) for i in range(a + 1, b, 2)]
-            + [(ln_slab.done, 4), (out_done, 1, 2)],
+                (out_done, 1, 0), (ln_slab.done, 0), (q1.done, 1), (in_done, 5, 0), (q2a.done, 1), (out_done, 0, 2),
+                (in_done, 7, 0), (q2b.done, 1), (ln_slab.done, 1), (out_done, 1, 1), (attn_slab.done, 2),
+                (in_done, 5, 1), (q0.done, 2), (in_done, 7, 1), (q1.done, 2), (q2a.done, 2), (q2b.done, 2),
+                (attn_slab.done, 3), (ln_slab.done, 2), (q0.done, 3), (out_done, 1, 2), (q1.done, 3), (q2a.done, 3),
+                (q2b.done, 3), (attn_slab.done, 4), (ln_slab.done, 3), (q0.done, 4), (q1.done, 4), (q2a.done, 4),
+                (q2b.done, 4), (ln_slab.done, 4),
+            ],
         }
     for c in f_copies.values():
         c.start()
@@ -735,7 +731,7 @@
         x = res[rows]
         r2 = lax.rsqrt(row_mean(x * x) + EPS)
         xr = x * r2
-        n2 = xr * ln2[...]
+        n2 = xr * ln2[1:2]
         n2b[rows] = n2.astype(BF16)
         cv = (cvT[0:1, :], cvT[1:2, :])
         fk0[rows] = x + keep * n2 + (cg[0] * shares[0][1]) * cv[0] + (cg[1] * shares[1][1]) * cv[1]
@@ -763,7 +759,7 @@
         dcat[rows, 128:256] = vecs.astype(BF16)
         dn2 = keep * g + dsn[rows] + dot(cat.astype(BF16), w_high)
         lnacc[0:8] += jnp.sum((dn2 * xr).reshape(8, 8, width), axis=0)
-        dn = dn2 * ln2[...]
+        dn = dn2 * ln2[1:2]
         dr = g + r2 * dn - xr * (r2 * r2) * row_mean(dn * x)
         dres[rows] = dr
         dbr[rows] = dr.astype(BF16)
@@ -773,15 +769,6 @@
             ref.wait()
     act("token")
     wattn, att = wattn.wait(), att.wait()
-    small = dot_tn(n2b[...], dcat[:, 0:128]) + dot_tn(cot[...], dcat[:, 128:256])
-    small = small + jnp.where(
-        lax.broadcasted_iota(jnp.int32, small.shape, 1) == 15, as_columns(lnacc[0:8]), 0.0
-    )
-    if plan:
-        attn_slab.store(small, width)
-    else:
-        d_small[...] = small
-
     @pl.loop(0, width // 256)
     def _(j):
         cols = tile(j, 256)
@@ -791,7 +778,7 @@
         cols = slice(j * 256, (j + 1) * 256)
         d = dot_tn(att[...], dbr[:, cols])
         if plan:
-            attn_slab.store(d, j * 256)
+            attn_slab.store(d, j)
         else:
             d_attn[:, cols] = d
     act("attn")
@@ -832,10 +819,11 @@
             if not plan:
                 d_qkv[:, cols] = d
             elif part < 2:
-                (q0, q1)[part].store(d, kind * 256)
+                (q0, q1)[part].store(d, kind)
+            elif kind < 2:
+                q2a.store(d, kind)
             else:
-                q2a.store(d[:, 0:128], kind * 128)
-                q2b.store(d[:, 128:256], kind * 128)
+                q2b.store(d, 0)
         act(f"part{part}")
 
     wqkv = wqkv.wait()
@@ -855,17 +843,18 @@
         r1 = lax.rsqrt(row_mean(x * x) + EPS)
         xr = x * r1
         d = dsn[rows]
-        dn = d * ln1[...]
+        dn = d * ln1[0:1]
         lnacc[8:16] += jnp.sum((d * xr).reshape(8, 8, width), axis=0)
         igrad[rows] = (dres[rows] + r1 * dn - xr * (r1 * r1) * row_mean(dn * x)).astype(BF16)
 
-    ln1_grad = jnp.where(
-        lax.broadcasted_iota(jnp.int32, (width, 128), 1) == 0, as_columns(lnacc[8:16]), 0.0
-    )
+    lanes = lax.broadcasted_iota(jnp.int32, (width, 128), 1)
+    small = dot_tn(n2b[...], dcat[:, 0:128]) + dot_tn(cot[...], dcat[:, 128:256])
+    small = small + jnp.where(lanes == 14, as_columns(lnacc[8:16]), 0.0)
+    small = small + jnp.where(lanes == 15, as_columns(lnacc[0:8]), 0.0)
     if plan:
-        ln_slab.store(ln1_grad, 0)
+        ln_slab.store(jnp.concatenate([small, small], axis=1), 0)
     else:
-        d_small[...] += jnp.where(lax.broadcasted_iota(jnp.int32, (width, 128), 1) == 14, as_columns(lnacc[8:16]), 0.0)
+        d_small[...] = small
     igrad_s.start()
     act("input")
 
@@ -934,6 +923,43 @@
         ),
         name=name,
     )(*args)
+
+
+def final_kernel(n, *refs):
+    src, small, dst = refs[:n], refs[n], refs[n + 1 : 2 * n + 1]
+    router, mix, vec, ln1, ln2 = refs[2 * n + 1 : 2 * n + 6]
+    near, sems = refs[2 * n + 6 : 3 * n + 6], refs[-1]
+    loads = [pltpu.make_async_copy(a, b, sems.at[0, i]) for i, (a, b) in enumerate(zip(src, near))]
+    copies = [pltpu.make_async_copy(a, b, sems.at[1, i]) for i, (a, b) in enumerate(zip(near, dst))]
+    for c in loads:
+        c.start()
+    rows = small.shape[0]
+    t = jnp.transpose(jnp.concatenate([small[...], jnp.zeros((128 - rows, 128), F32)], axis=0))[:, 0:rows]
+    router[...] = t[0:8]
+    mix[...] = t[8:12]
+    vec[...] = t[12:14]
+    ln1[...] = t[14:15]
+    ln2[...] = t[15:16]
+    for a, b in zip(loads, copies):
+        a.wait()
+        b.start()
+    for c in copies:
+        c.wait()
+
+
+def final(big, small):
+    rows = small.shape[0]
+    far, near = pl.BlockSpec(memory_space=pl.ANY), pl.BlockSpec(memory_space=pltpu.VMEM)
+    return pl.pallas_call(
+        functools.partial(final_kernel, len(big)),
+        out_shape=[jax.ShapeDtypeStruct(a.shape, a.dtype) for a in big]
+        + [shape(n, rows, dtype=F32) for n in (8, 4, 2, 1, 1)],
+        in_specs=[far] * len(big) + [near],
+        out_specs=[far] * len(big) + [near] * 5,
+        scratch_shapes=[pltpu.VMEM(a.shape, a.dtype) for a in big] + [pltpu.SemaphoreType.DMA((2, len(big)))],
+        compiler_params=pltpu.CompilerParams(vmem_limit_bytes=VMEM_LIMIT),
+        name="results",
+    )(*big, small)
 
 
 def body(
@@ -952,7 +978,8 @@
     cos, sin = (jnp.asarray(t) for t in rotary_tables(length))
     rT, pT = routes.T, prev_logits.T
     wrT, cmT, cvT = w_router.T, const_mix.T, const_vec.T
-    ln1, ln2 = ln1_gain.reshape(1, width), ln2_gain.reshape(1, width)
+    gains = jnp.stack([ln1_gain, ln2_gain])
+    ln1 = ln2 = gains
     peers = experts - 1
 
     q, k, v, pw, att, n1, res, meta, send, g_rows = call(
@@ -1029,9 +1056,8 @@
             V(part_of(slab_out, 4), BF16), V(part_of(slab_out, 8), BF16), DMA((2, 2 * tiles)), DMA((2, 2 * tiles)),
             DMA((3, slabs)), DMA((3, slabs)),
         ]
-        for cols in (wide, width, width, width // 2, width // 2, 128):
-            scratch += [V((width >> s, cols), BF16) for s in range(5)]
-            scratch += [V((2 * rows, cols), F32), V((rows, cols), F32), DMA((5,)), DMA((5,))]
+        for cols in (width, width, width, 512, 256, 256):
+            scratch += [V((2 * width >> s, cols // 2), BF16) for s in range(6)] + [DMA((5,)), DMA((5,))]
     plan = (stages, order) if within else ()
     n = len(args)
     staged = (0, 1, 2, 6, 7, 8, 9, 11, 12, 14, 15, 20, 21) + tuple(range(22, n)) + (n, n + 1)
@@ -1039,20 +1065,23 @@
     done = call(functools.partial(bwd_kernel, plan), outs, scratch, args, "backward", 2, (5, 10), staged)
     out, igrad, d_qkv, d_attn, small = done[:5]
     if within:
-        ln, g_in, g_out = done[5:]
-        ln = ln[:, 0]
-    else:
-        (g_in,) = g_in
-        g_in = jnp.moveaxis(g_in.reshape(tiles, 2, width, ft), 2, 0).transpose(0, 2, 1, 3).reshape(width, 2 * hidden)
-        g_out = jnp.moveaxis(g_out, 0, 1).reshape(hidden, width)
-        g_in = lax.psum_scatter(g_in, "dp", scatter_dimension=0, tiled=True).astype(F32)
-        g_out = lax.psum_scatter(g_out, "dp", scatter_dimension=0, tiled=True).astype(F32)
-        d_qkv, d_attn, small = (
-            lax.psum_scatter(d, ("dp", "expert"), scatter_dimension=0, tiled=True) for d in (d_qkv, d_attn, small)
+        out, igrad, d_qkv, d_attn, g_in, g_out, router, mix, vec, ln_one, ln_two = final(
+            (out, igrad, d_qkv, d_attn, done[6], done[7]), small
         )
-        ln = small[:, 14]
+        return (
+            out, igrad, ln_one.reshape(rows), d_qkv, d_attn, ln_two.reshape(rows), router.T, mix.T, vec.T,
+            g_in[None], g_out[None],
+        )
+    (g_in,) = g_in
+    g_in = jnp.moveaxis(g_in.reshape(tiles, 2, width, ft), 2, 0).transpose(0, 2, 1, 3).reshape(width, 2 * hidden)
+    g_out = jnp.moveaxis(g_out, 0, 1).reshape(hidden, width)
+    g_in = lax.psum_scatter(g_in, "dp", scatter_dimension=0, tiled=True).astype(F32)
+    g_out = lax.psum_scatter(g_out, "dp", scatter_dimension=0, tiled=True).astype(F32)
+    d_qkv, d_attn, small = (
+        lax.psum_scatter(d, ("dp", "expert"), scatter_dimension=0, tiled=True) for d in (d_qkv, d_attn, small)
+    )
     return (
-        out, igrad, ln, d_qkv, d_attn, small[:, 15], small[:, 0:8], small[:, 8:12], small[:, 12:14],
+        out, igrad, small[:, 14], d_qkv, d_attn, small[:, 15], small[:, 0:8], small[:, 8:12], small[:, 12:14],
         g_in[None], g_out[None],
     )
 

time: 213 us -> 191 us (0.90)
  local copies, waits for them, and re-layouts: 14.7 us -> 1.38 us
  Pallas kernels: 197 us -> 188 us
    pallas_call x3, Pallas kernels: 197 us -> 183 us  [call(): pl.pallas_call(wrapped, out_shape=outs, in_specs=specs[:len(args)], out_s...]
    unnamed x19 -> x0, local copies, waits for them, and re-layouts: 9.08 us -> none
    pallas_call x0 -> x1, Pallas kernels: none -> 4.8 us  [final(): pl.pallas_call(functools.partial(final_kernel, len(big)), out_shape=[jax....]
    slice x3 -> x0, local copies, waits for them, and re-layouts: 3.09 us -> none  [the longest x1 1.51 us: body(): small[:, 15]]
    reshape x2 -> x0, local copies, waits for them, and re-layouts: 2.53 us -> none  [body(): ln1, ln2 = (ln1_gain.reshape(1, width), ln2_gain.reshape(1, width))]
where the time goes in v5:
time: 191 us; the launch traced here: 190 us
  Pallas kernels  188 us (98%)
    pallas_call x3, Pallas kernels, call(): pl.pallas_call(wrapped, out_shape=outs, in_specs=specs[:len(args)], out_s...  183 us
    pallas_call x1, Pallas kernels, final(): pl.pallas_call(functools.partial(final_kernel, len(big)), out_shape=[jax....  4.8 us

profile of v5, /device:TPU:0, one launch (start us, length us, event | category | flops | bytes accessed | tf_op | source)
XLA Modules:
  0.0 190.4 jit_solution(7067875152741445190)
XLA Ops:
  0.6 0.7 stack.9
  1.3 0.7 stack.10
  2.0 0.6 pad_maximum_fusion.refs_4_.refs_7_.refs_13_.refs_16_
  2.6 31.9 %attention.1 = (bf16[512,768]{1,0:T(8,128)(2,1)}, bf16[512,768]{1,0:T(8,128)(2,1)}, bf16[512,768]{1,0:T(8,128)(2,1)}, bf16[12,512,512]{2,1,0:T(8,128)(2,1)}, bf1...) custom-call(bf16[512,768]{1,0:T(8,128)(2,1)} %refs_0_.3, ...), custom_call_target="tpu_custom_call" | custom-call | tf_op jit(solution)/shard_map/attention/pallas_call | solution.py:915
  34.6 73.9 %experts.1 = (bf16[4,256,768]{2,1,0:T(8,128)(2,1)}, bf16[4,256,896]{2,1,0:T(8,128)(2,1)}, bf16[2,2048,384]{2,1,0:T(8,128)(2,1)}, bf16[4,384,512]{2,1,0:T(8,128)(2,1)}, bf16[4,192,512]{2,1,0:T(8,128)(2,1)}) custom-call(bf16[4,256,896]{2,1,0:T(8,128)(2,1)} %get-tuple-element.46.refs_0_, bf16[4,256,768]{2,1,0:T(8,128)(2,1)} %get-tuple-element.47.refs_1_, ...), custom_call_target="tpu_custom_call" | custom-call | tf_op jit(solution)/shard_map/experts/pallas_call | solution.py:915
  108.4 77.0 %backward.1 = (bf16[512,768]{1,0:T(8,128)(2,1)}, bf16[512,768]{1,0:T(8,128)(2,1)}, f32[24,2304]{1,0:T(8,128)}, f32[24,768]{1,0:T(8,128)}, f32[24,128]{1,0:T(8,12...) custom-call(bf16[512,768]{1,0:T(8,128)(2,1)} %refs_0_.3, bf16[512,768]{1,0:T(8,128)(2,1)} %refs_1_.3, ...), custom_call_target="tpu_custom_call" | custom-call | tf_op jit(solution)/shard_map/backward/pallas_call | solution.py:915
  185.4 4.8 %results.1 = (bf16[512,768]{1,0:T(8,128)(2,1)}, bf16[512,768]{1,0:T(8,128)(2,1)}, f32[24,2304]{1,0:T(8,128)}, f32[24,768]{1,0:T(8,128)}, f32[96,4096]{1,0:T(8,12...) custom-call(bf16[512,768]{1,0:T(8,128)(2,1)} %get-tuple-element.59.r, ...), custom_call_target="tpu_custom_call" | custom-call | tf_op jit(solution)/shard_map/results/pallas_call | solution.py:953

commit v6 on v5

--- a/solution.py
+++ b/solution.py
@@ -136,8 +136,8 @@
 
 def fwd_kernel(
     tok, seg, rT, pT, ln1, wqkv, wattn, ln2, wrT, cmT, cot, cos, sin,
-    q_out, k_out, v_out, pw_out, att_out, n1_out, res_out, meta, send_out, g_rows,
-    proj, bias, wcat, rb, pb, n2b, n2l, gl, tg, onehot, g_out, send_sem, recv_sem, pw, send, pw_sem, row_sem,
+    q_out, k_out, v_out, pw_out, att_out, n1_out, res_out, meta, send_out, g_rows, gate_row,
+    bias, wcat, rb, pb, n2b, n2l, tg, onehot, g_out, send_sem, recv_sem, pw, send, pw_sem, row_sem,
 ):
     length, width = tok.near.shape
     capacity = length // 2
@@ -180,33 +180,30 @@
         (copies[r] if r else own_rows).start()
     tok = tok.wait()
 
-    @pl.loop(0, length // 64)
+    @pl.loop(0, length // 256)
     def _(i):
-        rows = tile(i, 64)
+        rows = tile(i, 256)
         x = tok[rows].astype(F32)
         r = lax.rsqrt(row_mean(x * x) + EPS)
         n1[rows] = (x * r * ln1[0:1]).astype(BF16)
 
     n1_out.start()
     wqkv, cos, sin = wqkv.wait(), cos.wait(), sin.wait()
-    for kind, (dst, done) in enumerate(((q, q_out), (k, k_out), (v, v_out))):
-
-        @pl.loop(0, width // 256)
-        def _(j):
+
+    @pl.loop(0, width // 256)
+    def _(j):
+        for kind, dst in enumerate((q, k, v)):
             cols = pl.ds(pl.multiple_of(kind * width + j * 256, 256), 256)
-            proj[...] = dot(n1[...], wqkv[:, cols])
-
-            @pl.loop(0, length // 128)
-            def _(i):
-                rows = tile(i, 128)
-                for part in range(2):
-                    x = proj[rows, part * 128 : part * 128 + 128]
-                    if kind < 2:
-                        x = rotate(x, cos[rows], sin[rows])
-                    if kind == 0:
-                        x = x * 0.125
-                    dst[rows, pl.ds(pl.multiple_of(j * 256 + part * 128, 128), 128)] = x.astype(BF16)
-
+            both = dot(n1[...], wqkv[:, cols])
+            for part in range(2):
+                x = both[:, part * 128 : part * 128 + 128]
+                if kind < 2:
+                    x = rotate(x, cos[...], sin[...])
+                if kind == 0:
+                    x = x * 0.125
+                dst[:, pl.ds(pl.multiple_of(j * 256 + part * 128, 128), 128)] = x.astype(BF16)
+
+    for done in (q_out, k_out, v_out):
         done.start()
 
     seg_f = seg[...].astype(F32)
@@ -226,8 +223,7 @@
         at = (pl.ds(2 * j, 2), slice(b * block, (b + 1) * block), slice(0, (b + 1) * block))
         return pltpu.make_async_copy(pw.at[at], pw_out.at[at], pw_sem.at[j, b])
 
-    @pl.loop(0, width // 128)
-    def _(j):
+    def heads(j):
         cols = tile(j, 128)
         for b in range(2):
             rows = slice(b * block, (b + 1) * block)
@@ -245,19 +241,21 @@
             att[rows, cols] = acc.astype(BF16)
             weights_copy(j, b).start()
 
+    @pl.loop(0, width // 256)
+    def _(jj):
+        heads(2 * jj)
+        heads(2 * jj + 1)
+
     att_out.start()
     wattn = wattn.wait()
 
-    @pl.loop(0, width // 256)
-    def _(j):
-        cols = tile(j, 256)
-        res[:, cols] = tok[:, cols].astype(F32) + dot(att[...], wattn[:, cols])
+    res[...] = tok[...].astype(F32) + dot(att[...], wattn[...])
 
     res_out.start()
 
-    @pl.loop(0, length // 64)
+    @pl.loop(0, length // 256)
     def _(i):
-        rows = tile(i, 64)
+        rows = tile(i, 256)
         x = res[rows]
         n2 = x * lax.rsqrt(row_mean(x * x) + EPS) * ln2[1:2]
         high = n2.astype(BF16)
@@ -304,23 +302,16 @@
         for n, value in enumerate(values):
             out = jnp.where(lane == n + 2, value, out)
         meta[rows] = out
-        for kk in range(2):
-            g_high = gates[kk].astype(BF16).astype(F32)
-            both = jnp.where(lane == 0, g_high, jnp.where(lane == 1, gates[kk] - g_high, 0.0))
-            gl[pl.ds(pl.multiple_of(kk * length + i * 128, 128), 128)] = both.astype(BF16)
 
     @pl.loop(0, experts)
     def _(e):
         owner = flip(lax.axis_index("expert"), 1)
         owner = jnp.where(e % 2 == 1, owner, lax.axis_index("expert"))
         owner = jnp.where(e // 2 == 1, flip(owner, 2), owner)
-        s_id = (lax.broadcasted_iota(jnp.int32, (capacity, length), 0) + owner * capacity).astype(F32)
-        gate = jnp.zeros((capacity, 128), F32)
-        for kk in range(2):
-            here = (pb[kk : kk + 1] == s_id).astype(F32).astype(BF16)
-            gate = gate + dot(here, gl[kk * length : (kk + 1) * length])
-        send[e, :, 0:width] = dot(onehot[tile(e, capacity)], n2b[...]).astype(BF16)
-        send[e, :, width : width + 128] = gate.astype(BF16)
+        slot = (lax.broadcasted_iota(jnp.int32, (length, capacity), 1) + owner * capacity).astype(F32)
+        gate = jnp.where(meta[:, 0:1] == slot, meta[:, 2:3], jnp.where(meta[:, 1:2] == slot, meta[:, 3:4], 0.0))
+        gate_row[e] = jnp.broadcast_to(jnp.sum(gate, axis=0, keepdims=True), (8, capacity))
+        send[e] = dot(onehot[tile(e, capacity)], n2b[...]).astype(BF16)
         pltpu.make_async_copy(send.at[e], send_out.at[e], row_sem.at[e]).start()
 
     for ref in (q_out, k_out, v_out, att_out, n1_out, res_out):
@@ -340,8 +331,9 @@
         c.wait()
 
 
-def expert_kernel(stages, xs, g_rows, win, wout, *refs):
-    f_out, d_back, go_out = refs[:3]
+def expert_kernel(stages, xs, g_rows, win, wout, gate_row, *refs):
+    f_out, d_back, go_out, dot_back = refs[:4]
+    refs = refs[:3] + refs[4:]
     f_rows, go = f_out.near, go_out.near
     if stages:
         late_out, early_out = refs[3:5]
@@ -356,8 +348,8 @@
     if stages:
         gi, p_first, in_send, in_recv, e_send, e_recv = refs[:6]
         refs = refs[6:]
-    x_send, x_recv, d_send, d_recv, own_sem = refs
-    groups, capacity, wide = xs.shape
+    x_send, x_recv, d_send, d_recv, own_sem, gates, dot_row, r_send, r_recv, s_send, s_recv = refs
+    groups, capacity, _ = xs.shape
     hidden, width = wout.near.shape[1:]
     tiles, rows_all, ft = hid.shape
     slabs = go.shape[0]
@@ -366,17 +358,21 @@
 
     greet([s[0] for s in stages], groups - 1)
     copies = exchange(xs, xr, x_send, x_recv)
-    for c in copies.values():
+    row_copies = exchange(gate_row, gates, r_send, r_recv)
+    for r, c in copies.items():
+        row_copies[r].start()
         c.start()
+    gates[0] = gate_row[0]
     own_x = pltpu.make_async_copy(xs.at[0], xr.at[0], own_sem.at[0])
     own_x.start()
     for ref in (g_rows, win, wout):
         ref.start()
 
     def gated(r):
-        pair = xr[r, :, width:wide].astype(F32)
-        lane = lax.broadcasted_iota(jnp.int32, pair.shape, 1)
-        gate = jnp.sum(jnp.where(lane < 2, pair, 0.0), axis=-1, keepdims=True)
+        if r:
+            row_copies[r].wait()
+            copies[r].wait()
+        gate = jnp.transpose(jnp.broadcast_to(gates[r, 0:1], (128, capacity)))[:, 0:1]
         dy[r * capacity : (r + 1) * capacity] = (g_rows[r].astype(F32) * gate).astype(BF16)
 
     def cols_of(f):
@@ -385,7 +381,7 @@
     def work(f, part):
         gate_cols, up_cols = cols_of(f)
         rows = slice(part * near, (part + 1) * near)
-        x = xr[2 * part : 2 * part + 2, :, 0:width].reshape(near, width)
+        x = xr[2 * part : 2 * part + 2].reshape(near, width)
         gate = dot(x, win[0, :, gate_cols])
         up = dot(x, win[0, :, up_cols])
         dh = dot_nt(dy[rows], wout[0, gate_cols, :])
@@ -422,7 +418,6 @@
 
     own_x.wait()
     g_rows = g_rows.wait()
-    copies[1].wait()
     gated(0)
     gated(1)
 
@@ -432,10 +427,8 @@
     def _(f):
         work(f, 0)
 
-    copies[3].wait()
-    copies[2].wait()
+    gated(3)
     gated(2)
-    gated(3)
 
     for part in range(2):
 
@@ -443,7 +436,7 @@
         def _(f):
             work(f, 1)
             for p in range(2):
-                d = dot_tn(xr[:, :, 0:width].reshape(rows_all, width), dgu[f, :, p * ft : (p + 1) * ft])
+                d = dot_tn(xr[...].reshape(rows_all, width), dgu[f, :, p * ft : (p + 1) * ft])
                 if not stages:
                     gi[2 * f + p] = d.astype(BF16)
                     continue
@@ -454,18 +447,22 @@
                 in_copy(part, f, p)[0].start()
 
     d_copies = exchange(d_out, d_back, d_send, d_recv)
+    dot_copies = exchange(dot_row, dot_back, s_send, s_recv)
     own_d = pltpu.make_async_copy(d_out.at[0], d_back.at[0], own_sem.at[1])
     for r in range(groups - 1, -1, -1):
         rows = slice(r * capacity, (r + 1) * capacity)
         y = f_acc[rows]
         f_rows[r] = y.astype(BF16)
         dots = jnp.sum(y * g_rows[r].astype(F32), axis=-1, keepdims=True)
-        high = dots.astype(BF16).astype(F32)
-        lane = lax.broadcasted_iota(jnp.int32, (capacity, 128), 1)
-        extra = jnp.where(lane == 0, high, jnp.where(lane == 1, dots - high, 0.0)).astype(BF16)
-        d_out[r, :, 0:width] = d_acc[rows].astype(BF16)
-        d_out[r, :, width:wide] = extra
-        (d_copies[r] if r else own_d).start()
+        as_rows = jnp.transpose(jnp.broadcast_to(dots, (capacity, 128)))[0:8]
+        d_out[r] = d_acc[rows].astype(BF16)
+        if r:
+            dot_row[r] = as_rows
+            dot_copies[r].start()
+            d_copies[r].start()
+        else:
+            dot_back[0] = as_rows
+            own_d.start()
     f_out.start()
 
     for c in range(slabs):
@@ -505,7 +502,8 @@
     f_out.wait()
     go_out.wait()
     own_d.wait()
-    for c in d_copies.values():
+    for r, c in d_copies.items():
+        dot_copies[r].wait()
         c.wait()
 
 
@@ -558,9 +556,9 @@
 
 def bwd_kernel(plan, *refs):
     (
-        tok, cot, res, meta, rT, f_rows, d_back, q, k, v, pw_far, att, n1, ln1, wqkv, wattn, ln2, wrT, cmT, cvT, cos, sin,
-    ) = refs[:22]
-    refs = refs[22:]
+        tok, cot, res, meta, dot_back, rT, f_rows, d_back, q, k, v, pw_far, att, n1, ln1, wqkv, wattn, ln2, wrT, cmT, cvT, cos, sin,
+    ) = refs[:23]
+    refs = refs[23:]
     if plan:
         stages, order = plan
         p_early, p_late, p_out, out_s, igrad_s, d_qkv, d_attn, d_small, d_ln, g_in_s, g_out_s = refs[:11]
@@ -709,10 +707,13 @@
     @pl.loop(0, length // 256)
     def _(i):
         rows = tile(i, 256)
-        first, second = (c.astype(F32).astype(BF16) for c in chosen(rows, 256))
-        dsn[rows] = dot(first + second, d_back[:, :, 0:width].reshape(slots, width))
-        for n, c in enumerate((first, second)):
-            dots[n, rows] = dot(c, d_back[:, :, width : width + 128].reshape(slots, 128))
+        masks = chosen(rows, 256)
+        either = (masks[0] | masks[1]).astype(F32).astype(BF16)
+        dsn[rows] = dot(either, d_back[...].reshape(slots, width))
+        line = jnp.concatenate([dot_back[r, 0:1] for r in range(experts)], axis=1)
+        lane = lax.broadcasted_iota(jnp.int32, (256, 128), 1)
+        for n, c in enumerate(masks):
+            dots[n, rows] = jnp.where(lane == 0, jnp.sum(jnp.where(c, line, 0.0), axis=-1, keepdims=True), 0.0)
 
     cot, res = cot.wait(), res.wait()
     w_high = wcat[...].astype(BF16)
@@ -742,7 +743,7 @@
         for j in range(2):
             special = jnp.where(lane == 6 + j, shares[j][0] * gn2 + shares[j][1] * gcv[j], special)
         dg = [
-            jnp.sum(h * special + jnp.where(lane < 2, dots[n, rows], 0.0), axis=-1, keepdims=True)
+            jnp.sum(h * special + dots[n, rows], axis=-1, keepdims=True)
             for n, h in enumerate(hits)
         ]
         mean_dg = g0 * dg[0] + g1 * dg[1]
@@ -982,18 +983,19 @@
     ln1 = ln2 = gains
     peers = experts - 1
 
-    q, k, v, pw, att, n1, res, meta, send, g_rows = call(
+    q, k, v, pw, att, n1, res, meta, send, g_rows, gate_row = call(
         fwd_kernel,
         [
             shape(length, width), shape(length, width), shape(length, width), shape(heads, length, length),
             shape(length, width), shape(length, width), shape(length, width, dtype=F32),
-            shape(length, 128, dtype=F32), shape(experts, capacity, width + 128), shape(experts, capacity, width),
+            shape(length, 128, dtype=F32), shape(experts, capacity, width), shape(experts, capacity, width),
+            shape(experts, 8, capacity, dtype=F32),
         ],
         [
-            V((length, 256), F32), V((length, length), F32), V((128, width), F32), V((3, length, 128), F32),
-            V((128, length), F32), V((length, width), BF16), V((length, width), BF16), V((2 * length, 128), BF16),
+            V((length, length), F32), V((128, width), F32), V((3, length, 128), F32),
+            V((128, length), F32), V((length, width), BF16), V((length, width), BF16),
             V((length, 128), F32), V((slots, length), BF16), V((experts, capacity, width), BF16),
-            DMA((peers,)), DMA((peers,)), V((heads, length, length), BF16), V((experts, capacity, width + 128), BF16),
+            DMA((peers,)), DMA((peers,)), V((heads, length, length), BF16), V((experts, capacity, width), BF16),
             DMA((width // 128, 2)), DMA((experts + 1,)),
         ],
         (tokens, segments, rT, pT, ln1, w_qkv, w_attn, ln2, wrT, cmT, cotangent, cos, sin),
@@ -1010,27 +1012,30 @@
     def part_of(s, n):
         return (s[0], s[1] // n, s[2])
 
-    wide = width + 128
     late = (tiles, width // 2, ft)
     early = (tiles, width // 4, ft)
-    f_rows, d_back, g_out, *g_in = call(
+    f_rows, d_back, g_out, dot_back, *g_in = call(
         functools.partial(expert_kernel, stages),
-        [shape(experts, capacity, width), shape(experts, capacity, wide), shape(*slab_out)]
+        [
+            shape(experts, capacity, width), shape(experts, capacity, width), shape(*slab_out),
+            shape(experts, 8, capacity, dtype=F32),
+        ]
         + ([shape(*late), shape(*early)] if within else [shape(*slab_in)]),
         [
-            V((experts, capacity, wide), BF16), V((slots, width), BF16), V((tiles, slots, ft), BF16),
+            V((experts, capacity, width), BF16), V((slots, width), BF16), V((tiles, slots, ft), BF16),
             V((tiles, slots, 2 * ft), BF16), V((slots, width), F32), V((slots, width), F32),
-            V((experts, capacity, wide), BF16),
+            V((experts, capacity, width), BF16),
         ]
         + ([V(slab_in, BF16), V(late, BF16)] + [DMA((2 * tiles,))] * 2 + [DMA((tiles,))] * 2 if within else [])
         + [DMA((peers,))] * 4
-        + [DMA((2,))],
-        (send, g_rows, expert_in, expert_out),
-        "experts", 1, (0, 5), (1, 2, 3, 4, 6) + ((7, 8) if within else (7,)),
+        + [DMA((2,)), V((experts, 8, capacity), F32), V((experts, 8, capacity), F32)]
+        + [DMA((peers,))] * 4,
+        (send, g_rows, expert_in, expert_out, gate_row),
+        "experts", 1, (0, 6), (1, 2, 3, 5, 7) + ((9, 10) if within else (9,)),
     )
 
     args = (
-        tokens, cotangent, res, meta, rT, f_rows, d_back, q, k, v, pw, att, n1, ln1, w_qkv, w_attn, ln2, wrT, cmT, cvT,
+        tokens, cotangent, res, meta, dot_back, rT, f_rows, d_back, q, k, v, pw, att, n1, ln1, w_qkv, w_attn, ln2, wrT, cmT, cvT,
         cos, sin,
     )
     n_all = n_dp * experts
@@ -1060,9 +1065,9 @@
             scratch += [V((2 * width >> s, cols // 2), BF16) for s in range(6)] + [DMA((5,)), DMA((5,))]
     plan = (stages, order) if within else ()
     n = len(args)
-    staged = (0, 1, 2, 6, 7, 8, 9, 11, 12, 14, 15, 20, 21) + tuple(range(22, n)) + (n, n + 1)
+    staged = (0, 1, 2, 7, 8, 9, 10, 12, 13, 15, 16, 21, 22) + tuple(range(23, n)) + (n, n + 1)
     staged += (n + 6, n + 7) if within else ()
-    done = call(functools.partial(bwd_kernel, plan), outs, scratch, args, "backward", 2, (5, 10), staged)
+    done = call(functools.partial(bwd_kernel, plan), outs, scratch, args, "backward", 2, (6, 11), staged)
     out, igrad, d_qkv, d_attn, small = done[:5]
     if within:
         out, igrad, d_qkv, d_attn, g_in, g_out, router, mix, vec, ln_one, ln_two = final(

time: 191 us -> 184 us (0.963)
  Pallas kernels: 188 us -> 180 us
    pallas_call x3, Pallas kernels: 183 us -> 176 us  [call(): pl.pallas_call(wrapped, out_shape=outs, in_specs=specs[:len(args)], out_s...]
where the time goes in v6:
time: 184 us; the launch traced here: 183 us
  Pallas kernels  180 us (98%)
    pallas_call x3, Pallas kernels, call(): pl.pallas_call(wrapped, out_shape=outs, in_specs=specs[:len(args)], out_s...  176 us
    pallas_call x1, Pallas kernels, final(): pl.pallas_call(functools.partial(final_kernel, len(big)), out_shape=[jax....  4.8 us

profile of v6, /device:TPU:0, one launch (start us, length us, event | category | flops | bytes accessed | tf_op | source)
XLA Modules:
  0.0 183.3 jit_solution(4558320354160869570)
XLA Ops:
  0.6 0.7 stack.9
  1.3 0.7 stack.10
  2.0 0.6 pad_maximum_fusion.refs_4_.refs_7_.refs_14_.refs_17_
  2.6 25.6 %attention.1 = (bf16[512,768]{1,0:T(8,128)(2,1)}, bf16[512,768]{1,0:T(8,128)(2,1)}, bf16[512,768]{1,0:T(8,128)(2,1)}, bf16[12,512,512]{2,1,0:T(8,128)(2,1)}, bf1...) custom-call(bf16[512,768]{1,0:T(8,128)(2,1)} %refs_0_.3, ...), custom_call_target="tpu_custom_call" | custom-call | tf_op jit(solution)/shard_map/attention/pallas_call | solution.py:916
  28.3 72.3 %experts.1 = (bf16[4,256,768]{2,1,0:T(8,128)(2,1)}, bf16[4,256,768]{2,1,0:T(8,128)(2,1)}, bf16[2,2048,384]{2,1,0:T(8,128)(2,1)}, f32[4,8,256]{2,1,0:T(8,128)}, b...) custom-call(bf16[4,256,768]{2,1,0:T(8,128)(2,1)} %get-tuple-element.48.refs_0_, ...), custom_call_target="tpu_custom_call" | custom-call | tf_op jit(solution)/shard_map/experts/pallas_call | solution.py:916
  100.6 77.7 %backward.1 = (bf16[512,768]{1,0:T(8,128)(2,1)}, bf16[512,768]{1,0:T(8,128)(2,1)}, f32[24,2304]{1,0:T(8,128)}, f32[24,768]{1,0:T(8,128)}, f32[24,128]{1,0:T(8,12...) custom-call(bf16[512,768]{1,0:T(8,128)(2,1)} %refs_0_.3, bf16[512,768]{1,0:T(8,128)(2,1)} %refs_1_.3, ...), custom_call_target="tpu_custom_call" | custom-call | tf_op jit(solution)/shard_map/backward/pallas_call | solution.py:916
  178.3 4.8 %results.1 = (bf16[512,768]{1,0:T(8,128)(2,1)}, bf16[512,768]{1,0:T(8,128)(2,1)}, f32[24,2304]{1,0:T(8,128)}, f32[24,768]{1,0:T(8,128)}, f32[96,4096]{1,0:T(8,12...) custom-call(bf16[512,768]{1,0:T(8,128)(2,1)} %get-tuple-element.63.r, ...), custom_call_target="tpu_custom_call" | custom-call | tf_op jit(solution)/shard_map/results/pallas_call | solution.py:954

commit v7 on v6

--- a/solution.py
+++ b/solution.py
@@ -55,6 +55,10 @@
     return jnp.mean(x, axis=-1, keepdims=True)
 
 
+def as_row(gain):
+    return gain[...].reshape(1, gain.shape[0])
+
+
 def pick(x, lane, index):
     return jnp.sum(jnp.where(lane == index, x, 0.0), axis=-1, keepdims=True)
 
@@ -89,13 +93,14 @@
     return e
 
 
-def greet(masks, peers=0):
+def greet(masks, peers=0, wait=True):
     barrier = pltpu.get_barrier_semaphore()
     for mask in masks:
         pl.semaphore_signal(barrier, inc=1, device_id=partner(mask), device_id_type=MESH)
     for r in range(1, peers + 1):
         pl.semaphore_signal(barrier, inc=1, device_id={"expert": across(r)}, device_id_type=MESH)
-    pl.semaphore_wait(barrier, len(masks) + peers)
+    if wait:
+        pl.semaphore_wait(barrier, len(masks) + peers)
 
 
 def exchange(src, dst, send_sem, recv_sem):
@@ -135,9 +140,9 @@
 
 
 def fwd_kernel(
-    tok, seg, rT, pT, ln1, wqkv, wattn, ln2, wrT, cmT, cot, cos, sin,
-    q_out, k_out, v_out, pw_out, att_out, n1_out, res_out, meta, send_out, g_rows, gate_row,
-    bias, wcat, rb, pb, n2b, n2l, tg, onehot, g_out, send_sem, recv_sem, pw, send, pw_sem, row_sem,
+    tok, seg, rT, ln1, wqkv, wattn, ln2, cot, cos, sin,
+    q_out, k_out, v_out, pw_out, att_out, n1_out, res_out, tg, send_out, g_rows, high_out, low_out,
+    bias, rb, pb, onehot, g_out, send_sem, recv_sem, pw, send, pw_sem, row_sem,
 ):
     length, width = tok.near.shape
     capacity = length // 2
@@ -146,7 +151,8 @@
     for ref in (cot, tok, wqkv, cos, sin, wattn):
         ref.start()
     q, k, v, att, n1, res = (ref.near for ref in (q_out, k_out, v_out, att_out, n1_out, res_out))
-    greet((), experts - 1)
+    n2b, n2l = high_out.near, low_out.near
+    greet((), experts - 1, wait=False)
     for kk in range(2):
         rb[kk] = jnp.transpose(jnp.broadcast_to(rT[kk : kk + 1, :].astype(F32), (128, length)))
     all_lane = lax.broadcasted_iota(jnp.int32, (length, 128), 1).astype(F32)
@@ -170,6 +176,7 @@
     pb[...] = target
 
     cot = cot.wait()
+    pl.semaphore_wait(pltpu.get_barrier_semaphore(), experts - 1)
     copies = exchange(g_out, g_rows, send_sem, recv_sem)
     own_rows = pltpu.make_async_copy(g_out.at[0], g_rows.at[0], row_sem.at[experts])
     for r in range(experts - 1, -1, -1):
@@ -185,7 +192,7 @@
         rows = tile(i, 256)
         x = tok[rows].astype(F32)
         r = lax.rsqrt(row_mean(x * x) + EPS)
-        n1[rows] = (x * r * ln1[0:1]).astype(BF16)
+        n1[rows] = (x * r * as_row(ln1)).astype(BF16)
 
     n1_out.start()
     wqkv, cos, sin = wqkv.wait(), cos.wait(), sin.wait()
@@ -257,19 +264,82 @@
     def _(i):
         rows = tile(i, 256)
         x = res[rows]
-        n2 = x * lax.rsqrt(row_mean(x * x) + EPS) * ln2[1:2]
+        n2 = x * lax.rsqrt(row_mean(x * x) + EPS) * as_row(ln2)
         high = n2.astype(BF16)
         n2b[rows] = high
         n2l[rows] = (n2 - high.astype(F32)).astype(BF16)
 
+    high_out.start()
+    low_out.start()
+
+    @pl.loop(0, experts)
+    def _(e):
+        send[e] = dot(onehot[tile(e, capacity)], n2b[...]).astype(BF16)
+        pltpu.make_async_copy(send.at[e], send_out.at[e], row_sem.at[e]).start()
+
+    for ref in (q_out, k_out, v_out, att_out, n1_out, res_out, high_out, low_out):
+        ref.wait()
+
+    @pl.loop(0, width // 128)
+    def _(j):
+        for b in range(2):
+            weights_copy(j, b).wait()
+
+    @pl.loop(0, experts)
+    def _(e):
+        pltpu.make_async_copy(send.at[e], send_out.at[e], row_sem.at[e]).wait()
+
+    own_rows.wait()
+    for c in copies.values():
+        c.wait()
+
+
+def expert_kernel(stages, xs, g_rows, win, wout, n2b, n2l, tg, rT, pT, wrT, cmT, *refs):
+    f_out, d_back, go_out, dot_back, meta = refs[:5]
+    refs = refs[:3] + refs[5:]
+    f_rows, go = f_out.near, go_out.near
+    if stages:
+        late_out, early_out = refs[3:5]
+        p_late, p_early = late_out.near, early_out.near
+        refs = refs[5:]
+    else:
+        gi_out = refs[3]
+        gi = gi_out.near
+        refs = refs[4:]
+    xr, dy, hid, dgu, f_acc, d_acc, d_out = refs[:7]
+    refs = refs[7:]
+    if stages:
+        gi, p_first, in_send, in_recv, e_send, e_recv = refs[:6]
+        refs = refs[6:]
+    x_send, x_recv, d_send, d_recv, own_sem, gates, gate_row, dot_row, wcat, rb, r_send, r_recv, s_send, s_recv = refs
+    groups, capacity, _ = xs.shape
+    hidden, width = wout.near.shape[1:]
+    tiles, rows_all, ft = hid.shape
+    slabs = go.shape[0]
+    shards = 2 ** len(stages[0]) if stages else 0
+    near = rows_all // 2
+
+    greet([s[0] for s in stages], groups - 1)
+    copies = exchange(xs, xr, x_send, x_recv)
+    n2b.start()
+    n2l.start()
+    for c in copies.values():
+        c.start()
+    own_x = pltpu.make_async_copy(xs.at[0], xr.at[0], own_sem.at[0])
+    own_x.start()
+    for ref in (g_rows, win, wout):
+        ref.start()
+    n2b, n2l = n2b.wait(), n2l.wait()
+    length = n2b.shape[0]
     wcat[...] = jnp.zeros_like(wcat)
     wcat[0:8] = wrT[...]
     wcat[8:12] = cmT[...]
     w_high = wcat[...].astype(BF16)
     w_low = (wcat[...] - w_high.astype(F32)).astype(BF16)
 
-    pb[8:16] = pT[...]
-    rb[2] = jnp.transpose(jnp.concatenate([pb[8:16], jnp.zeros((120, length), F32)], axis=0))
+    for kk in range(2):
+        rb[kk] = jnp.transpose(jnp.broadcast_to(rT[kk : kk + 1, :].astype(F32), (128, length)))
+    rb[2] = jnp.transpose(jnp.concatenate([pT[...], jnp.zeros((120, length), F32)], axis=0))
 
     @pl.loop(0, length // 128)
     def _(i):
@@ -303,70 +373,16 @@
             out = jnp.where(lane == n + 2, value, out)
         meta[rows] = out
 
-    @pl.loop(0, experts)
-    def _(e):
-        owner = flip(lax.axis_index("expert"), 1)
-        owner = jnp.where(e % 2 == 1, owner, lax.axis_index("expert"))
-        owner = jnp.where(e // 2 == 1, flip(owner, 2), owner)
-        slot = (lax.broadcasted_iota(jnp.int32, (length, capacity), 1) + owner * capacity).astype(F32)
+    row_copies = exchange(gate_row, gates, r_send, r_recv)
+    for r in range(groups - 1, -1, -1):
+        slot = (lax.broadcasted_iota(jnp.int32, (length, capacity), 1) + across(r) * capacity).astype(F32)
         gate = jnp.where(meta[:, 0:1] == slot, meta[:, 2:3], jnp.where(meta[:, 1:2] == slot, meta[:, 3:4], 0.0))
-        gate_row[e] = jnp.broadcast_to(jnp.sum(gate, axis=0, keepdims=True), (8, capacity))
-        send[e] = dot(onehot[tile(e, capacity)], n2b[...]).astype(BF16)
-        pltpu.make_async_copy(send.at[e], send_out.at[e], row_sem.at[e]).start()
-
-    for ref in (q_out, k_out, v_out, att_out, n1_out, res_out):
-        ref.wait()
-
-    @pl.loop(0, width // 128)
-    def _(j):
-        for b in range(2):
-            weights_copy(j, b).wait()
-
-    @pl.loop(0, experts)
-    def _(e):
-        pltpu.make_async_copy(send.at[e], send_out.at[e], row_sem.at[e]).wait()
-
-    own_rows.wait()
-    for c in copies.values():
-        c.wait()
-
-
-def expert_kernel(stages, xs, g_rows, win, wout, gate_row, *refs):
-    f_out, d_back, go_out, dot_back = refs[:4]
-    refs = refs[:3] + refs[4:]
-    f_rows, go = f_out.near, go_out.near
-    if stages:
-        late_out, early_out = refs[3:5]
-        p_late, p_early = late_out.near, early_out.near
-        refs = refs[5:]
-    else:
-        gi_out = refs[3]
-        gi = gi_out.near
-        refs = refs[4:]
-    xr, dy, hid, dgu, f_acc, d_acc, d_out = refs[:7]
-    refs = refs[7:]
-    if stages:
-        gi, p_first, in_send, in_recv, e_send, e_recv = refs[:6]
-        refs = refs[6:]
-    x_send, x_recv, d_send, d_recv, own_sem, gates, dot_row, r_send, r_recv, s_send, s_recv = refs
-    groups, capacity, _ = xs.shape
-    hidden, width = wout.near.shape[1:]
-    tiles, rows_all, ft = hid.shape
-    slabs = go.shape[0]
-    shards = 2 ** len(stages[0]) if stages else 0
-    near = rows_all // 2
-
-    greet([s[0] for s in stages], groups - 1)
-    copies = exchange(xs, xr, x_send, x_recv)
-    row_copies = exchange(gate_row, gates, r_send, r_recv)
-    for r, c in copies.items():
-        row_copies[r].start()
-        c.start()
-    gates[0] = gate_row[0]
-    own_x = pltpu.make_async_copy(xs.at[0], xr.at[0], own_sem.at[0])
-    own_x.start()
-    for ref in (g_rows, win, wout):
-        ref.start()
+        line = jnp.broadcast_to(jnp.sum(gate, axis=0, keepdims=True), (8, capacity))
+        if r:
+            gate_row[r] = line
+            row_copies[r].start()
+        else:
+            gates[0] = line
 
     def gated(r):
         if r:
@@ -393,8 +409,12 @@
         hid[f, rows] = h
         dgu[f, rows, 0:ft] = da
         dgu[f, rows, ft : 2 * ft] = db
-        y = dot(h, wout[0, gate_cols, :])
-        d = dot_nt(da, win[0, :, gate_cols]) + dot_nt(db, win[0, :, up_cols])
+
+    def gather(f, part):
+        gate_cols, up_cols = cols_of(f)
+        rows = slice(part * near, (part + 1) * near)
+        y = dot(hid[f, rows], wout[0, gate_cols, :])
+        d = dot_nt(dgu[f, rows, 0:ft], win[0, :, gate_cols]) + dot_nt(dgu[f, rows, ft : 2 * ft], win[0, :, up_cols])
 
         @pl.when(f == 0)
         def _():
@@ -426,6 +446,7 @@
     @pl.loop(0, tiles)
     def _(f):
         work(f, 0)
+        gather(f, 0)
 
     gated(3)
     gated(2)
@@ -445,6 +466,7 @@
                     at = place_of(j, [m for _, m in stages[p]]) * size
                     gi[2 * f + p, at : at + size] = d[j * size : (j + 1) * size].astype(BF16)
                 in_copy(part, f, p)[0].start()
+            gather(f, 1)
 
     d_copies = exchange(d_out, d_back, d_send, d_recv)
     dot_copies = exchange(dot_row, dot_back, s_send, s_recv)
@@ -632,7 +654,10 @@
             if s < 2:
                 out_copy(i, s + 1).start()
 
-        attn_slab, q0, q1, q2a, q2b, ln_slab = (Slab(order, r) for r in slab_refs)
+        turned = order[:3] + (order[4], order[3])
+        attn_slab, q0, q1, q2a, q2b, ln_slab = (
+            Slab(turned if n == 4 else order, r) for n, r in enumerate(slab_refs)
+        )
 
         def columns(ref, at):
             return ((ref, at), (ref, at + 128))
@@ -644,33 +669,29 @@
         q2b.out = [columns(d_qkv, 2 * width + 512)]
         ln_slab.out = [((d_ln, 0), (d_small, 0))]
 
-        for i in (1, 2):
-            in_copy(i, 1).start()
-        out_copy(0, 0).start()
-        in_copy(6, 0).start()
-        in_copy(3, 1).start()
+        for i, n in ((4, 0), (5, 0), (0, 1), (3, 1), (1, 1), (6, 0)):
+            in_copy(i, n).start()
         out_copy(1, 0).start()
         acts = {
-            "token": [(out_start, in_copy, 5, 0), (in_done, 1, 1)],
-            "attn": [
-                (out_start, in_copy, 0, 1), (out_start, in_copy, 4, 0), (attn_slab.start,), (in_done, 6, 0),
-                (in_done, 2, 1),
+            "token": [(in_done, 4, 0), (in_done, 5, 0), (in_done, 0, 1)],
+            "attn": [(out_start, out_copy, 0, 0), (attn_slab.start,), (in_done, 3, 1)],
+            "part0": [
+                (out_start, out_copy, 2, 0), (out_start, in_copy, 2, 1), (q0.start,), (in_done, 1, 1),
+                (attn_slab.done, 0), (in_done, 6, 0), (out_done, 1, 0),
             ],
-            "part0": [(q0.start,), (in_done, 3, 1), (attn_slab.done, 0)],
-            "part1": [
-                (out_start, in_copy, 7, 0), (q1.start,), (in_done, 0, 1), (out_done, 0, 0), (in_done, 4, 0),
-                (q0.done, 0),
+            "part1": [(out_start, in_copy, 7, 0), (q1.start,), (in_done, 4, 1), (q0.done, 0), (in_done, 5, 1)],
+            "part2": [
+                (q2a.start,), (q2b.start,), (attn_slab.done, 1), (q1.done, 0), (in_done, 2, 1), (out_done, 0, 0),
             ],
-            "part2": [(q2a.start,), (q2b.start,), (in_done, 6, 1), (q1.done, 0), (attn_slab.done, 1)],
-            "norm": [(q2a.done, 0), (q2b.done, 0), (q0.done, 1), (out_done, 0, 1)],
-            "input": [(ln_slab.start,), (in_done, 4, 1)],
+            "norm": [(out_done, 1, 1), (q2a.done, 0), (in_done, 6, 1), (q2b.done, 0), (q0.done, 1)],
+            "input": [(ln_slab.start,)],
             "output": [
-                (out_done, 1, 0), (ln_slab.done, 0), (q1.done, 1), (in_done, 5, 0), (q2a.done, 1), (out_done, 0, 2),
-                (in_done, 7, 0), (q2b.done, 1), (ln_slab.done, 1), (out_done, 1, 1), (attn_slab.done, 2),
-                (in_done, 5, 1), (q0.done, 2), (in_done, 7, 1), (q1.done, 2), (q2a.done, 2), (q2b.done, 2),
-                (attn_slab.done, 3), (ln_slab.done, 2), (q0.done, 3), (out_done, 1, 2), (q1.done, 3), (q2a.done, 3),
-                (q2b.done, 3), (attn_slab.done, 4), (ln_slab.done, 3), (q0.done, 4), (q1.done, 4), (q2a.done, 4),
-                (q2b.done, 4), (ln_slab.done, 4),
+                (out_done, 0, 1), (q1.done, 1), (ln_slab.done, 0), (out_done, 2, 0), (out_done, 1, 2), (q2a.done, 1),
+                (in_done, 7, 0), (q2b.done, 1), (out_done, 0, 2), (ln_slab.done, 1), (attn_slab.done, 2),
+                (out_done, 2, 1), (q0.done, 2), (in_done, 7, 1), (g_in_s.start,), (attn_slab.done, 3), (q1.done, 2),
+                (q2a.done, 2), (out_done, 2, 2), (g_out_s.start,), (q0.done, 3), (q2b.done, 2), (attn_slab.done, 4),
+                (ln_slab.done, 2), (q1.done, 3), (q2a.done, 3), (q0.done, 4), (q2b.done, 3), (ln_slab.done, 3),
+                (q1.done, 4), (q2b.done, 4), (q2a.done, 4), (ln_slab.done, 4),
             ],
         }
     for c in f_copies.values():
@@ -732,7 +753,7 @@
         x = res[rows]
         r2 = lax.rsqrt(row_mean(x * x) + EPS)
         xr = x * r2
-        n2 = xr * ln2[1:2]
+        n2 = xr * as_row(ln2)
         n2b[rows] = n2.astype(BF16)
         cv = (cvT[0:1, :], cvT[1:2, :])
         fk0[rows] = x + keep * n2 + (cg[0] * shares[0][1]) * cv[0] + (cg[1] * shares[1][1]) * cv[1]
@@ -760,7 +781,7 @@
         dcat[rows, 128:256] = vecs.astype(BF16)
         dn2 = keep * g + dsn[rows] + dot(cat.astype(BF16), w_high)
         lnacc[0:8] += jnp.sum((dn2 * xr).reshape(8, 8, width), axis=0)
-        dn = dn2 * ln2[1:2]
+        dn = dn2 * as_row(ln2)
         dr = g + r2 * dn - xr * (r2 * r2) * row_mean(dn * x)
         dres[rows] = dr
         dbr[rows] = dr.astype(BF16)
@@ -844,7 +865,7 @@
         r1 = lax.rsqrt(row_mean(x * x) + EPS)
         xr = x * r1
         d = dsn[rows]
-        dn = d * ln1[0:1]
+        dn = d * as_row(ln1)
         lnacc[8:16] += jnp.sum((d * xr).reshape(8, 8, width), axis=0)
         igrad[rows] = (dres[rows] + r1 * dn - xr * (r1 * r1) * row_mean(dn * x)).astype(BF16)
 
@@ -875,8 +896,6 @@
     out_s.wait()
     igrad_s.wait()
     if plan:
-        g_in_s.start()
-        g_out_s.start()
         g_in_s.wait()
         g_out_s.wait()
 
@@ -979,30 +998,27 @@
     cos, sin = (jnp.asarray(t) for t in rotary_tables(length))
     rT, pT = routes.T, prev_logits.T
     wrT, cmT, cvT = w_router.T, const_mix.T, const_vec.T
-    gains = jnp.stack([ln1_gain, ln2_gain])
-    ln1 = ln2 = gains
+    ln1, ln2 = ln1_gain, ln2_gain
     peers = experts - 1
 
-    q, k, v, pw, att, n1, res, meta, send, g_rows, gate_row = call(
+    q, k, v, pw, att, n1, res, target, send, g_rows, high, low = call(
         fwd_kernel,
         [
             shape(length, width), shape(length, width), shape(length, width), shape(heads, length, length),
             shape(length, width), shape(length, width), shape(length, width, dtype=F32),
             shape(length, 128, dtype=F32), shape(experts, capacity, width), shape(experts, capacity, width),
-            shape(experts, 8, capacity, dtype=F32),
+            shape(length, width), shape(length, width),
         ],
         [
-            V((length, length), F32), V((128, width), F32), V((3, length, 128), F32),
-            V((128, length), F32), V((length, width), BF16), V((length, width), BF16),
-            V((length, 128), F32), V((slots, length), BF16), V((experts, capacity, width), BF16),
+            V((length, length), F32), V((3, length, 128), F32), V((128, length), F32), V((slots, length), BF16), V((experts, capacity, width), BF16),
             DMA((peers,)), DMA((peers,)), V((heads, length, length), BF16), V((experts, capacity, width), BF16),
             DMA((width // 128, 2)), DMA((experts + 1,)),
         ],
-        (tokens, segments, rT, pT, ln1, w_qkv, w_attn, ln2, wrT, cmT, cotangent, cos, sin),
-        "attention", 0, (16, 21, 22), (0, 5, 6, 10, 11, 12, 13, 14, 15, 17, 18, 19),
+        (tokens, segments, rT, ln1, w_qkv, w_attn, ln2, cotangent, cos, sin),
+        "attention", 0, (13, 18, 19), (0, 4, 5, 7, 8, 9, 10, 11, 12, 14, 15, 16, 20, 21),
     )
 
-    tiles, slabs = 4, 2
+    tiles, slabs = 4, 3
     ft = hidden // tiles
     within = n_dp == 8 and experts == 4
     stages = ((("dp", 1), ("dp", 2), ("dp", 4)), (("dp", 2), ("dp", 1), ("dp", 4))) if within else ()
@@ -1014,11 +1030,11 @@
 
     late = (tiles, width // 2, ft)
     early = (tiles, width // 4, ft)
-    f_rows, d_back, g_out, dot_back, *g_in = call(
+    f_rows, d_back, g_out, dot_back, meta, *g_in = call(
         functools.partial(expert_kernel, stages),
         [
             shape(experts, capacity, width), shape(experts, capacity, width), shape(*slab_out),
-            shape(experts, 8, capacity, dtype=F32),
+            shape(experts, 8, capacity, dtype=F32), shape(length, 128, dtype=F32),
         ]
         + ([shape(*late), shape(*early)] if within else [shape(*slab_in)]),
         [
@@ -1028,10 +1044,12 @@
         ]
         + ([V(slab_in, BF16), V(late, BF16)] + [DMA((2 * tiles,))] * 2 + [DMA((tiles,))] * 2 if within else [])
         + [DMA((peers,))] * 4
-        + [DMA((2,)), V((experts, 8, capacity), F32), V((experts, 8, capacity), F32)]
+        + [DMA((2,))]
+        + [V((experts, 8, capacity), F32)] * 3
+        + [V((128, width), F32), V((3, length, 128), F32)]
         + [DMA((peers,))] * 4,
-        (send, g_rows, expert_in, expert_out, gate_row),
-        "experts", 1, (0, 6), (1, 2, 3, 5, 7) + ((9, 10) if within else (9,)),
+        (send, g_rows, expert_in, expert_out, high, low, target, rT, pT, wrT, cmT),
+        "experts", 1, (0, 12), (1, 2, 3, 4, 5, 11, 13) + ((16, 17) if within else (16,)),
     )
 
     args = (

time: 184 us -> 176 us (0.957)
  Pallas kernels: 180 us -> 175 us
    pallas_call x3, Pallas kernels: 176 us -> 170 us  [call(): pl.pallas_call(wrapped, out_shape=outs, in_specs=specs[:len(args)], out_s...]
where the time goes in v7:
time: 176 us
  Pallas kernels  175 us (99%)
    pallas_call x3, Pallas kernels, call(): pl.pallas_call(wrapped, out_shape=outs, in_specs=specs[:len(args)], out_s...  170 us
    pallas_call x1, Pallas kernels, final(): pl.pallas_call(functools.partial(final_kernel, len(big)), out_shape=[jax....  4.8 us

profile of v7, /device:TPU:0, one launch (start us, length us, event | category | flops | bytes accessed | tf_op | source)
XLA Modules:
  0.0 175.6 jit_solution(16707620676778121083)
XLA Ops:
  0.6 24.3 %attention.1 = (bf16[512,768]{1,0:T(8,128)(2,1)}, bf16[512,768]{1,0:T(8,128)(2,1)}, bf16[512,768]{1,0:T(8,128)(2,1)}, bf16[12,512,512]{2,1,0:T(8,128)(2,1)}, bf1...) custom-call(bf16[512,768]{1,0:T(8,128)(2,1)} %refs_0_.3, ...), custom_call_target="tpu_custom_call" | custom-call | tf_op jit(solution)/shard_map/attention/pallas_call | solution.py:935
  24.9 72.3 %experts.1 = (bf16[4,256,768]{2,1,0:T(8,128)(2,1)}, bf16[4,256,768]{2,1,0:T(8,128)(2,1)}, bf16[3,2048,256]{2,1,0:T(8,128)(2,1)}, f32[4,8,256]{2,1,0:T(8,128)}, f...) custom-call(bf16[4,256,768]{2,1,0:T(8,128)(2,1)} %get-tuple-element.49.refs_0_, ...), custom_call_target="tpu_custom_call" | custom-call | tf_op jit(solution)/shard_map/experts/pallas_call | solution.py:935
  97.2 73.4 %backward.1 = (bf16[512,768]{1,0:T(8,128)(2,1)}, bf16[512,768]{1,0:T(8,128)(2,1)}, f32[24,2304]{1,0:T(8,128)}, f32[24,768]{1,0:T(8,128)}, f32[24,128]{1,0:T(8,12...) custom-call(bf16[512,768]{1,0:T(8,128)(2,1)} %refs_0_.3, bf16[512,768]{1,0:T(8,128)(2,1)} %refs_1_.3, ...), custom_call_target="tpu_custom_call" | custom-call | tf_op jit(solution)/shard_map/backward/pallas_call | solution.py:935
  170.6 4.8 %results.1 = (bf16[512,768]{1,0:T(8,128)(2,1)}, bf16[512,768]{1,0:T(8,128)(2,1)}, f32[24,2304]{1,0:T(8,128)}, f32[24,768]{1,0:T(8,128)}, f32[96,4096]{1,0:T(8,12...) custom-call(bf16[512,768]{1,0:T(8,128)(2,1)} %get-tuple-element.67.r, ...), custom_call_target="tpu_custom_call" | custom-call | tf_op jit(solution)/shard_map/results/pallas_call | solution.py:973

commit v8 on v7

--- a/solution.py
+++ b/solution.py
@@ -158,19 +158,11 @@
     all_lane = lax.broadcasted_iota(jnp.int32, (length, 128), 1).astype(F32)
     count = ((rb[0] == all_lane).astype(F32) + (rb[1] == all_lane).astype(F32)).astype(BF16)
 
-    @pl.loop(0, length // 128)
-    def _(i):
-        rows = tile(i, 128)
-        lane = lax.broadcasted_iota(jnp.int32, (128, 128), 1)
-        lane_f = lane.astype(F32)
-        t_id = lax.broadcasted_iota(jnp.int32, (128, length), 0) + i * 128
-        before = (t_id > lax.broadcasted_iota(jnp.int32, (128, length), 1)).astype(F32).astype(BF16)
-        place = dot(before, count) + lane_f * float(capacity) + 1.0
-        out = jnp.zeros((128, 128), F32)
-        for kk in range(2):
-            hit = (rb[kk, rows] == lane_f) & (lane < experts)
-            out = jnp.where(lane == kk, jnp.sum(jnp.where(hit, place, 0.0), axis=-1, keepdims=True) - 1.0, out)
-        tg[rows] = out
+    t_id = lax.broadcasted_iota(jnp.int32, (length, length), 0)
+    before = (t_id > lax.broadcasted_iota(jnp.int32, (length, length), 1)).astype(F32).astype(BF16)
+    place = jnp.where(all_lane < experts, dot(before, count) + all_lane * float(capacity) + 1.0, 0.0)
+    slot = [jnp.sum(jnp.where(rb[kk] == all_lane, place, 0.0), axis=-1, keepdims=True) - 1.0 for kk in range(2)]
+    tg[...] = jnp.where(all_lane == 0, slot[0], jnp.where(all_lane == 1, slot[1], 0.0))
 
     target = jnp.transpose(tg[...])
     pb[...] = target
@@ -300,7 +292,7 @@
     f_rows, go = f_out.near, go_out.near
     if stages:
         late_out, early_out = refs[3:5]
-        p_late, p_early = late_out.near, early_out.near
+        p_late = late_out.near
         refs = refs[5:]
     else:
         gi_out = refs[3]
@@ -309,8 +301,8 @@
     xr, dy, hid, dgu, f_acc, d_acc, d_out = refs[:7]
     refs = refs[7:]
     if stages:
-        gi, p_first, in_send, in_recv, e_send, e_recv = refs[:6]
-        refs = refs[6:]
+        gi, p_first, p_early, in_send, in_recv, e_send, e_recv, e_out = refs[:8]
+        refs = refs[8:]
     x_send, x_recv, d_send, d_recv, own_sem, gates, gate_row, dot_row, wcat, rb, r_send, r_recv, s_send, s_recv = refs
     groups, capacity, _ = xs.shape
     hidden, width = wout.near.shape[1:]
@@ -341,10 +333,10 @@
         rb[kk] = jnp.transpose(jnp.broadcast_to(rT[kk : kk + 1, :].astype(F32), (128, length)))
     rb[2] = jnp.transpose(jnp.concatenate([pT[...], jnp.zeros((120, length), F32)], axis=0))
 
-    @pl.loop(0, length // 128)
+    @pl.loop(0, length // 256)
     def _(i):
-        rows = tile(i, 128)
-        lane = lax.broadcasted_iota(jnp.int32, (128, 128), 1)
+        rows = tile(i, 256)
+        lane = lax.broadcasted_iota(jnp.int32, (256, 128), 1)
         lane_f = lane.astype(F32)
         high = n2b[rows]
         mixed = dot_nt(high, w_high) + dot_nt(high, w_low) + dot_nt(n2l[rows], w_high)
@@ -387,7 +379,6 @@
     def gated(r):
         if r:
             row_copies[r].wait()
-            copies[r].wait()
         gate = jnp.transpose(jnp.broadcast_to(gates[r, 0:1], (128, capacity)))[:, 0:1]
         dy[r * capacity : (r + 1) * capacity] = (g_rows[r].astype(F32) * gate).astype(BF16)
 
@@ -431,6 +422,9 @@
         slab = 2 * f + p
         return half_copy(gi.at[slab], dst, stages[p][0], width // 2, in_send.at[slab], in_recv.at[slab]), dst
 
+    def early_store(slab):
+        return pltpu.make_async_copy(p_early.at[slab], early_out.at[slab], e_out.at[slab])
+
     def early_copy(slab):
         return half_copy(
             p_first.at[slab], p_early.at[slab], stages[slab % 2][1], width // 4, e_send.at[slab], e_recv.at[slab]
@@ -440,6 +434,7 @@
     g_rows = g_rows.wait()
     gated(0)
     gated(1)
+    copies[1].wait()
 
     win, wout = win.wait(), wout.wait()
 
@@ -450,6 +445,8 @@
 
     gated(3)
     gated(2)
+    copies[3].wait()
+    copies[2].wait()
 
     for part in range(2):
 
@@ -515,9 +512,10 @@
         for slab in range(tiles):
             early_copy(slab).wait()
             half_add(p_first.at[slab], p_early.at[slab], stages[slab % 2][1], width // 4)
-        early_out.start()
+            early_store(slab).start()
         late_out.wait()
-        early_out.wait()
+        for slab in range(tiles):
+            early_store(slab).wait()
     else:
         gi_out.start()
         gi_out.wait()
@@ -673,10 +671,10 @@
             in_copy(i, n).start()
         out_copy(1, 0).start()
         acts = {
-            "token": [(in_done, 4, 0), (in_done, 5, 0), (in_done, 0, 1)],
-            "attn": [(out_start, out_copy, 0, 0), (attn_slab.start,), (in_done, 3, 1)],
+            "token": [(out_start, out_copy, 0, 0), (in_done, 4, 0), (in_done, 5, 0), (in_done, 0, 1)],
+            "attn": [(attn_slab.start,), (in_done, 3, 1)],
             "part0": [
-                (out_start, out_copy, 2, 0), (out_start, in_copy, 2, 1), (q0.start,), (in_done, 1, 1),
+                (out_start, in_copy, 2, 1), (q0.start,), (in_done, 1, 1), (out_start, out_copy, 2, 0),
                 (attn_slab.done, 0), (in_done, 6, 0), (out_done, 1, 0),
             ],
             "part1": [(out_start, in_copy, 7, 0), (q1.start,), (in_done, 4, 1), (q0.done, 0), (in_done, 5, 1)],
@@ -1042,14 +1040,14 @@
             V((tiles, slots, 2 * ft), BF16), V((slots, width), F32), V((slots, width), F32),
             V((experts, capacity, width), BF16),
         ]
-        + ([V(slab_in, BF16), V(late, BF16)] + [DMA((2 * tiles,))] * 2 + [DMA((tiles,))] * 2 if within else [])
+        + ([V(slab_in, BF16), V(late, BF16), V(early, BF16)] + [DMA((2 * tiles,))] * 2 + [DMA((tiles,))] * 3 if within else [])
         + [DMA((peers,))] * 4
         + [DMA((2,))]
         + [V((experts, 8, capacity), F32)] * 3
         + [V((128, width), F32), V((3, length, 128), F32)]
         + [DMA((peers,))] * 4,
         (send, g_rows, expert_in, expert_out, high, low, target, rT, pT, wrT, cmT),
-        "experts", 1, (0, 12), (1, 2, 3, 4, 5, 11, 13) + ((16, 17) if within else (16,)),
+        "experts", 1, (0, 12) + ((17,) if within else ()), (1, 2, 3, 4, 5, 11, 13, 16),
     )
 
     args = (

time: 176 us -> 176 us (level)
  no operation moved by 1% of the time
where the time goes in v8:
time: 176 us
  Pallas kernels  175 us (99%)
    pallas_call x3, Pallas kernels, call(): pl.pallas_call(wrapped, out_shape=outs, in_specs=specs[:len(args)], out_s...  170 us
    pallas_call x1, Pallas kernels, final(): pl.pallas_call(functools.partial(final_kernel, len(big)), out_shape=[jax....  4.8 us

profile of v8, /device:TPU:0, one launch (start us, length us, event | category | flops | bytes accessed | tf_op | source)
XLA Modules:
  0.0 175.6 jit_solution(10590625465000342408)
XLA Ops:
  0.6 24.0 %attention.1 = (bf16[512,768]{1,0:T(8,128)(2,1)}, bf16[512,768]{1,0:T(8,128)(2,1)}, bf16[512,768]{1,0:T(8,128)(2,1)}, bf16[12,512,512]{2,1,0:T(8,128)(2,1)}, bf1...) custom-call(bf16[512,768]{1,0:T(8,128)(2,1)} %refs_0_.3, ...), custom_call_target="tpu_custom_call" | custom-call | tf_op jit(solution)/shard_map/attention/pallas_call | solution.py:933
  24.6 72.1 %experts.1 = (bf16[4,256,768]{2,1,0:T(8,128)(2,1)}, bf16[4,256,768]{2,1,0:T(8,128)(2,1)}, bf16[3,2048,256]{2,1,0:T(8,128)(2,1)}, f32[4,8,256]{2,1,0:T(8,128)}, f...) custom-call(bf16[4,256,768]{2,1,0:T(8,128)(2,1)} %get-tuple-element.49.refs_0_, ...), custom_call_target="tpu_custom_call" | custom-call | tf_op jit(solution)/shard_map/experts/pallas_call | solution.py:933
  96.7 73.9 %backward.1 = (bf16[512,768]{1,0:T(8,128)(2,1)}, bf16[512,768]{1,0:T(8,128)(2,1)}, f32[24,2304]{1,0:T(8,128)}, f32[24,768]{1,0:T(8,128)}, f32[24,128]{1,0:T(8,12...) custom-call(bf16[512,768]{1,0:T(8,128)(2,1)} %refs_0_.3, bf16[512,768]{1,0:T(8,128)(2,1)} %refs_1_.3, ...), custom_call_target="tpu_custom_call" | custom-call | tf_op jit(solution)/shard_map/backward/pallas_call | solution.py:933
  170.6 4.8 %results.1 = (bf16[512,768]{1,0:T(8,128)(2,1)}, bf16[512,768]{1,0:T(8,128)(2,1)}, f32[24,2304]{1,0:T(8,128)}, f32[24,768]{1,0:T(8,128)}, f32[96,4096]{1,0:T(8,12...) custom-call(bf16[512,768]{1,0:T(8,128)(2,1)} %get-tuple-element.67.r, ...), custom_call_target="tpu_custom_call" | custom-call | tf_op jit(solution)/shard_map/results/pallas_call | solution.py:971
